TPU v7x, 32 devices: a whole 2x2x4 slice. The times are simulated.
32 devices in a mesh: grp: 2 (over y), gx: 4 (over z), gy: 4 (over x, core).
Axes of the slice: x: 2, y: 2, z: 4, core: 2. Of those that a mesh axis runs over, the one named last changes fastest.
Arguments:
- counts: int32 [256, 256, 256], P(('grp', 'gx'), 'gy'), parts along dimension 0, may hold values from -40 to 999
Outputs:
- denoised: float32 [256, 256, 256], P(('grp', 'gx'), 'gy'), parts along dimension 0
There are 2 independent parts, one for each index of `grp`. A program takes and returns all parts, laid end to end along the dimension named above; each array names one. Nothing has to cross between parts.
All inputs are finite; a program needn't handle non-finite values.
Results may differ from a plain program's by a relative error of at most 0.00005.
Values sent between devices are 32-bit elements; how exact they have to be, the bound alone decides.
No kernel may reach another device: no remote copies, remote signals or barrier semaphores. Data moves between devices by JAX's collectives and lax.ppermute only.
A program may use at most 64 MiB of HBM per device.

v0:
```python
import functools
import math

import jax
import jax.numpy as jnp
import ml_dtypes
import numpy as np
from jax import lax
from jax.experimental import pallas as pl
from jax.experimental.pallas import tpu as pltpu
from jax.sharding import PartitionSpec as P

R3 = math.sqrt(3.0)
H0 = (1.0 + R3) / (4.0 * math.sqrt(2.0))
RHO = (1.0 - R3) / (1.0 + R3)
LOW_TAPS = [H0 * t for t in (1.0, R3, -R3 * RHO, RHO)]
HIGH_TAPS = [LOW_TAPS[3], -LOW_TAPS[2], LOW_TAPS[1], -LOW_TAPS[0]]
KAPPA = -R3 * (1.0 + RHO * RHO)
THRESHOLD = 0.1
LANES = 128


def shifted(x, axis, by):
    count = lax.axis_size(axis)
    return lax.ppermute(x, axis, [(i, (i + by) % count) for i in range(count)])


def time_matrix(length, width):
    matrix = np.zeros((width, width), np.float64)
    half = length // 2
    for k in range(half):
        for j in range(4):
            matrix[(2 * k + j) % length, k] += LOW_TAPS[j] * H0 * H0
            matrix[(2 * k + j) % length, half + k] += HIGH_TAPS[j] * H0 * H0
    return matrix


def parts_of(matrix):
    single = matrix.astype(np.float32)
    high = single.astype(ml_dtypes.bfloat16)
    low = (single - high.astype(np.float32)).astype(ml_dtypes.bfloat16)
    return np.stack([high, low])


def dot_parts(x, m_ref):
    high = x.astype(jnp.bfloat16)
    low = (x - high.astype(jnp.float32)).astype(jnp.bfloat16)
    dot = functools.partial(jnp.dot, preferred_element_type=jnp.float32)
    return dot(high, m_ref[0]) + (dot(low, m_ref[0]) + dot(high, m_ref[1]))


def ceil8(n):
    return (n + 7) // 8 * 8


class Sizes:
    def __init__(self, x, y, t):
        self.x, self.y, self.t = x, y, t
        self.lx = [x // 2 + 1, x // 4 + 2, x // 8 + 2]
        self.ly = [y // 2 + 1, y // 4 + 2, y // 8 + 2]
        self.py = [ceil8(n) for n in self.ly]
        p1, p2, p3 = self.py
        self.g = [(self.lx[0], 2, 4, p1, LANES), (self.lx[1], 2, 2, p2, LANES), (self.lx[2], 2, 2, p3, LANES)]
        self.zin = [y, p1, p2]
        self.zbase = [6, 5, 6]
        self.zrows = [ceil8(2 * (p - 1) + 4 + b) for p, b in zip(self.py, self.zbase)]
        self.xp = 4 * p1 + 2 * 2 * p2 + 3 * 2 * p3
        self.xn = 4 * p1 + 3 * 2 * p2 + 3 * 2 * p3
        n1, n2, n3 = self.lx[0] * 4, self.lx[1] * 2, self.lx[2] * 2
        self.yp = ceil8(n1 + 2 * n2 + 3 * n3)
        self.yn = ceil8(n1 + 3 * n2 + 3 * n3)


def lattice(v0, v1, v2, v3):
    a = v0 + R3 * v1
    b = v3 - R3 * v2
    return a + RHO * b, RHO * a - b


def lattice_t(low_next, high_next, low_here, high_here):
    a = low_next + RHO * high_next
    b = RHO * low_here - high_here
    return a - R3 * b, R3 * a + b


def x_lattice_static(rows, shape):
    v = [jnp.zeros(shape, jnp.float32) if r is None else r for r in rows]
    return lattice(*v)


def y_analysis(z_ref, index, base, count, low_ref, low_index, high_ref, high_index):
    v = [z_ref[index + (pl.ds(base + j, count, stride=2), slice(None))] for j in range(4)]
    low, high = lattice(*v)
    low_ref[low_index] = low
    high_ref[high_index] = high


def forward(sz, u_ref, f1, f2, f3, g1, g2, g3, a1, z1, a2, z2, a3, z3):
    x, y, t = sz.x, sz.y, sz.t
    half = t // 2

    def rows_x(s, carry):
        low, high = lattice(*[u_ref[2 * s + j] for j in range(4)])
        a1[s, 0] = low
        a1[s, 1] = high
        return carry

    lax.fori_loop(0, sz.lx[0], rows_x, 0)

    step = 6
    for s0 in range(0, sz.lx[0], step):
        n = min(step, sz.lx[0] - s0)
        out = dot_parts(a1[s0 : s0 + n].reshape(n * 2 * y, t), f1).reshape(n, 2, y, t)
        z1[s0 : s0 + n, :, 0, 8 : 8 + y, :] = out[..., :half]
        z1[s0 : s0 + n, :, 1, 8 : 8 + y, :] = out[..., half:]

    def cols_1(s, carry):
        z1[s, :, :, 0:8, :] = jnp.zeros((2, 2, 8, LANES), jnp.float32)
        tail = sz.zrows[0] - 8 - y
        z1[s, :, :, 8 + y :, :] = jnp.zeros((2, 2, tail, LANES), jnp.float32)
        for xb in range(2):
            for tb in range(2):
                y_analysis(z1, (s, xb, tb), sz.zbase[0], sz.py[0], g1, (s, xb, tb), g1, (s, xb, 2 + tb))
        return carry

    lax.fori_loop(0, sz.lx[0], cols_1, 0)

    for level, (src, offset, a, z, f, g) in enumerate(((g1, 3, a2, z2, f2, g2), (g2, 2, a3, z3, f3, g3)), 1):
        rows_in, count = sz.lx[level - 1], sz.lx[level]
        p_in, p_out = sz.py[level - 1], sz.py[level]
        for s in range(count):
            picks = [2 * s + j - offset for j in range(4)]
            rows = [src[i, 0, 0] if 0 <= i < rows_in else None for i in picks]
            low, high = x_lattice_static(rows, (p_in, LANES))
            a[s, 0] = low
            a[s, 1] = high
        out = dot_parts(a[...].reshape(count * 2 * p_in, LANES), f)
        z[:, :, 0:8, :] = jnp.zeros((count, 2, 8, LANES), jnp.float32)
        z[:, :, 8 : 8 + p_in, :] = out.reshape(count, 2, p_in, LANES)
        tail = sz.zrows[level] - 8 - p_in
        if tail:
            z[:, :, 8 + p_in :, :] = jnp.zeros((count, 2, tail, LANES), jnp.float32)
        for s in range(count):
            for xb in range(2):
                y_analysis(z, (s, xb), sz.zbase[level], p_out, g, (s, xb, 0), g, (s, xb, 1))


def pack_x(sz, g1, g2, g3, mp, mn):
    p1, p2, p3 = sz.py

    def put(ref, pieces):
        at = 0
        for piece, rows in pieces:
            ref[at : at + rows] = piece.reshape(rows, LANES)
            at += rows

    l2, l3 = sz.lx[1], sz.lx[2]
    put(mp, [(g1[0, 1], 4 * p1), (g2[0, 1], 2 * p2), (g2[1, 1], 2 * p2),
             (g3[0, 1], 2 * p3), (g3[1, 0], 2 * p3), (g3[1, 1], 2 * p3)])
    put(mn, [(g1[sz.lx[0] - 1, 0], 4 * p1), (g2[l2 - 2, 0], 2 * p2), (g2[l2 - 2, 1], 2 * p2), (g2[l2 - 1, 0], 2 * p2),
             (g3[l3 - 2, 0], 2 * p3), (g3[l3 - 2, 1], 2 * p3), (g3[l3 - 1, 0], 2 * p3)])


def fix_x(sz, g1, g2, g3, rn, rp):
    p1, p2, p3 = sz.py
    l1, l2, l3 = sz.lx

    def take(ref, at, n, p):
        return ref[at : at + n * p].reshape(n, p, LANES)

    high = take(rn, 0, 4, p1)
    g1[l1 - 1, 0] += -RHO * high
    g1[l1 - 1, 1] += high
    low = take(rp, 0, 4, p1)
    g1[0, 0] += low
    g1[0, 1] += RHO * low
    at = 4 * p1
    h0 = take(rn, at, 2, p2)
    h1 = take(rn, at + 2 * p2, 2, p2)
    g2[l2 - 2, 0] += -RHO * h0
    g2[l2 - 2, 1] += h0
    g2[l2 - 1, 0] += KAPPA * h0 - RHO * h1
    g2[l2 - 1, 1] += h1
    w0 = take(rp, at, 2, p2)
    w1 = take(rp, at + 2 * p2, 2, p2)
    w2 = take(rp, at + 4 * p2, 2, p2)
    g2[0, 0] += w0
    g2[0, 1] += w1
    g2[1, 0] += w2
    g2[1, 1] += RHO * w2
    an = at + 4 * p2
    h0 = take(rn, an, 2, p3)
    g3[l3 - 2, 0] += -RHO * h0
    g3[l3 - 2, 1] += h0
    g3[l3 - 1, 0] += take(rn, an + 2 * p3, 2, p3)
    g3[l3 - 1, 1] += take(rn, an + 4 * p3, 2, p3)
    ap = at + 6 * p2
    g3[0, 0] += take(rp, ap, 2, p3)
    g3[0, 1] += take(rp, ap + 2 * p3, 2, p3)
    w2 = take(rp, ap + 4 * p3, 2, p3)
    g3[1, 0] += w2
    g3[1, 1] += RHO * w2


def pack_y(sz, g1, g2, g3, mp, mn):
    k1, k2, k3 = sz.ly
    at_p = at_n = 0
    for s in range(sz.lx[0]):
        for xb in range(2):
            for tb in range(2):
                mp[at_p : at_p + 1] = g1[s, xb, 2 + tb, 0:1]
                mn[at_n : at_n + 1] = g1[s, xb, tb, k1 - 1 : k1]
                at_p += 1
                at_n += 1
    for s in range(sz.lx[1]):
        for xb in range(2):
            mp[at_p : at_p + 2] = g2[s, xb, 1, 0:2]
            mn[at_n : at_n + 2] = g2[s, xb, 0, k2 - 2 : k2]
            mn[at_n + 2 : at_n + 3] = g2[s, xb, 1, k2 - 2 : k2 - 1]
            at_p += 2
            at_n += 3
    for s in range(sz.lx[2]):
        for xb in range(2):
            mp[at_p : at_p + 2] = g3[s, xb, 1, 0:2]
            mp[at_p + 2 : at_p + 3] = g3[s, xb, 0, 1:2]
            mn[at_n : at_n + 2] = g3[s, xb, 0, k3 - 2 : k3]
            mn[at_n + 2 : at_n + 3] = g3[s, xb, 1, k3 - 2 : k3 - 1]
            at_p += 3
            at_n += 3
    if at_p < sz.yp:
        mp[at_p:] = jnp.zeros((sz.yp - at_p, LANES), jnp.float32)
    if at_n < sz.yn:
        mn[at_n:] = jnp.zeros((sz.yn - at_n, LANES), jnp.float32)


def fix_y(sz, g1, g2, g3, rn, rp):
    k1, k2, k3 = sz.ly
    at_p = at_n = 0

    def add(g, index, row, value):
        g[index + (slice(row, row + 1), slice(None))] += value

    for s in range(sz.lx[0]):
        for xb in range(2):
            for tb in range(2):
                high = rn[at_n : at_n + 1]
                add(g1, (s, xb, tb), k1 - 1, -RHO * high)
                add(g1, (s, xb, 2 + tb), k1 - 1, high)
                low = rp[at_p : at_p + 1]
                add(g1, (s, xb, tb), 0, low)
                add(g1, (s, xb, 2 + tb), 0, RHO * low)
                at_p += 1
                at_n += 1
    for s in range(sz.lx[1]):
        for xb in range(2):
            h0, h1 = rn[at_n : at_n + 1], rn[at_n + 1 : at_n + 2]
            add(g2, (s, xb, 0), k2 - 2, -RHO * h0)
            add(g2, (s, xb, 1), k2 - 2, h0)
            add(g2, (s, xb, 0), k2 - 1, KAPPA * h0 - RHO * h1)
            add(g2, (s, xb, 1), k2 - 1, h1)
            w0, w2, w1 = (rp[at_p + i : at_p + i + 1] for i in range(3))
            add(g2, (s, xb, 0), 0, w0)
            add(g2, (s, xb, 1), 0, w1)
            add(g2, (s, xb, 0), 1, w2)
            add(g2, (s, xb, 1), 1, RHO * w2)
            at_n += 2
            at_p += 3
    for s in range(sz.lx[2]):
        for xb in range(2):
            h0, h1, l1 = (rn[at_n + i : at_n + i + 1] for i in range(3))
            add(g3, (s, xb, 0), k3 - 2, -RHO * h0)
            add(g3, (s, xb, 1), k3 - 2, h0)
            add(g3, (s, xb, 0), k3 - 1, l1)
            add(g3, (s, xb, 1), k3 - 1, h1)
            w0, w2, w1 = (rp[at_p + i : at_p + i + 1] for i in range(3))
            add(g3, (s, xb, 0), 0, w0)
            add(g3, (s, xb, 1), 0, w1)
            add(g3, (s, xb, 0), 1, w2)
            add(g3, (s, xb, 1), 1, RHO * w2)
            at_n += 3
            at_p += 3


def shrink(v):
    return v - jnp.clip(v, -THRESHOLD, THRESHOLD)


def y_synthesis(low, high, count, t_ref, v_ref, index, start):
    a = low + RHO * high
    b = RHO * low - high
    t_ref[...] = a
    a = t_ref[1 : 1 + count]
    b = b[:count]
    v_ref[index + (pl.ds(start, count, stride=2), slice(None))] = a - R3 * b
    v_ref[index + (pl.ds(start + 1, count, stride=2), slice(None))] = R3 * a + b


def lane_below(limit, shape):
    return lax.broadcasted_iota(jnp.int32, shape, 1) < limit


def inverse(sz, details, emit, i1, i2, i3, ta, v3, b3, v2, b2, v1, b1):
    y, t = sz.y, sz.t
    half = t // 2
    p1, p2, p3 = sz.py
    l1, l2, l3 = sz.lx
    third = lane_below(t // 8, (p3, LANES))

    for s in range(l3):
        for xb in range(2):
            low = details(2, s, xb, 0, third if xb == 0 else None)
            high = details(2, s, xb, 1, None)
            y_synthesis(low, high, sz.ly[1] // 2, ta.at[2, s, xb, 0:p3], v3, (s, xb), 0)
    b3[...] = dot_parts(v3[...].reshape(l3 * 2 * p2, LANES), i3).reshape(l3, 2, p2, LANES)

    second = lane_below(t // 4, (p2, LANES))
    for p in range(l2 // 2):
        even, odd = lattice_t(b3[p + 1, 0], b3[p + 1, 1], b3[p, 0], b3[p, 1])
        for s, coarse in ((2 * p, even), (2 * p + 1, odd)):
            for xb in range(2):
                low = details(1, s, xb, 0, None)
                if xb == 0:
                    low = jnp.where(second, coarse, low)
                high = details(1, s, xb, 1, None)
                y_synthesis(low, high, (sz.ly[0] + 1) // 2, ta.at[1, s, xb, 0:p2], v2, (s, xb), 7)
    b2[...] = dot_parts(v2[:, :, 8 : 8 + p1, :].reshape(l2 * 2 * p1, LANES), i2).reshape(l2, 2, p1, LANES)

    def level_1(s, coarse):
        for xb in range(2):
            for tb in range(2):
                if xb == 0 and tb == 0:
                    low = coarse
                else:
                    low = details(0, s, xb, tb, None)
                high = details(0, s, xb, 2 + tb, None)
                y_synthesis(low, high, y // 2, ta.at[0, s, xb * 2 + tb, 0:p1], v1, (s, xb, tb), 0)

    def coarse_rows(p):
        return lattice_t(b2[p + 1, 0], b2[p + 1, 1], b2[p, 0], b2[p, 1])

    level_1(0, coarse_rows(0)[1])

    def pair_1(p, carry):
        even, odd = coarse_rows(p)
        level_1(2 * p - 1, even)
        level_1(2 * p, odd)
        return carry

    lax.fori_loop(1, l2 - 1, pair_1, 0)

    step = 6
    for s0 in range(0, l1, step):
        n = min(step, l1 - s0)
        v = jnp.concatenate([v1[s0 : s0 + n, :, 0], v1[s0 : s0 + n, :, 1]], axis=-1)
        b1[s0 : s0 + n] = dot_parts(v.reshape(n * 2 * y, t), i1).reshape(n, 2, y, t)

    def rows_x(p, carry):
        even, odd = lattice_t(b1[p + 1, 0], b1[p + 1, 1], b1[p, 0], b1[p, 1])
        emit(p, even, odd)
        return carry

    lax.fori_loop(0, sz.x // 2, rows_x, 0)


def border(sz, u_ref):
    zeros = jnp.zeros((2, sz.y, sz.t), jnp.float32)
    u_ref[0:2] = zeros
    u_ref[sz.x + 2 : sz.x + 4] = zeros


def first_kernel(sz, c_ref, f1, f2, f3, w_ref, g1, g2, g3, mp, mn, u, *scratch):
    border(sz, u)

    def rows(x, carry):
        value = c_ref[x].astype(jnp.float32) * (1.0 / 64.0)
        weight = 1.0 / (1.0 + jnp.abs(value))
        w_ref[x] = weight
        u[x + 2] = weight * value
        return carry

    lax.fori_loop(0, sz.x, rows, 0)
    forward(sz, u, f1, f2, f3, g1, g2, g3, *scratch)
    pack_x(sz, g1, g2, g3, mp, mn)


def edge_kernel(sz, g1i, g2i, g3i, rn, rp, g1, g2, g3, mp, mn):
    fix_x(sz, g1, g2, g3, rn, rp)
    pack_y(sz, g1, g2, g3, mp, mn)


def middle_kernel(sz, g1i, g2i, g3i, rn, rp, w_ref, f1, f2, f3, i1, i2, i3,
                  g1, g2, g3, q1, q2, q3, mp, mn, u, ta, v3, b3, v2, b2, v1, b1, *scratch):
    fix_y(sz, g1, g2, g3, rn, rp)
    border(sz, u)

    def details(level, s, xb, q, approx_lanes):
        value = (g1, g2, g3)[level][s, xb, q]
        small = shrink(value)
        return small if approx_lanes is None else jnp.where(approx_lanes, value, small)

    def emit(p, even, odd):
        u[2 * p + 2] = w_ref[2 * p] * even
        u[2 * p + 3] = w_ref[2 * p + 1] * odd

    inverse(sz, details, emit, i1, i2, i3, ta, v3, b3, v2, b2, v1, b1)
    forward(sz, u, f1, f2, f3, q1, q2, q3, *scratch)
    pack_x(sz, q1, q2, q3, mp, mn)


def last_kernel(sz, q1i, q2i, q3i, rn, rp, g1, g2, g3, i1, i2, i3, q1, q2, q3, out, ta, v3, b3, v2, b2, v1, b1):
    fix_y(sz, q1, q2, q3, rn, rp)

    def details(level, s, xb, q, approx_lanes):
        first = (g1, g2, g3)[level][s, xb, q]
        second = (q1, q2, q3)[level][s, xb, q]
        small = shrink(shrink(first) + (first - second))
        if approx_lanes is None:
            return small
        return jnp.where(approx_lanes, first + (first - second), small)

    def emit(p, even, odd):
        out[2 * p] = even
        out[2 * p + 1] = odd

    inverse(sz, details, emit, i1, i2, i3, ta, v3, b3, v2, b2, v1, b1)


def call(kernel, sz, outs, scratch, aliases, *args):
    vmem = pl.BlockSpec(memory_space=pltpu.VMEM)
    return pl.pallas_call(
        functools.partial(kernel, sz),
        out_shape=[jax.ShapeDtypeStruct(s, jnp.float32) for s in outs],
        in_specs=[vmem] * len(args),
        out_specs=[vmem] * len(outs),
        scratch_shapes=[pltpu.VMEM(s, jnp.float32) for s in scratch],
        input_output_aliases=aliases,
        compiler_params=pltpu.CompilerParams(vmem_limit_bytes=36 * 2**20),
    )(*args)


def on_device(counts):
    sz = Sizes(*counts.shape)
    t = sz.t
    fw = [time_matrix(t, t), time_matrix(t // 2, LANES), time_matrix(t // 4, LANES)]
    f = [jnp.asarray(parts_of(m)) for m in fw]
    i = [jnp.asarray(parts_of(m.T)) for m in fw]
    l1, l2, l3 = sz.lx
    p1, p2, p3 = sz.py
    wide = (sz.x, sz.y, sz.t)
    u = (sz.x + 4, sz.y, sz.t)
    fw_scratch = [(l1, 2, sz.y, t), (l1, 2, 2, sz.zrows[0], LANES), (l2, 2, p1, LANES), (l2, 2, sz.zrows[1], LANES),
                  (l3, 2, p2, LANES), (l3, 2, sz.zrows[2], LANES)]
    bw_scratch = [(3, l1, 4, p1 + 8, LANES), (l3, 2, p2, LANES), (l3, 2, p2, LANES), (l2, 2, p1 + 8, LANES),
                  (l2, 2, p1, LANES), (l1, 2, 2, sz.y, LANES), (l1, 2, sz.y, t)]
    to_prev, to_next = (sz.xp, LANES), (sz.xn, LANES)
    y_prev, y_next = (sz.yp, LANES), (sz.yn, LANES)
    same = {0: 0, 1: 1, 2: 2}

    def exchange(g, mp, mn):
        rn = shifted(mp, "gx", -1)
        rp = shifted(mn, "gx", 1)
        *g, mp, mn = call(edge_kernel, sz, sz.g + [y_prev, y_next], [], same, *g, rn, rp)
        return g, shifted(mp, "gy", -1), shifted(mn, "gy", 1)

    weight, *g, mp, mn = call(first_kernel, sz, [wide] + sz.g + [to_prev, to_next], [u] + fw_scratch, {}, counts, *f)
    g, rn, rp = exchange(g, mp, mn)
    *rest, mp, mn = call(middle_kernel, sz, sz.g + sz.g + [to_prev, to_next], [u] + bw_scratch + fw_scratch, same,
                         *g, rn, rp, weight, *f, *i)
    g, q = rest[:3], rest[3:]
    q, rn, rp = exchange(q, mp, mn)
    return call(last_kernel, sz, sz.g + [wide], bw_scratch, same, *q, rn, rp, *g, *i)[3]


def solution(mesh):
    spec = P(("grp", "gx"), "gy", None)
    return jax.shard_map(on_device, mesh=mesh, in_specs=(spec,), out_specs=spec, check_vma=False)
```

profile of v0, /device:TPU:0, one launch (start us, length us, event | category | flops | bytes accessed | tf_op | source)
XLA Modules:
  0.0 53.9 jit_solution(17779595033572577390)
XLA Ops:
  0.0 0.0 copy-start
  0.0 1.6 %copy-done = s32[32,64,256]{2,1,0:T(8,128)S(1)} copy-done((s32[32,64,256]{2,1,0:T(8,128)S(1)}, s32[32,64,256]{2,1,0:T(8,128)}, u32[]{:S(2)}) %copy-start) | copy-done | bytes 2097176
  1.6 0.0 copy-start.2
  1.6 0.9 %copy-done.2 = bf16[2,256,256]{2,1,0:T(8,128)(2,1)S(1)} copy-done((bf16[2,256,256]{2,1,0:T(8,128)(2,1)S(1)}, bf16[2,256,256]{2,1,0:T(8,128)(2,1)}, u32[]{:S(2)}) %copy-start.2) | copy-done | bytes 262168
  2.5 0.0 copy-start.5
  2.5 0.8 %copy-done.5 = bf16[2,128,128]{2,1,0:T(8,128)(2,1)S(1)} copy-done((bf16[2,128,128]{2,1,0:T(8,128)(2,1)S(1)}, bf16[2,128,128]{2,1,0:T(8,128)(2,1)}, u32[]{:S(2)}) %copy-start.5) | copy-done | bytes 65560
  3.4 0.0 copy-start.6
  3.4 0.8 %copy-done.6 = bf16[2,128,128]{2,1,0:T(8,128)(2,1)S(1)} copy-done((bf16[2,128,128]{2,1,0:T(8,128)(2,1)S(1)}, bf16[2,128,128]{2,1,0:T(8,128)(2,1)}, u32[]{:S(2)}) %copy-start.6) | copy-done | bytes 65560
  4.2 0.0 copy-start.1
  4.2 0.0 copy-start.3
  4.2 0.0 copy-start.4
  4.2 3.8 %shard_map.73 = (f32[32,64,256]{2,1,0:T(8,128)S(1)}, f32[17,2,4,40,128]{4,3,2,1,0:T(8,128)S(1)}, f32[10,2,2,24,128]{4,3,2,1,0:T(8,128)S(1)}, f32[6,2,2,16,128]{4...) custom-call(s32[32,64,256]{2,1,0:T(8,128)S(1)} %copy-done, bf16[2,256,256]{2,1,0:T(8,128)(2,1)S(1)} %copy-done.2, ...), custom_call_target="tpu_custom_call" | custom-call | tf_op jit(solution)/shard_map/pallas_call | solution.py:430
  8.0 3.1 %collective-permute-start.1 = (f32[400,128]{1,0:T(8,128)S(1)}, f32[400,128]{1,0:T(8,128)S(1)}, u32[]{:S(2)}, u32[]{:S(2)}) collective-permute-start(f32[400,128]{1,0:T(8,128)S(1)} %get-tuple-element.34), channel_id=1, source_target_pairs={{0,4},{4,8},{8,12},{12,0},{1,5},{5,9},{9,13},{13,1},{2,6},{6,10},{... | collective-permute-start | bytes 614408 | tf_op jit(solution)/shard_map/ppermute | solution.py:25
  11.1 2.1 %collective-permute-start = (f32[352,128]{1,0:T(8,128)S(1)}, f32[352,128]{1,0:T(8,128)S(1)}, u32[]{:S(2)}, u32[]{:S(2)}) collective-permute-start(f32[352,128]{1,0:T(8,128)S(1)} %get-tuple-element.33), channel_id=1, source_target_pairs={{0,12},{4,0},{8,4},{12,8},{1,13},{5,1},{9,5},{13,9},{2,14},{6,2},{... | collective-permute-start | bytes 540680 | tf_op jit(solution)/shard_map/ppermute | solution.py:25
  13.2 8.3 %collective-permute-done.rn = f32[352,128]{1,0:T(8,128)S(1)} collective-permute-done((f32[352,128]{1,0:T(8,128)S(1)}, f32[352,128]{1,0:T(8,128)S(1)}, u32[]{:S(2)}, u32[]{:S(2)}) %collective-permute-start) | collective-permute-done | bytes 180256 | tf_op jit(solution)/shard_map/ppermute | solution.py:25
  21.5 0.0 collective-permute-done.1.rp
  21.5 0.1 shard_map.74
  21.6 0.1 collective-permute-start.3
  21.7 1.7 %collective-permute-start.2 = (f32[144,128]{1,0:T(8,128)S(1)}, f32[144,128]{1,0:T(8,128)S(1)}, u32[]{:S(2)}, u32[]{:S(2)}) collective-permute-start(f32[144,128]{1,0:T(8,128)S(1)} %get-tuple-element.38), channel_id=1, source_target_pairs={{0,3},{1,0},{2,1},{3,2},{4,7},{5,4},{6,5},{7,6},{8,11},{9,8},{10,9... | collective-permute-start | bytes 221192 | tf_op jit(solution)/shard_map/ppermute | solution.py:25
  23.4 2.0 %collective-permute-done.2.rn = f32[144,128]{1,0:T(8,128)S(1)} collective-permute-done((f32[144,128]{1,0:T(8,128)S(1)}, f32[144,128]{1,0:T(8,128)S(1)}, u32[]{:S(2)}, u32[]{:S(2)}) %collective-permute-start.2) | collective-permute-done | bytes 73760 | tf_op jit(solution)/shard_map/ppermute | solution.py:25
  25.4 0.2 collective-permute-done.3.rp
  25.6 0.0 copy-done.1
  25.6 0.0 copy-done.3
  25.6 0.0 copy-done.4
  25.6 6.5 %shard_map.75 = (f32[17,2,4,40,128]{4,3,2,1,0:T(8,128)S(1)}, f32[10,2,2,24,128]{4,3,2,1,0:T(8,128)S(1)}, f32[6,2,2,16,128]{4,3,2,1,0:T(8,128)S(1)}, f32[17,2,4,4...) custom-call(f32[17,2,4,40,128]{4,3,2,1,0:T(8,128)S(1)} %get-tuple-el, ...), custom_call_target="tpu_custom_call", output_to_operand_aliasing={{0}: (0, {}), {1}: (1, {}), {2}: (2, {})} | custom-call | tf_op jit(solution)/shard_map/pallas_call | solution.py:430
  32.1 1.2 %collective-permute-start.5 = (f32[400,128]{1,0:T(8,128)S(1)}, f32[400,128]{1,0:T(8,128)S(1)}, u32[]{:S(2)}, u32[]{:S(2)}) collective-permute-start(f32[400,128]{1,0:T(8,128)S(1)} %get-tuple-element.45), channel_id=1, source_target_pairs={{0,4},{4,8},{8,12},{12,0},{1,5},{5,9},{9,13},{13,1},{2,6},{6,10},{... | collective-permute-start | bytes 614408 | tf_op jit(solution)/shard_map/ppermute | solution.py:25
  33.3 2.7 %collective-permute-start.4 = (f32[352,128]{1,0:T(8,128)S(1)}, f32[352,128]{1,0:T(8,128)S(1)}, u32[]{:S(2)}, u32[]{:S(2)}) collective-permute-start(f32[352,128]{1,0:T(8,128)S(1)} %get-tuple-element.44), channel_id=1, source_target_pairs={{0,12},{4,0},{8,4},{12,8},{1,13},{5,1},{9,5},{13,9},{2,14},{6,2},{... | collective-permute-start | bytes 540680 | tf_op jit(solution)/shard_map/ppermute | solution.py:25
  36.0 8.9 %collective-permute-done.4.rn = f32[352,128]{1,0:T(8,128)S(1)} collective-permute-done((f32[352,128]{1,0:T(8,128)S(1)}, f32[352,128]{1,0:T(8,128)S(1)}, u32[]{:S(2)}, u32[]{:S(2)}) %collective-permute-start.4) | collective-permute-done | bytes 180256 | tf_op jit(solution)/shard_map/ppermute | solution.py:25
  44.9 0.0 collective-permute-done.5.rp
  44.9 0.1 shard_map.76
  45.0 0.2 collective-permute-start.7
  45.2 1.6 %collective-permute-start.6 = (f32[144,128]{1,0:T(8,128)S(1)}, f32[144,128]{1,0:T(8,128)S(1)}, u32[]{:S(2)}, u32[]{:S(2)}) collective-permute-start(f32[144,128]{1,0:T(8,128)S(1)} %get-tuple-element.49), channel_id=1, source_target_pairs={{0,3},{1,0},{2,1},{3,2},{4,7},{5,4},{6,5},{7,6},{8,11},{9,8},{10,9... | collective-permute-start | bytes 221192 | tf_op jit(solution)/shard_map/ppermute | solution.py:25
  46.8 2.0 %collective-permute-done.6.rn = f32[144,128]{1,0:T(8,128)S(1)} collective-permute-done((f32[144,128]{1,0:T(8,128)S(1)}, f32[144,128]{1,0:T(8,128)S(1)}, u32[]{:S(2)}, u32[]{:S(2)}) %collective-permute-start.6) | collective-permute-done | bytes 73760 | tf_op jit(solution)/shard_map/ppermute | solution.py:25
  48.8 0.2 collective-permute-done.7.rp
  49.0 4.9 %shard_map.77 = (f32[17,2,4,40,128]{4,3,2,1,0:T(8,128)S(1)}, f32[10,2,2,24,128]{4,3,2,1,0:T(8,128)S(1)}, f32[6,2,2,16,128]{4,3,2,1,0:T(8,128)S(1)}, f32[32,64,256]{2,1,0:T(8,128)}) custom-call(f32[17,2,4,40,128]{4,3,2,1,0:T(8,128)S(1)} %get-tuple-element.46.q1i, ...), custom_call_target="tpu_custom_call", output_to_operand_aliasing={{0}: (0, {}), {1}: (1, {}), {2}: (2, {})} | custom-call | tf_op jit(solution)/shard_map/pallas_call | solution.py:430
Async XLA Ops:
  0.0 1.6 %copy-start = (s32[32,64,256]{2,1,0:T(8,128)S(1)}, s32[32,64,256]{2,1,0:T(8,128)}, u32[]{:S(2)}) copy-start(s32[32,64,256]{2,1,0:T(8,128)} %c_ref.1) | copy-start | bytes 6291460
  1.6 0.9 %copy-start.2 = (bf16[2,256,256]{2,1,0:T(8,128)(2,1)S(1)}, bf16[2,256,256]{2,1,0:T(8,128)(2,1)}, u32[]{:S(2)}) copy-start(bf16[2,256,256]{2,1,0:T(8,128)(2,1)} %constant.12.clone.f1) | copy-start | bytes 786436
  2.5 0.8 %copy-start.5 = (bf16[2,128,128]{2,1,0:T(8,128)(2,1)S(1)}, bf16[2,128,128]{2,1,0:T(8,128)(2,1)}, u32[]{:S(2)}) copy-start(bf16[2,128,128]{2,1,0:T(8,128)(2,1)} %constant.14.clone.f3) | copy-start | bytes 196612
  3.4 0.8 %copy-start.6 = (bf16[2,128,128]{2,1,0:T(8,128)(2,1)S(1)}, bf16[2,128,128]{2,1,0:T(8,128)(2,1)}, u32[]{:S(2)}) copy-start(bf16[2,128,128]{2,1,0:T(8,128)(2,1)} %constant.13.clone.f2) | copy-start | bytes 196612
  4.2 21.4 %copy-start.1 = (bf16[2,256,256]{2,1,0:T(8,128)(2,1)S(1)}, bf16[2,256,256]{2,1,0:T(8,128)(2,1)}, u32[]{:S(2)}) copy-start(bf16[2,256,256]{2,1,0:T(8,128)(2,1)} %constant.15.clone.i1) | copy-start | bytes 786436
  4.2 21.4 %copy-start.3 = (bf16[2,128,128]{2,1,0:T(8,128)(2,1)S(1)}, bf16[2,128,128]{2,1,0:T(8,128)(2,1)}, u32[]{:S(2)}) copy-start(bf16[2,128,128]{2,1,0:T(8,128)(2,1)} %constant.17.clone.i3) | copy-start | bytes 196612
  4.2 21.4 %copy-start.4 = (bf16[2,128,128]{2,1,0:T(8,128)(2,1)S(1)}, bf16[2,128,128]{2,1,0:T(8,128)(2,1)}, u32[]{:S(2)}) copy-start(bf16[2,128,128]{2,1,0:T(8,128)(2,1)} %constant.16.clone.i2) | copy-start | bytes 196612
  8.0 13.5 %collective-permute-start.1 = (f32[400,128]{1,0:T(8,128)S(1)}, f32[400,128]{1,0:T(8,128)S(1)}, u32[]{:S(2)}, u32[]{:S(2)}) collective-permute-start(f32[400,128]{1,0:T(8,128)S(1)} %get-tuple-element.34), channel_id=1, source_target_pairs={{0,4},{4,8},{8,12},{12,0},{1,5},{5,9},{9,13},{13,1},{2,6},{6,10},{... | collective-permute-start | bytes 614408 | tf_op jit(solution)/shard_map/ppermute | solution.py:25
  11.1 10.4 %collective-permute-start = (f32[352,128]{1,0:T(8,128)S(1)}, f32[352,128]{1,0:T(8,128)S(1)}, u32[]{:S(2)}, u32[]{:S(2)}) collective-permute-start(f32[352,128]{1,0:T(8,128)S(1)} %get-tuple-element.33), channel_id=1, source_target_pairs={{0,12},{4,0},{8,4},{12,8},{1,13},{5,1},{9,5},{13,9},{2,14},{6,2},{... | collective-permute-start | bytes 540680 | tf_op jit(solution)/shard_map/ppermute | solution.py:25
  21.6 4.0 %collective-permute-start.3 = (f32[168,128]{1,0:T(8,128)S(1)}, f32[168,128]{1,0:T(8,128)S(1)}, u32[]{:S(2)}, u32[]{:S(2)}) collective-permute-start(f32[168,128]{1,0:T(8,128)S(1)} %get-tuple-element.39), channel_id=1, source_target_pairs={{0,1},{1,2},{2,3},{3,0},{4,5},{5,6},{6,7},{7,4},{8,9},{9,10},{10,1... | collective-permute-start | bytes 258056 | tf_op jit(solution)/shard_map/ppermute | solution.py:25
  21.7 3.7 %collective-permute-start.2 = (f32[144,128]{1,0:T(8,128)S(1)}, f32[144,128]{1,0:T(8,128)S(1)}, u32[]{:S(2)}, u32[]{:S(2)}) collective-permute-start(f32[144,128]{1,0:T(8,128)S(1)} %get-tuple-element.38), channel_id=1, source_target_pairs={{0,3},{1,0},{2,1},{3,2},{4,7},{5,4},{6,5},{7,6},{8,11},{9,8},{10,9... | collective-permute-start | bytes 221192 | tf_op jit(solution)/shard_map/ppermute | solution.py:25
  32.1 12.8 %collective-permute-start.5 = (f32[400,128]{1,0:T(8,128)S(1)}, f32[400,128]{1,0:T(8,128)S(1)}, u32[]{:S(2)}, u32[]{:S(2)}) collective-permute-start(f32[400,128]{1,0:T(8,128)S(1)} %get-tuple-element.45), channel_id=1, source_target_pairs={{0,4},{4,8},{8,12},{12,0},{1,5},{5,9},{9,13},{13,1},{2,6},{6,10},{... | collective-permute-start | bytes 614408 | tf_op jit(solution)/shard_map/ppermute | solution.py:25
  33.3 11.6 %collective-permute-start.4 = (f32[352,128]{1,0:T(8,128)S(1)}, f32[352,128]{1,0:T(8,128)S(1)}, u32[]{:S(2)}, u32[]{:S(2)}) collective-permute-start(f32[352,128]{1,0:T(8,128)S(1)} %get-tuple-element.44), channel_id=1, source_target_pairs={{0,12},{4,0},{8,4},{12,8},{1,13},{5,1},{9,5},{13,9},{2,14},{6,2},{... | collective-permute-start | bytes 540680 | tf_op jit(solution)/shard_map/ppermute | solution.py:25
  45.0 4.0 %collective-permute-start.7 = (f32[168,128]{1,0:T(8,128)S(1)}, f32[168,128]{1,0:T(8,128)S(1)}, u32[]{:S(2)}, u32[]{:S(2)}) collective-permute-start(f32[168,128]{1,0:T(8,128)S(1)} %get-tuple-element.50), channel_id=1, source_target_pairs={{0,1},{1,2},{2,3},{3,0},{4,5},{5,6},{6,7},{7,4},{8,9},{9,10},{10,1... | collective-permute-start | bytes 258056 | tf_op jit(solution)/shard_map/ppermute | solution.py:25
  45.2 3.6 %collective-permute-start.6 = (f32[144,128]{1,0:T(8,128)S(1)}, f32[144,128]{1,0:T(8,128)S(1)}, u32[]{:S(2)}, u32[]{:S(2)}) collective-permute-start(f32[144,128]{1,0:T(8,128)S(1)} %get-tuple-element.49), channel_id=1, source_target_pairs={{0,3},{1,0},{2,1},{3,2},{4,7},{5,4},{6,5},{7,6},{8,11},{9,8},{10,9... | collective-permute-start | bytes 221192 | tf_op jit(solution)/shard_map/ppermute | solution.py:25
where the time goes:
time: 54.8 us; the launch traced here: 53.9 us
  waiting for transfers between devices  21.5 us (39%)
  Pallas kernels  15.5 us (28%)
  starting transfers between devices  12.6 us (23%)
  local copies, waits for them, and re-layouts  4.23 us (8%)
    ppermute x8, waiting for transfers between devices, shifted(): return lax.ppermute(x, axis, [(i, (i + by) % count) for i in range(count)])  21.5 us
    pallas_call x5, Pallas kernels, call(): pl.pallas_call(functools.partial(kernel, sz), out_shape=[jax.ShapeDtypeSt...  15.5 us
    ppermute x8, starting transfers between devices, shifted(): return lax.ppermute(x, axis, [(i, (i + by) % count) for i in range(count)])  12.6 us
    unnamed x14, local copies, waits for them, and re-layouts  4.23 us
  transfers between devices with their start and end apart: 8, of which 6 were waited for; matrix products, arithmetic and copies ran while one was open for 0% of the time, Pallas kernels for 0%

commit v1 on v0

--- a/solution.py
+++ b/solution.py
@@ -3,7 +3,6 @@
 
 import jax
 import jax.numpy as jnp
-import ml_dtypes
 import numpy as np
 from jax import lax
 from jax.experimental import pallas as pl
@@ -35,16 +34,28 @@
     return matrix
 
 
-def parts_of(matrix):
-    single = matrix.astype(np.float32)
-    high = single.astype(ml_dtypes.bfloat16)
-    low = (single - high.astype(np.float32)).astype(ml_dtypes.bfloat16)
-    return np.stack([high, low])
+def pack_matrices(first, second, third):
+    packed = np.zeros((first.shape[0] + LANES, first.shape[0]), np.float32)
+    packed[: first.shape[0]] = first
+    packed[first.shape[0] :, :LANES] = second
+    packed[first.shape[0] :, LANES : 2 * LANES] = third
+    return packed
+
+
+def split(x):
+    high = x.astype(jnp.bfloat16)
+    return high, (x - high.astype(jnp.float32)).astype(jnp.bfloat16)
+
+
+def unpack_matrices(packed, m1, m2, m3):
+    t = packed.shape[1]
+    m1[0], m1[1] = split(packed[:t])
+    m2[0], m2[1] = split(packed[t:, :LANES])
+    m3[0], m3[1] = split(packed[t:, LANES : 2 * LANES])
 
 
 def dot_parts(x, m_ref):
-    high = x.astype(jnp.bfloat16)
-    low = (x - high.astype(jnp.float32)).astype(jnp.bfloat16)
+    high, low = split(x)
     dot = functools.partial(jnp.dot, preferred_element_type=jnp.float32)
     return dot(high, m_ref[0]) + (dot(low, m_ref[0]) + dot(high, m_ref[1]))
 
@@ -64,11 +75,29 @@
         self.zin = [y, p1, p2]
         self.zbase = [6, 5, 6]
         self.zrows = [ceil8(2 * (p - 1) + 4 + b) for p, b in zip(self.py, self.zbase)]
-        self.xp = 4 * p1 + 2 * 2 * p2 + 3 * 2 * p3
-        self.xn = 4 * p1 + 3 * 2 * p2 + 3 * 2 * p3
+        self.main = [y // 2, y // 4, y // 8]
+        self.xp_pieces = [4, 4, 3]
+        self.xn_pieces = [4, 6, 3]
+        self.xp = self.x_rows(self.xp_pieces)
+        self.xn = self.x_rows(self.xn_pieces)
         n1, n2, n3 = self.lx[0] * 4, self.lx[1] * 2, self.lx[2] * 2
         self.yp = ceil8(n1 + 2 * n2 + 3 * n3)
         self.yn = ceil8(n1 + 3 * n2 + 3 * n3)
+
+
+    def x_rows(self, pieces):
+        return ceil8(sum(n * w for n, w in zip(pieces, self.ly)))
+
+    def x_offsets(self, pieces):
+        at = 0
+        mains, extras = [], []
+        for n, m in zip(pieces, self.main):
+            mains.append([at + i * m for i in range(n)])
+            at += n * m
+        for n, m, w in zip(pieces, self.main, self.ly):
+            extras.append([at + i * (w - m) for i in range(n)])
+            at += n * (w - m)
+        return [list(zip(a, b)) for a, b in zip(mains, extras)]
 
 
 def lattice(v0, v1, v2, v3):
@@ -146,60 +175,71 @@
 
 
 def pack_x(sz, g1, g2, g3, mp, mn):
-    p1, p2, p3 = sz.py
-
-    def put(ref, pieces):
-        at = 0
-        for piece, rows in pieces:
-            ref[at : at + rows] = piece.reshape(rows, LANES)
-            at += rows
-
-    l2, l3 = sz.lx[1], sz.lx[2]
-    put(mp, [(g1[0, 1], 4 * p1), (g2[0, 1], 2 * p2), (g2[1, 1], 2 * p2),
-             (g3[0, 1], 2 * p3), (g3[1, 0], 2 * p3), (g3[1, 1], 2 * p3)])
-    put(mn, [(g1[sz.lx[0] - 1, 0], 4 * p1), (g2[l2 - 2, 0], 2 * p2), (g2[l2 - 2, 1], 2 * p2), (g2[l2 - 1, 0], 2 * p2),
-             (g3[l3 - 2, 0], 2 * p3), (g3[l3 - 2, 1], 2 * p3), (g3[l3 - 1, 0], 2 * p3)])
+    l1, l2, l3 = sz.lx
+    lower = lane_below(LANES // 2, (1, LANES))
+
+    def put(ref, pieces, level, items):
+        m, w = sz.main[level], sz.ly[level]
+        for (main, extra), item in zip(sz.x_offsets(pieces)[level], items):
+            for at, lo, hi in ((main, 0, m), (extra, m, w)):
+                if level < 2:
+                    value = item[lo:hi]
+                else:
+                    value = jnp.where(lower, item[0, lo:hi], pltpu.roll(item[1, lo:hi], LANES // 2, 1))
+                ref[at : at + hi - lo] = value
+
+    put(mp, sz.xp_pieces, 0, [g1.at[0, 1, q] for q in range(4)])
+    put(mn, sz.xn_pieces, 0, [g1.at[l1 - 1, 0, q] for q in range(4)])
+    put(mp, sz.xp_pieces, 1, [g2.at[s, 1, q] for s in (0, 1) for q in (0, 1)])
+    put(mn, sz.xn_pieces, 1, [g2.at[s, b, q] for s, b in ((l2 - 2, 0), (l2 - 2, 1), (l2 - 1, 0)) for q in (0, 1)])
+    put(mp, sz.xp_pieces, 2, [g3.at[0, 1], g3.at[1, 0], g3.at[1, 1]])
+    put(mn, sz.xn_pieces, 2, [g3.at[l3 - 2, 0], g3.at[l3 - 2, 1], g3.at[l3 - 1, 0]])
 
 
 def fix_x(sz, g1, g2, g3, rn, rp):
-    p1, p2, p3 = sz.py
     l1, l2, l3 = sz.lx
-
-    def take(ref, at, n, p):
-        return ref[at : at + n * p].reshape(n, p, LANES)
-
-    high = take(rn, 0, 4, p1)
-    g1[l1 - 1, 0] += -RHO * high
-    g1[l1 - 1, 1] += high
-    low = take(rp, 0, 4, p1)
-    g1[0, 0] += low
-    g1[0, 1] += RHO * low
-    at = 4 * p1
-    h0 = take(rn, at, 2, p2)
-    h1 = take(rn, at + 2 * p2, 2, p2)
-    g2[l2 - 2, 0] += -RHO * h0
-    g2[l2 - 2, 1] += h0
-    g2[l2 - 1, 0] += KAPPA * h0 - RHO * h1
-    g2[l2 - 1, 1] += h1
-    w0 = take(rp, at, 2, p2)
-    w1 = take(rp, at + 2 * p2, 2, p2)
-    w2 = take(rp, at + 4 * p2, 2, p2)
-    g2[0, 0] += w0
-    g2[0, 1] += w1
-    g2[1, 0] += w2
-    g2[1, 1] += RHO * w2
-    an = at + 4 * p2
-    h0 = take(rn, an, 2, p3)
-    g3[l3 - 2, 0] += -RHO * h0
-    g3[l3 - 2, 1] += h0
-    g3[l3 - 1, 0] += take(rn, an + 2 * p3, 2, p3)
-    g3[l3 - 1, 1] += take(rn, an + 4 * p3, 2, p3)
-    ap = at + 6 * p2
-    g3[0, 0] += take(rp, ap, 2, p3)
-    g3[0, 1] += take(rp, ap + 2 * p3, 2, p3)
-    w2 = take(rp, ap + 4 * p3, 2, p3)
-    g3[1, 0] += w2
-    g3[1, 1] += RHO * w2
+    lower = lane_below(LANES // 2, (1, LANES))
+
+    def take(ref, pieces, level, lo, hi):
+        part = 0 if lo == 0 else 1
+        return [ref[at[part] : at[part] + hi - lo] for at in sz.x_offsets(pieces)[level]]
+
+    def halves(value):
+        return [jnp.where(lower, v, 0.0) for v in (value, pltpu.roll(value, LANES // 2, 1))]
+
+    for level in range(3):
+        m, w = sz.main[level], sz.ly[level]
+        for lo, hi in ((0, m), (m, w)):
+            n = take(rn, sz.xp_pieces, level, lo, hi)
+            p = take(rp, sz.xn_pieces, level, lo, hi)
+            if level == 0:
+                for q in range(4):
+                    g1[l1 - 1, 0, q, lo:hi] += -RHO * n[q]
+                    g1[l1 - 1, 1, q, lo:hi] += n[q]
+                    g1[0, 0, q, lo:hi] += p[q]
+                    g1[0, 1, q, lo:hi] += RHO * p[q]
+            elif level == 1:
+                for q in range(2):
+                    h0, h1 = n[q], n[2 + q]
+                    g2[l2 - 2, 0, q, lo:hi] += -RHO * h0
+                    g2[l2 - 2, 1, q, lo:hi] += h0
+                    g2[l2 - 1, 0, q, lo:hi] += KAPPA * h0 - RHO * h1
+                    g2[l2 - 1, 1, q, lo:hi] += h1
+                    g2[0, 0, q, lo:hi] += p[q]
+                    g2[0, 1, q, lo:hi] += p[2 + q]
+                    g2[1, 0, q, lo:hi] += p[4 + q]
+                    g2[1, 1, q, lo:hi] += RHO * p[4 + q]
+            else:
+                n, p = [halves(v) for v in n], [halves(v) for v in p]
+                for q in range(2):
+                    g3[l3 - 2, 0, q, lo:hi] += -RHO * n[0][q]
+                    g3[l3 - 2, 1, q, lo:hi] += n[0][q]
+                    g3[l3 - 1, 0, q, lo:hi] += n[1][q]
+                    g3[l3 - 1, 1, q, lo:hi] += n[2][q]
+                    g3[0, 0, q, lo:hi] += p[0][q]
+                    g3[0, 1, q, lo:hi] += p[1][q]
+                    g3[1, 0, q, lo:hi] += p[2][q]
+                    g3[1, 1, q, lo:hi] += RHO * p[2][q]
 
 
 def pack_y(sz, g1, g2, g3, mp, mn):
@@ -299,18 +339,49 @@
     return lax.broadcasted_iota(jnp.int32, shape, 1) < limit
 
 
-def inverse(sz, details, emit, i1, i2, i3, ta, v3, b3, v2, b2, v1, b1):
+def level_1_columns(sz, details, s, xb, tb, coarse, ta, v1, index):
+    low = coarse if coarse is not None else details(0, s, xb, tb, None)
+    high = details(0, s, xb, 2 + tb, None)
+    y_synthesis(low, high, sz.y // 2, ta.at[s, xb * 2 + tb, 0 : sz.py[0]], v1, index, 0)
+
+
+def times_back(sz, v_low, v_high, i1):
+    v = jnp.concatenate([v_low, v_high], axis=-1)
+    return dot_parts(v.reshape(-1, sz.t), i1).reshape(v.shape)
+
+
+def inner_inverse(sz, details, i1, va, ba, ta, v1):
+    l1 = sz.lx[0]
+
+    def rows(s, carry):
+        level_1_columns(sz, details, s, 0, 1, None, ta, va, (s,))
+        level_1_columns(sz, details, s, 1, 0, None, ta, v1, (s, 0))
+        level_1_columns(sz, details, s, 1, 1, None, ta, v1, (s, 1))
+        return carry
+
+    lax.fori_loop(1, l1 - 1, rows, 0)
+    step = 8
+    for s0 in range(1, l1 - 1, step):
+        n = min(step, l1 - 1 - s0)
+        ba[s0 : s0 + n] = times_back(sz, v1[s0 : s0 + n, 0], v1[s0 : s0 + n, 1], i1)
+
+
+def inverse(sz, details, emit, va, ba, i1, i2, i3, ta1, ta, v3, b3, v2, b2, v1, b1, ve):
     y, t = sz.y, sz.t
-    half = t // 2
     p1, p2, p3 = sz.py
     l1, l2, l3 = sz.lx
     third = lane_below(t // 8, (p3, LANES))
 
+    for e, s in enumerate((0, l1 - 1)):
+        level_1_columns(sz, details, s, 0, 1, None, ta1, va, (s,))
+        level_1_columns(sz, details, s, 1, 0, None, ta1, ve, (e, 0))
+        level_1_columns(sz, details, s, 1, 1, None, ta1, ve, (e, 1))
+
     for s in range(l3):
         for xb in range(2):
             low = details(2, s, xb, 0, third if xb == 0 else None)
             high = details(2, s, xb, 1, None)
-            y_synthesis(low, high, sz.ly[1] // 2, ta.at[2, s, xb, 0:p3], v3, (s, xb), 0)
+            y_synthesis(low, high, sz.ly[1] // 2, ta.at[1, s, xb, 0:p3], v3, (s, xb), 0)
     b3[...] = dot_parts(v3[...].reshape(l3 * 2 * p2, LANES), i3).reshape(l3, 2, p2, LANES)
 
     second = lane_below(t // 4, (p2, LANES))
@@ -322,44 +393,37 @@
                 if xb == 0:
                     low = jnp.where(second, coarse, low)
                 high = details(1, s, xb, 1, None)
-                y_synthesis(low, high, (sz.ly[0] + 1) // 2, ta.at[1, s, xb, 0:p2], v2, (s, xb), 7)
+                y_synthesis(low, high, (sz.ly[0] + 1) // 2, ta.at[0, s, xb, 0:p2], v2, (s, xb), 7)
     b2[...] = dot_parts(v2[:, :, 8 : 8 + p1, :].reshape(l2 * 2 * p1, LANES), i2).reshape(l2, 2, p1, LANES)
 
-    def level_1(s, coarse):
-        for xb in range(2):
-            for tb in range(2):
-                if xb == 0 and tb == 0:
-                    low = coarse
-                else:
-                    low = details(0, s, xb, tb, None)
-                high = details(0, s, xb, 2 + tb, None)
-                y_synthesis(low, high, y // 2, ta.at[0, s, xb * 2 + tb, 0:p1], v1, (s, xb, tb), 0)
+    edge = times_back(sz, ve[:, 0], ve[:, 1], i1)
+    ba[0] = edge[0]
+    ba[l1 - 1] = edge[1]
 
     def coarse_rows(p):
         return lattice_t(b2[p + 1, 0], b2[p + 1, 1], b2[p, 0], b2[p, 1])
 
-    level_1(0, coarse_rows(0)[1])
+    level_1_columns(sz, details, 0, 0, 0, coarse_rows(0)[1], ta1, v1, (0,))
 
     def pair_1(p, carry):
         even, odd = coarse_rows(p)
-        level_1(2 * p - 1, even)
-        level_1(2 * p, odd)
+        level_1_columns(sz, details, 2 * p - 1, 0, 0, even, ta1, v1, (2 * p - 1,))
+        level_1_columns(sz, details, 2 * p, 0, 0, odd, ta1, v1, (2 * p,))
         return carry
 
     lax.fori_loop(1, l2 - 1, pair_1, 0)
 
-    step = 6
+    step = 9
     for s0 in range(0, l1, step):
         n = min(step, l1 - s0)
-        v = jnp.concatenate([v1[s0 : s0 + n, :, 0], v1[s0 : s0 + n, :, 1]], axis=-1)
-        b1[s0 : s0 + n] = dot_parts(v.reshape(n * 2 * y, t), i1).reshape(n, 2, y, t)
+        b1[s0 : s0 + n] = times_back(sz, v1[s0 : s0 + n], va[s0 : s0 + n], i1)
 
     def rows_x(p, carry):
-        even, odd = lattice_t(b1[p + 1, 0], b1[p + 1, 1], b1[p, 0], b1[p, 1])
+        even, odd = lattice_t(b1[p + 1], ba[p + 1], b1[p], ba[p])
         emit(p, even, odd)
         return carry
 
-    lax.fori_loop(0, sz.x // 2, rows_x, 0)
+    return rows_x
 
 
 def border(sz, u_ref):
@@ -368,48 +432,47 @@
     u_ref[sz.x + 2 : sz.x + 4] = zeros
 
 
-def first_kernel(sz, c_ref, f1, f2, f3, w_ref, g1, g2, g3, mp, mn, u, *scratch):
+def first_kernel(sz, c_hbm, f_hbm, w_ref, g1, g2, g3, mp, mn, c, fv, f1, f2, f3, u, sems, *scratch):
+    step = 8
+    chunks = range(0, sz.x, step)
+    copies = [pltpu.make_async_copy(c_hbm.at[x0 : x0 + step], c.at[x0 : x0 + step], sems.at[i])
+              for i, x0 in enumerate(chunks)]
+    matrices = pltpu.make_async_copy(f_hbm, fv, sems.at[len(copies)])
+    for copy in copies + [matrices]:
+        copy.start()
     border(sz, u)
 
     def rows(x, carry):
-        value = c_ref[x].astype(jnp.float32) * (1.0 / 64.0)
+        value = c[x].astype(jnp.float32) * (1.0 / 64.0)
         weight = 1.0 / (1.0 + jnp.abs(value))
         w_ref[x] = weight
         u[x + 2] = weight * value
         return carry
 
-    lax.fori_loop(0, sz.x, rows, 0)
+    for x0, copy in zip(chunks, copies):
+        copy.wait()
+        lax.fori_loop(x0, x0 + step, rows, 0)
+    matrices.wait()
+    unpack_matrices(fv, f1, f2, f3)
     forward(sz, u, f1, f2, f3, g1, g2, g3, *scratch)
+    pack_y(sz, g1, g2, g3, mp, mn)
+
+
+def edge_kernel(sz, g1i, g2i, g3i, rn, rp, g1, g2, g3, mp, mn):
+    fix_y(sz, g1, g2, g3, rn, rp)
     pack_x(sz, g1, g2, g3, mp, mn)
 
 
-def edge_kernel(sz, g1i, g2i, g3i, rn, rp, g1, g2, g3, mp, mn):
-    fix_x(sz, g1, g2, g3, rn, rp)
-    pack_y(sz, g1, g2, g3, mp, mn)
-
-
-def middle_kernel(sz, g1i, g2i, g3i, rn, rp, w_ref, f1, f2, f3, i1, i2, i3,
-                  g1, g2, g3, q1, q2, q3, mp, mn, u, ta, v3, b3, v2, b2, v1, b1, *scratch):
-    fix_y(sz, g1, g2, g3, rn, rp)
-    border(sz, u)
-
+def first_details(g1, g2, g3):
     def details(level, s, xb, q, approx_lanes):
         value = (g1, g2, g3)[level][s, xb, q]
         small = shrink(value)
         return small if approx_lanes is None else jnp.where(approx_lanes, value, small)
 
-    def emit(p, even, odd):
-        u[2 * p + 2] = w_ref[2 * p] * even
-        u[2 * p + 3] = w_ref[2 * p + 1] * odd
-
-    inverse(sz, details, emit, i1, i2, i3, ta, v3, b3, v2, b2, v1, b1)
-    forward(sz, u, f1, f2, f3, q1, q2, q3, *scratch)
-    pack_x(sz, q1, q2, q3, mp, mn)
-
-
-def last_kernel(sz, q1i, q2i, q3i, rn, rp, g1, g2, g3, i1, i2, i3, q1, q2, q3, out, ta, v3, b3, v2, b2, v1, b1):
-    fix_y(sz, q1, q2, q3, rn, rp)
-
+    return details
+
+
+def second_details(g1, g2, g3, q1, q2, q3):
     def details(level, s, xb, q, approx_lanes):
         first = (g1, g2, g3)[level][s, xb, q]
         second = (q1, q2, q3)[level][s, xb, q]
@@ -418,57 +481,121 @@
             return small
         return jnp.where(approx_lanes, first + (first - second), small)
 
+    return details
+
+
+def inner_first_kernel(sz, g1, iv, va, ba, i1, i2, i3, ta, v1):
+    unpack_matrices(iv, i1, i2, i3)
+    inner_inverse(sz, first_details(g1, None, None), i1, va, ba, ta, v1)
+
+
+def inner_last_kernel(sz, g1, q1, iv, va, ba, i1, i2, i3, ta, v1):
+    unpack_matrices(iv, i1, i2, i3)
+    inner_inverse(sz, second_details(g1, None, None, q1, None, None), i1, va, ba, ta, v1)
+
+
+def middle_kernel(sz, g1i, g2i, g3i, vai, bai, rn, rp, w_ref, fv, iv, g1, g2, g3, va, ba, q1, q2, q3, mp, mn,
+                  u, f1, f2, f3, i1, i2, i3, ta1, ta, v3, b3, v2, b2, v1, b1, ve, *scratch):
+    unpack_matrices(fv, f1, f2, f3)
+    unpack_matrices(iv, i1, i2, i3)
+    fix_x(sz, g1, g2, g3, rn, rp)
+    border(sz, u)
+
+    def emit(p, even, odd):
+        u[2 * p + 2] = w_ref[2 * p] * even
+        u[2 * p + 3] = w_ref[2 * p + 1] * odd
+
+    rows = inverse(sz, first_details(g1, g2, g3), emit, va, ba, i1, i2, i3, ta1, ta, v3, b3, v2, b2, v1, b1, ve)
+    lax.fori_loop(0, sz.x // 2, rows, 0)
+    forward(sz, u, f1, f2, f3, q1, q2, q3, *scratch)
+    pack_y(sz, q1, q2, q3, mp, mn)
+
+
+def last_kernel(sz, q1i, q2i, q3i, vai, bai, rn, rp, g1, g2, g3, iv, q1, q2, q3, va, ba, out_hbm,
+                out, sems, i1, i2, i3, ta1, ta, v3, b3, v2, b2, v1, b1, ve):
+    unpack_matrices(iv, i1, i2, i3)
+    fix_x(sz, q1, q2, q3, rn, rp)
+
     def emit(p, even, odd):
         out[2 * p] = even
         out[2 * p + 1] = odd
 
-    inverse(sz, details, emit, i1, i2, i3, ta, v3, b3, v2, b2, v1, b1)
-
-
-def call(kernel, sz, outs, scratch, aliases, *args):
-    vmem = pl.BlockSpec(memory_space=pltpu.VMEM)
+    details = second_details(g1, g2, g3, q1, q2, q3)
+    rows = inverse(sz, details, emit, va, ba, i1, i2, i3, ta1, ta, v3, b3, v2, b2, v1, b1, ve)
+    step = 8
+    copies = []
+    for i, x0 in enumerate(range(0, sz.x, step)):
+        lax.fori_loop(x0 // 2, (x0 + step) // 2, rows, 0)
+        copies.append(pltpu.make_async_copy(out.at[x0 : x0 + step], out_hbm.at[x0 : x0 + step], sems.at[i]))
+        copies[-1].start()
+    for copy in copies:
+        copy.wait()
+
+
+VMEM = pltpu.MemorySpace.VMEM
+HBM = pltpu.MemorySpace.HBM
+
+
+def call(kernel, sz, outs, scratch, aliases, *args, ins_hbm=(), outs_hbm=(), flops=0):
+    def specs(n, in_hbm):
+        return [pl.BlockSpec(memory_space=HBM if k in in_hbm else VMEM) for k in range(n)]
+
     return pl.pallas_call(
         functools.partial(kernel, sz),
         out_shape=[jax.ShapeDtypeStruct(s, jnp.float32) for s in outs],
-        in_specs=[vmem] * len(args),
-        out_specs=[vmem] * len(outs),
-        scratch_shapes=[pltpu.VMEM(s, jnp.float32) for s in scratch],
+        in_specs=specs(len(args), ins_hbm),
+        out_specs=specs(len(outs), outs_hbm),
+        scratch_shapes=scratch,
         input_output_aliases=aliases,
+        cost_estimate=pl.CostEstimate(flops=flops, bytes_accessed=flops // 100, transcendentals=0) if flops else None,
         compiler_params=pltpu.CompilerParams(vmem_limit_bytes=36 * 2**20),
     )(*args)
 
 
 def on_device(counts):
     sz = Sizes(*counts.shape)
-    t = sz.t
-    fw = [time_matrix(t, t), time_matrix(t // 2, LANES), time_matrix(t // 4, LANES)]
-    f = [jnp.asarray(parts_of(m)) for m in fw]
-    i = [jnp.asarray(parts_of(m.T)) for m in fw]
+    x, y, t = counts.shape
     l1, l2, l3 = sz.lx
     p1, p2, p3 = sz.py
-    wide = (sz.x, sz.y, sz.t)
-    u = (sz.x + 4, sz.y, sz.t)
-    fw_scratch = [(l1, 2, sz.y, t), (l1, 2, 2, sz.zrows[0], LANES), (l2, 2, p1, LANES), (l2, 2, sz.zrows[1], LANES),
-                  (l3, 2, p2, LANES), (l3, 2, sz.zrows[2], LANES)]
-    bw_scratch = [(3, l1, 4, p1 + 8, LANES), (l3, 2, p2, LANES), (l3, 2, p2, LANES), (l2, 2, p1 + 8, LANES),
-                  (l2, 2, p1, LANES), (l1, 2, 2, sz.y, LANES), (l1, 2, sz.y, t)]
+    matrices = [time_matrix(t, t), time_matrix(t // 2, LANES), time_matrix(t // 4, LANES)]
+    f = jnp.asarray(pack_matrices(*matrices))
+    i = jnp.asarray(pack_matrices(*[m.T for m in matrices]))
+
+    def f32(*shapes):
+        return [pltpu.VMEM(s, jnp.float32) for s in shapes]
+
+    parts = [pltpu.VMEM((2, n, n), jnp.bfloat16) for n in (t, LANES, LANES)]
+    u = f32((x + 4, y, t))
+    sems = [pltpu.SemaphoreType.DMA((x // 8 + 1,))]
+    fw = f32((l1, 2, y, t), (l1, 2, 2, sz.zrows[0], LANES), (l2, 2, p1, LANES), (l2, 2, sz.zrows[1], LANES),
+             (l3, 2, p2, LANES), (l3, 2, sz.zrows[2], LANES))
+    ta1 = f32((l1, 4, p1 + 8, LANES))
+    bw = ta1 + f32((2, l2, 2, p2 + 8, LANES), (l3, 2, p2, LANES), (l3, 2, p2, LANES), (l2, 2, p1 + 8, LANES),
+                   (l2, 2, p1, LANES), (l1, y, LANES), (l1, y, t), (2, 2, y, LANES))
     to_prev, to_next = (sz.xp, LANES), (sz.xn, LANES)
     y_prev, y_next = (sz.yp, LANES), (sz.yn, LANES)
-    same = {0: 0, 1: 1, 2: 2}
+    halves = [(l1, y, LANES), (l1, y, t)]
+    inner = parts + ta1 + f32((l1, 2, y, LANES))
+    work = 6 * l1 * y * t * t
 
     def exchange(g, mp, mn):
-        rn = shifted(mp, "gx", -1)
-        rp = shifted(mn, "gx", 1)
-        *g, mp, mn = call(edge_kernel, sz, sz.g + [y_prev, y_next], [], same, *g, rn, rp)
-        return g, shifted(mp, "gy", -1), shifted(mn, "gy", 1)
-
-    weight, *g, mp, mn = call(first_kernel, sz, [wide] + sz.g + [to_prev, to_next], [u] + fw_scratch, {}, counts, *f)
+        rn, rp = shifted(mp, "gy", -1), shifted(mn, "gy", 1)
+        *g, mp, mn = call(edge_kernel, sz, sz.g + [to_prev, to_next], [], {0: 0, 1: 1, 2: 2}, *g, rn, rp)
+        return g, shifted(mp, "gx", -1), shifted(mn, "gx", 1)
+
+    weight, *g, mp, mn = call(first_kernel, sz, [(x, y, t)] + sz.g + [y_prev, y_next],
+                              [pltpu.VMEM((x, y, t), jnp.int32)] + f32(f.shape) + parts + u + sems + fw,
+                              {}, counts, f, ins_hbm=(0, 1))
     g, rn, rp = exchange(g, mp, mn)
-    *rest, mp, mn = call(middle_kernel, sz, sz.g + sz.g + [to_prev, to_next], [u] + bw_scratch + fw_scratch, same,
-                         *g, rn, rp, weight, *f, *i)
-    g, q = rest[:3], rest[3:]
+    kept = call(inner_first_kernel, sz, halves, inner, {}, g[0], i, flops=work)
+    same = {k: k for k in range(5)}
+    *rest, mp, mn = call(middle_kernel, sz, sz.g + halves + sz.g + [y_prev, y_next], u + parts + parts + bw + fw, same,
+                         *g, *kept, rn, rp, weight, f, i)
+    g, q = rest[:3], rest[5:]
     q, rn, rp = exchange(q, mp, mn)
-    return call(last_kernel, sz, sz.g + [wide], bw_scratch, same, *q, rn, rp, *g, *i)[3]
+    kept = call(inner_last_kernel, sz, halves, inner, {}, g[0], q[0], i, flops=work)
+    return call(last_kernel, sz, sz.g + halves + [(x, y, t)], f32((x, y, t)) + sems + parts + bw, same,
+                *q, *kept, rn, rp, *g, i, outs_hbm=(5,))[5]
 
 
 def solution(mesh):

time: 54.8 us -> 46.1 us (0.84); the launches traced: 53.9 us -> 45.9 us
  waiting for transfers between devices: 21.5 us -> 15 us
  local copies, waits for them, and re-layouts: 4.23 us -> 2.59 us
  Pallas kernels: 15.5 us -> 16.1 us
    ppermute x8, waiting for transfers between devices: 21.5 us -> 15 us  [shifted(): return lax.ppermute(x, axis, [(i, (i + by) % count) for i in range(count)])]
    unnamed x14 -> x6, local copies, waits for them, and re-layouts: 4.23 us -> 2.59 us
    pallas_call x5 -> x7, Pallas kernels: 15.5 us -> 16.1 us  [call(): pl.pallas_call(functools.partial(kernel, sz), out_shape=[jax.ShapeDtypeSt...]
  transfers between devices with their start and end apart: 8 -> 8, of which waited for: 6 -> 5; matrix products, arithmetic and copies ran while one was open for 0% -> 0% of each run, Pallas kernels for 0% -> 5%
where the time goes in v1:
time: 46.1 us; the launch traced here: 45.9 us
  Pallas kernels  16.1 us (35%)
  waiting for transfers between devices  15 us (33%)
  starting transfers between devices  12.1 us (26%)
  local copies, waits for them, and re-layouts  2.59 us (6%)
    pallas_call x7, Pallas kernels, call(): pl.pallas_call(functools.partial(kernel, sz), out_shape=[jax.ShapeDtypeSt...  16.1 us
    ppermute x8, waiting for transfers between devices, shifted(): return lax.ppermute(x, axis, [(i, (i + by) % count) for i in range(count)])  15 us
    ppermute x8, starting transfers between devices, shifted(): return lax.ppermute(x, axis, [(i, (i + by) % count) for i in range(count)])  12.1 us
    unnamed x6, local copies, waits for them, and re-layouts  2.59 us
  transfers between devices with their start and end apart: 8, of which 5 were waited for; matrix products, arithmetic and copies ran while one was open for 0% of the time, Pallas kernels for 5%

profile of v1, /device:TPU:0, one launch (start us, length us, event | category | flops | bytes accessed | tf_op | source)
XLA Modules:
  0.0 45.9 jit_solution(14996156291189584423)
XLA Ops:
  0.0 0.0 copy-start.1
  0.0 1.6 %copy-done.1 = s32[32,64,256]{2,1,0:T(8,128)S(1)} copy-done((s32[32,64,256]{2,1,0:T(8,128)S(1)}, s32[32,64,256]{2,1,0:T(8,128)}, u32[]{:S(2)}) %copy-start.1) | copy-done | bytes 2097176
  1.6 0.0 copy-start.2
  1.6 1.0 %copy-done.2 = f32[384,256]{1,0:T(8,128)S(1)} copy-done((f32[384,256]{1,0:T(8,128)S(1)}, f32[384,256]{1,0:T(8,128)}, u32[]{:S(2)}) %copy-start.2) | copy-done | bytes 393240
  2.6 4.2 %shard_map.37 = (f32[32,64,256]{2,1,0:T(8,128)S(1)}, f32[17,2,4,40,128]{4,3,2,1,0:T(8,128)S(1)}, f32[10,2,2,24,128]{4,3,2,1,0:T(8,128)S(1)}, f32[6,2,2,16,128]{4...) custom-call(s32[32,64,256]{2,1,0:T(8,128)S(1)} %copy-done.1, f32[384,256]{1,0:T(8,128)S(1)} %copy-done.2), custom_call_target="tpu_custom_call" | custom-call | tf_op jit(solution)/shard_map/pallas_call | solution.py:543
  6.8 0.0 copy-start
  6.9 0.5 %collective-permute-start.1 = (f32[168,128]{1,0:T(8,128)S(1)}, f32[168,128]{1,0:T(8,128)S(1)}, u32[]{:S(2)}, u32[]{:S(2)}) collective-permute-start(f32[168,128]{1,0:T(8,128)S(1)} %get-tuple-element.38), channel_id=1, source_target_pairs={{0,1},{1,2},{2,3},{3,0},{4,5},{5,6},{6,7},{7,4},{8,9},{9,10},{10,1... | collective-permute-start | bytes 258056 | tf_op jit(solution)/shard_map/ppermute | solution.py:24
  7.4 2.0 %collective-permute-start = (f32[144,128]{1,0:T(8,128)S(1)}, f32[144,128]{1,0:T(8,128)S(1)}, u32[]{:S(2)}, u32[]{:S(2)}) collective-permute-start(f32[144,128]{1,0:T(8,128)S(1)} %get-tuple-element.37), channel_id=1, source_target_pairs={{0,3},{1,0},{2,1},{3,2},{4,7},{5,4},{6,5},{7,6},{8,11},{9,8},{10,9... | collective-permute-start | bytes 221192 | tf_op jit(solution)/shard_map/ppermute | solution.py:24
  9.4 2.7 %collective-permute-done.rn = f32[144,128]{1,0:T(8,128)S(1)} collective-permute-done((f32[144,128]{1,0:T(8,128)S(1)}, f32[144,128]{1,0:T(8,128)S(1)}, u32[]{:S(2)}, u32[]{:S(2)}) %collective-permute-start) | collective-permute-done | bytes 73760 | tf_op jit(solution)/shard_map/ppermute | solution.py:24
  12.0 0.0 collective-permute-done.1.rp
  12.0 0.3 shard_map.38
  12.3 1.9 %collective-permute-start.3 = (f32[272,128]{1,0:T(8,128)S(1)}, f32[272,128]{1,0:T(8,128)S(1)}, u32[]{:S(2)}, u32[]{:S(2)}) collective-permute-start(f32[272,128]{1,0:T(8,128)S(1)} %get-tuple-element.45), channel_id=1, source_target_pairs={{0,4},{4,8},{8,12},{12,0},{1,5},{5,9},{9,13},{13,1},{2,6},{6,10},{... | collective-permute-start | bytes 417800 | tf_op jit(solution)/shard_map/ppermute | solution.py:24
  14.2 2.1 %collective-permute-start.2 = (f32[240,128]{1,0:T(8,128)S(1)}, f32[240,128]{1,0:T(8,128)S(1)}, u32[]{:S(2)}, u32[]{:S(2)}) collective-permute-start(f32[240,128]{1,0:T(8,128)S(1)} %get-tuple-element.44), channel_id=1, source_target_pairs={{0,12},{4,0},{8,4},{12,8},{1,13},{5,1},{9,5},{13,9},{2,14},{6,2},{... | collective-permute-start | bytes 368648 | tf_op jit(solution)/shard_map/ppermute | solution.py:24
  16.3 0.0 copy-done
  16.3 1.1 %shard_map.39 = (f32[17,64,128]{2,1,0:T(8,128)S(1)}, f32[17,64,256]{2,1,0:T(8,128)S(1)}) custom-call(f32[17,2,4,40,128]{4,3,2,1,0:T(8,128)S(1)} %get-tuple-element.39.g1.g1i, f32[384,256]{1,0:T(8,128)S(1)} %copy-done), custom_call_target="tpu_custom_call" | custom-call | flops 427819008 | bytes 4278190 | tf_op jit(solution)/shard_map/pallas_call | solution.py:543
  17.5 5.8 %collective-permute-done.2.rn = f32[240,128]{1,0:T(8,128)S(1)} collective-permute-done((f32[240,128]{1,0:T(8,128)S(1)}, f32[240,128]{1,0:T(8,128)S(1)}, u32[]{:S(2)}, u32[]{:S(2)}) %collective-permute-start.2) | collective-permute-done | bytes 122912 | tf_op jit(solution)/shard_map/ppermute | solution.py:24
  23.3 0.0 collective-permute-done.3.rp
  23.3 5.4 %shard_map.40 = (f32[17,2,4,40,128]{4,3,2,1,0:T(8,128)S(1)}, f32[10,2,2,24,128]{4,3,2,1,0:T(8,128)S(1)}, f32[6,2,2,16,128]{4,3,2,1,0:T(8,128)S(1)}, f32[17,64,12...) custom-call(f32[17,2,4,40,128]{4,3,2,1,0:T(8,128)S(1)} %get-tuple-el, ...), custom_call_target="tpu_custom_call", output_to_operand_aliasing={{0}: (0, {}), {1}: (1, {}), {2}: (2, {}), {3}: (3, {}), {4}... | custom-call | tf_op jit(solution)/shard_map/pallas_call | solution.py:543
  28.7 0.2 collective-permute-start.5
  28.9 1.6 %collective-permute-start.4 = (f32[144,128]{1,0:T(8,128)S(1)}, f32[144,128]{1,0:T(8,128)S(1)}, u32[]{:S(2)}, u32[]{:S(2)}) collective-permute-start(f32[144,128]{1,0:T(8,128)S(1)} %get-tuple-element.50), channel_id=1, source_target_pairs={{0,3},{1,0},{2,1},{3,2},{4,7},{5,4},{6,5},{7,6},{8,11},{9,8},{10,9... | collective-permute-start | bytes 221192 | tf_op jit(solution)/shard_map/ppermute | solution.py:24
  30.5 2.0 %collective-permute-done.4.rn = f32[144,128]{1,0:T(8,128)S(1)} collective-permute-done((f32[144,128]{1,0:T(8,128)S(1)}, f32[144,128]{1,0:T(8,128)S(1)}, u32[]{:S(2)}, u32[]{:S(2)}) %collective-permute-start.4) | collective-permute-done | bytes 73760 | tf_op jit(solution)/shard_map/ppermute | solution.py:24
  32.5 0.2 collective-permute-done.5.rp
  32.7 0.3 shard_map.41
  33.0 0.7 %collective-permute-start.7 = (f32[272,128]{1,0:T(8,128)S(1)}, f32[272,128]{1,0:T(8,128)S(1)}, u32[]{:S(2)}, u32[]{:S(2)}) collective-permute-start(f32[272,128]{1,0:T(8,128)S(1)} %get-tuple-element.59), channel_id=1, source_target_pairs={{0,4},{4,8},{8,12},{12,0},{1,5},{5,9},{9,13},{13,1},{2,6},{6,10},{... | collective-permute-start | bytes 417800 | tf_op jit(solution)/shard_map/ppermute | solution.py:24
  33.7 3.2 %collective-permute-start.6 = (f32[240,128]{1,0:T(8,128)S(1)}, f32[240,128]{1,0:T(8,128)S(1)}, u32[]{:S(2)}, u32[]{:S(2)}) collective-permute-start(f32[240,128]{1,0:T(8,128)S(1)} %get-tuple-element.58), channel_id=1, source_target_pairs={{0,12},{4,0},{8,4},{12,8},{1,13},{5,1},{9,5},{13,9},{2,14},{6,2},{... | collective-permute-start | bytes 368648 | tf_op jit(solution)/shard_map/ppermute | solution.py:24
  36.9 1.3 %shard_map.42 = (f32[17,64,128]{2,1,0:T(8,128)S(1)}, f32[17,64,256]{2,1,0:T(8,128)S(1)}) custom-call(f32[17,2,4,40,128]{4,3,2,1,0:T(8,128)S(1)} %get-tuple-element.55.g1, f32[17,2,4,40,128]{4,3,2,1,0:T(8,128)S(1)} %get-tuple-element.52.q1.q1i, f32[384,256]{1,0:T(8,128)S(1)} %copy-done), custom_call_target="tpu_custom_call" | custom-call | flops 427819008 | bytes 4278190 | tf_op jit(solution)/shard_map/pallas_call | solution.py:543
  38.2 4.3 %collective-permute-done.6.rn = f32[240,128]{1,0:T(8,128)S(1)} collective-permute-done((f32[240,128]{1,0:T(8,128)S(1)}, f32[240,128]{1,0:T(8,128)S(1)}, u32[]{:S(2)}, u32[]{:S(2)}) %collective-permute-start.6) | collective-permute-done | bytes 122912 | tf_op jit(solution)/shard_map/ppermute | solution.py:24
  42.5 0.0 collective-permute-done.7.rp
  42.5 3.4 %shard_map.43 = (f32[17,2,4,40,128]{4,3,2,1,0:T(8,128)S(1)}, f32[10,2,2,24,128]{4,3,2,1,0:T(8,128)S(1)}, f32[6,2,2,16,128]{4,3,2,1,0:T(8,128)S(1)}, f32[17,64,12...) custom-call(f32[17,2,4,40,128]{4,3,2,1,0:T(8,128)S(1)} %get-tuple-el, ...), custom_call_target="tpu_custom_call", output_to_operand_aliasing={{0}: (0, {}), {1}: (1, {}), {2}: (2, {}), {3}: (3, {}), {4}... | custom-call | tf_op jit(solution)/shard_map/pallas_call | solution.py:543
Async XLA Ops:
  0.0 1.6 %copy-start.1 = (s32[32,64,256]{2,1,0:T(8,128)S(1)}, s32[32,64,256]{2,1,0:T(8,128)}, u32[]{:S(2)}) copy-start(s32[32,64,256]{2,1,0:T(8,128)} %c_hbm.1) | copy-start | bytes 6291460
  1.6 1.0 %copy-start.2 = (f32[384,256]{1,0:T(8,128)S(1)}, f32[384,256]{1,0:T(8,128)}, u32[]{:S(2)}) copy-start(f32[384,256]{1,0:T(8,128)} %constant.4.clone.f_hbm.fv) | copy-start | bytes 1179652
  6.8 9.5 %copy-start = (f32[384,256]{1,0:T(8,128)S(1)}, f32[384,256]{1,0:T(8,128)}, u32[]{:S(2)}) copy-start(f32[384,256]{1,0:T(8,128)} %constant.5.clone.iv) | copy-start | bytes 1179652
  6.9 5.2 %collective-permute-start.1 = (f32[168,128]{1,0:T(8,128)S(1)}, f32[168,128]{1,0:T(8,128)S(1)}, u32[]{:S(2)}, u32[]{:S(2)}) collective-permute-start(f32[168,128]{1,0:T(8,128)S(1)} %get-tuple-element.38), channel_id=1, source_target_pairs={{0,1},{1,2},{2,3},{3,0},{4,5},{5,6},{6,7},{7,4},{8,9},{9,10},{10,1... | collective-permute-start | bytes 258056 | tf_op jit(solution)/shard_map/ppermute | solution.py:24
  7.4 4.6 %collective-permute-start = (f32[144,128]{1,0:T(8,128)S(1)}, f32[144,128]{1,0:T(8,128)S(1)}, u32[]{:S(2)}, u32[]{:S(2)}) collective-permute-start(f32[144,128]{1,0:T(8,128)S(1)} %get-tuple-element.37), channel_id=1, source_target_pairs={{0,3},{1,0},{2,1},{3,2},{4,7},{5,4},{6,5},{7,6},{8,11},{9,8},{10,9... | collective-permute-start | bytes 221192 | tf_op jit(solution)/shard_map/ppermute | solution.py:24
  12.3 11.0 %collective-permute-start.3 = (f32[272,128]{1,0:T(8,128)S(1)}, f32[272,128]{1,0:T(8,128)S(1)}, u32[]{:S(2)}, u32[]{:S(2)}) collective-permute-start(f32[272,128]{1,0:T(8,128)S(1)} %get-tuple-element.45), channel_id=1, source_target_pairs={{0,4},{4,8},{8,12},{12,0},{1,5},{5,9},{9,13},{13,1},{2,6},{6,10},{... | collective-permute-start | bytes 417800 | tf_op jit(solution)/shard_map/ppermute | solution.py:24
  14.2 9.1 %collective-permute-start.2 = (f32[240,128]{1,0:T(8,128)S(1)}, f32[240,128]{1,0:T(8,128)S(1)}, u32[]{:S(2)}, u32[]{:S(2)}) collective-permute-start(f32[240,128]{1,0:T(8,128)S(1)} %get-tuple-element.44), channel_id=1, source_target_pairs={{0,12},{4,0},{8,4},{12,8},{1,13},{5,1},{9,5},{13,9},{2,14},{6,2},{... | collective-permute-start | bytes 368648 | tf_op jit(solution)/shard_map/ppermute | solution.py:24
  28.7 4.0 %collective-permute-start.5 = (f32[168,128]{1,0:T(8,128)S(1)}, f32[168,128]{1,0:T(8,128)S(1)}, u32[]{:S(2)}, u32[]{:S(2)}) collective-permute-start(f32[168,128]{1,0:T(8,128)S(1)} %get-tuple-element.51), channel_id=1, source_target_pairs={{0,1},{1,2},{2,3},{3,0},{4,5},{5,6},{6,7},{7,4},{8,9},{9,10},{10,1... | collective-permute-start | bytes 258056 | tf_op jit(solution)/shard_map/ppermute | solution.py:24
  28.9 3.6 %collective-permute-start.4 = (f32[144,128]{1,0:T(8,128)S(1)}, f32[144,128]{1,0:T(8,128)S(1)}, u32[]{:S(2)}, u32[]{:S(2)}) collective-permute-start(f32[144,128]{1,0:T(8,128)S(1)} %get-tuple-element.50), channel_id=1, source_target_pairs={{0,3},{1,0},{2,1},{3,2},{4,7},{5,4},{6,5},{7,6},{8,11},{9,8},{10,9... | collective-permute-start | bytes 221192 | tf_op jit(solution)/shard_map/ppermute | solution.py:24
  33.0 9.6 %collective-permute-start.7 = (f32[272,128]{1,0:T(8,128)S(1)}, f32[272,128]{1,0:T(8,128)S(1)}, u32[]{:S(2)}, u32[]{:S(2)}) collective-permute-start(f32[272,128]{1,0:T(8,128)S(1)} %get-tuple-element.59), channel_id=1, source_target_pairs={{0,4},{4,8},{8,12},{12,0},{1,5},{5,9},{9,13},{13,1},{2,6},{6,10},{... | collective-permute-start | bytes 417800 | tf_op jit(solution)/shard_map/ppermute | solution.py:24
  33.7 8.9 %collective-permute-start.6 = (f32[240,128]{1,0:T(8,128)S(1)}, f32[240,128]{1,0:T(8,128)S(1)}, u32[]{:S(2)}, u32[]{:S(2)}) collective-permute-start(f32[240,128]{1,0:T(8,128)S(1)} %get-tuple-element.58), channel_id=1, source_target_pairs={{0,12},{4,0},{8,4},{12,8},{1,13},{5,1},{9,5},{13,9},{2,14},{6,2},{... | collective-permute-start | bytes 368648 | tf_op jit(solution)/shard_map/ppermute | solution.py:24

commit v2 on v1

v2 whole, which is shorter than its diff:
```python
import functools
import math

import jax
import jax.numpy as jnp
from jax import lax
from jax.experimental import pallas as pl
from jax.experimental.pallas import tpu as pltpu
from jax.sharding import PartitionSpec as P

R3 = math.sqrt(3.0)
H0 = (1.0 + R3) / (4.0 * math.sqrt(2.0))
RHO = (1.0 - R3) / (1.0 + R3)
LOW_TAPS = [H0 * t for t in (1.0, R3, -R3 * RHO, RHO)]
HIGH_TAPS = [LOW_TAPS[3], -LOW_TAPS[2], LOW_TAPS[1], -LOW_TAPS[0]]
KAPPA = -R3 * (1.0 + RHO * RHO)
THRESHOLD = 0.1
LANES = 128


def shifted(x, axis, by):
    count = lax.axis_size(axis)
    return lax.ppermute(x, axis, [(i, (i + by) % count) for i in range(count)])


def time_matrix(length, width, transposed):
    half = length // 2
    row = lax.broadcasted_iota(jnp.int32, (width, width), 1 if transposed else 0)
    col = lax.broadcasted_iota(jnp.int32, (width, width), 0 if transposed else 1)
    is_low = col < half
    offset = lax.rem(row - 2 * jnp.where(is_low, col, col - half) + 2 * length, jnp.int32(length))
    value = jnp.zeros((width, width), jnp.float32)
    for j in range(4):
        tap = jnp.where(is_low, jnp.float32(LOW_TAPS[j] * H0 * H0), jnp.float32(HIGH_TAPS[j] * H0 * H0))
        value = jnp.where(offset == j, tap, value)
    return value if length == width else jnp.where((row < length) & (col < length), value, 0.0)


def split(x):
    high = x.astype(jnp.bfloat16)
    return high, (x - high.astype(jnp.float32)).astype(jnp.bfloat16)


def dot_parts(x, m_ref):
    high, low = split(x)
    dot = functools.partial(jnp.dot, preferred_element_type=jnp.float32)
    return dot(high, m_ref[0]) + (dot(low, m_ref[0]) + dot(high, m_ref[1]))


def ceil8(n):
    return (n + 7) // 8 * 8


class Sizes:
    def __init__(self, x, y, t):
        self.x, self.y, self.t = x, y, t
        self.lx = [x // 2 + 1, x // 4 + 2, x // 8 + 2]
        self.ly = [y // 2 + 1, y // 4 + 2, y // 8 + 2]
        self.py = [ceil8(n) for n in self.ly]
        p1, p2, p3 = self.py
        self.g = [(self.lx[0], 2, p1, LANES), (self.lx[0], 3, 2, p1, LANES), (self.lx[1], 2, 2, p2, LANES),
                  (self.lx[2], 2, 2, p3, LANES)]
        self.zin = [y, p1, p2]
        self.zbase = [6, 5, 6]
        self.zrows = [ceil8(2 * (p - 1) + 4 + b) for p, b in zip(self.py, self.zbase)]
        self.main = [y // 2, y // 4, y // 8]
        self.xp_pieces = [4, 4, 3]
        self.xn_pieces = [4, 6, 3]
        self.xp = self.x_rows(self.xp_pieces)
        self.xn = self.x_rows(self.xn_pieces)
        n1, n2, n3 = self.lx[0] * 4, self.lx[1] * 2, self.lx[2] * 2
        self.yp = ceil8(n1 + 2 * n2 + 3 * n3)
        self.yn = ceil8(n1 + 3 * n2 + 3 * n3)


    def x_rows(self, pieces):
        return ceil8(sum(n * w for n, w in zip(pieces, self.ly)))

    def x_offsets(self, pieces):
        at = 0
        mains, extras = [], []
        for n, m in zip(pieces, self.main):
            mains.append([at + i * m for i in range(n)])
            at += n * m
        for n, m, w in zip(pieces, self.main, self.ly):
            extras.append([at + i * (w - m) for i in range(n)])
            at += n * (w - m)
        return [list(zip(a, b)) for a, b in zip(mains, extras)]


def lattice(v0, v1, v2, v3):
    a = v0 + R3 * v1
    b = v3 - R3 * v2
    return a + RHO * b, RHO * a - b


def lattice_t(low_next, high_next, low_here, high_here):
    a = low_next + RHO * high_next
    b = RHO * low_here - high_here
    return a - R3 * b, R3 * a + b


def x_lattice_static(rows, shape):
    v = [jnp.zeros(shape, jnp.float32) if r is None else r for r in rows]
    return lattice(*v)


class Bands:
    def __init__(self, ga, gb, g2, g3):
        self.ga, self.gb, self.g2, self.g3 = ga, gb, g2, g3

    def at(self, level, s, xb, q):
        if level == 1:
            return self.g2.at[s, xb, q]
        if level == 2:
            return self.g3.at[s, xb, q]
        pair, yb = 2 * xb + q % 2, q // 2
        return self.ga.at[s, yb] if pair == 0 else self.gb.at[s, pair - 1, yb]


def y_analysis(z_ref, base, count, low_ref, high_ref):
    v = [z_ref[pl.ds(base + j, count, stride=2), :] for j in range(4)]
    low, high = lattice(*v)
    low_ref[...] = low
    high_ref[...] = high


def u_rows(u, x, y):
    return pl.ds(pl.multiple_of(x * y, 8), y)


def x_lattice_rows(u, h, s, y):
    return lattice(*[u[h, u_rows(u, 2 * s + j, y), :] for j in range(4)])


def pad_z(z, index, lo, hi, total):
    z[index + (slice(0, lo), slice(None))] = jnp.zeros((lo, LANES), jnp.float32)
    if hi < total:
        z[index + (slice(hi, total), slice(None))] = jnp.zeros((total - hi, LANES), jnp.float32)


def forward_coarse(sz, u, f1, f2, f3, g, zh, mp, mn, a1, z1, a2, z2, a3, z3):
    x, y, t = sz.x, sz.y, sz.t
    l1 = sz.lx[0]

    def rows_x(s, carry):
        for h in range(2):
            a1[h, s] = x_lattice_rows(u, h, s, y)[0]
        return carry

    lax.fori_loop(0, l1, rows_x, 0)

    step = 9
    for s0 in range(0, l1, step):
        n = min(step, l1 - s0)
        out = dot_parts(jnp.concatenate([a1[0, s0 : s0 + n], a1[1, s0 : s0 + n]], axis=-1).reshape(n * y, t), f1)
        out = out.reshape(n, y, t)
        z1[s0 : s0 + n, 8 : 8 + y, :] = out[..., :LANES]
        zh[s0 : s0 + n, 8 : 8 + y, :] = out[..., LANES:]

    def cols_1(s, carry):
        pad_z(z1, (s,), 8, 8 + y, sz.zrows[0])
        y_analysis(z1.at[s], sz.zbase[0], sz.py[0], g.at(0, s, 0, 0), g.at(0, s, 0, 2))
        return carry

    lax.fori_loop(0, l1, cols_1, 0)

    def column(h, j, col):
        return u[h, pl.ds(j * y + col, l1, stride=2 * y), :]

    edges = []
    for c0, c1, w0, w1 in ((0, 1, R3, -1.0), (y - 2, y - 1, 1.0, R3)):
        halves = [lattice(*[w0 * column(h, j, c0) + w1 * column(h, j, c1) for j in range(4)]) for h in range(2)]
        pad = jnp.zeros((ceil8(l1) - l1, t), jnp.float32)
        for xb in range(2):
            edges += [jnp.concatenate([halves[0][xb], halves[1][xb]], axis=-1), pad]
    out = dot_parts(jnp.concatenate(edges, axis=0), f1)
    for m, at in ((mp, 0), (mn, 2)):
        for tb in range(2):
            for xb in range(2):
                row = (at + xb) * ceil8(l1)
                to = (2 * tb + xb) * l1
                m[to : to + l1] = out[row : row + l1, tb * LANES : (tb + 1) * LANES]

    for level, (offset, a, z, f) in enumerate(((3, a2, z2, f2), (2, a3, z3, f3)), 1):
        rows_in, count = sz.lx[level - 1], sz.lx[level]
        p_in, p_out = sz.py[level - 1], sz.py[level]
        for s in range(count):
            picks = [2 * s + j - offset for j in range(4)]
            rows = [g.at(level - 1, i, 0, 0)[...] if 0 <= i < rows_in else None for i in picks]
            low, high = x_lattice_static(rows, (p_in, LANES))
            a[s, 0] = low
            a[s, 1] = high
        out = dot_parts(a[...].reshape(count * 2 * p_in, LANES), f)
        z[:, :, 8 : 8 + p_in, :] = out.reshape(count, 2, p_in, LANES)
        for s in range(count):
            for xb in range(2):
                pad_z(z, (s, xb), 8, 8 + p_in, sz.zrows[level])
                y_analysis(z.at[s, xb], sz.zbase[level], p_out, g.at(level, s, xb, 0), g.at(level, s, xb, 1))
    pack_y(sz, g, mp, mn)


def forward_fine_kernel(sz, u, zh, f1, gb, zl, a1, z1):
    x, y, t = sz.x, sz.y, sz.t
    l1 = sz.lx[0]

    def rows_x(s, carry):
        for h in range(2):
            a1[h, s] = x_lattice_rows(u, h, s, y)[1]
        return carry

    lax.fori_loop(0, l1, rows_x, 0)

    step = 9
    for s0 in range(0, l1, step):
        n = min(step, l1 - s0)
        out = dot_parts(jnp.concatenate([a1[0, s0 : s0 + n], a1[1, s0 : s0 + n]], axis=-1).reshape(n * y, t), f1)
        out = out.reshape(n, y, t)
        z1[s0 : s0 + n, 0, 8 : 8 + y, :] = out[..., :LANES]
        z1[s0 : s0 + n, 1, 8 : 8 + y, :] = out[..., LANES:]

    def cols_1(s, carry):
        zl[8 : 8 + y] = zh[s, 8 : 8 + y, :]
        y_analysis(zl, sz.zbase[0], sz.py[0], gb.at[s, 0, 0], gb.at[s, 0, 1])
        for tb in range(2):
            pad_z(z1, (s, tb), 8, 8 + y, sz.zrows[0])
            y_analysis(z1.at[s, tb], sz.zbase[0], sz.py[0], gb.at[s, 1 + tb, 0], gb.at[s, 1 + tb, 1])
        return carry

    pad_z(zl, (), 8, 8 + y, sz.zrows[0])
    lax.fori_loop(0, l1, cols_1, 0)


def pack_x(sz, g, mp, mn):
    l1, l2, l3 = sz.lx
    lower = lane_below(LANES // 2, (1, LANES))

    def put(ref, pieces, level, items):
        m, w = sz.main[level], sz.ly[level]
        for (main, extra), item in zip(sz.x_offsets(pieces)[level], items):
            for at, lo, hi in ((main, 0, m), (extra, m, w)):
                value = item[0][lo:hi]
                if level == 2:
                    value = jnp.where(lower, value, pltpu.roll(item[1][lo:hi], LANES // 2, 1))
                ref[at : at + hi - lo] = value

    put(mp, sz.xp_pieces, 0, [[g.at(0, 0, 1, q)] for q in range(4)])
    put(mn, sz.xn_pieces, 0, [[g.at(0, l1 - 1, 0, q)] for q in range(4)])
    put(mp, sz.xp_pieces, 1, [[g.at(1, s, 1, q)] for s in (0, 1) for q in (0, 1)])
    put(mn, sz.xn_pieces, 1, [[g.at(1, s, b, q)] for s, b in ((l2 - 2, 0), (l2 - 2, 1), (l2 - 1, 0)) for q in (0, 1)])
    put(mp, sz.xp_pieces, 2, [[g.at(2, s, b, q) for q in (0, 1)] for s, b in ((0, 1), (1, 0), (1, 1))])
    put(mn, sz.xn_pieces, 2, [[g.at(2, s, b, q) for q in (0, 1)] for s, b in ((l3 - 2, 0), (l3 - 2, 1), (l3 - 1, 0))])


def fix_x(sz, g, rn, rp):
    l1, l2, l3 = sz.lx
    lower = lane_below(LANES // 2, (1, LANES))

    def take(ref, pieces, level, lo, hi):
        part = 0 if lo == 0 else 1
        return [ref[at[part] : at[part] + hi - lo] for at in sz.x_offsets(pieces)[level]]

    def halves(value):
        return [jnp.where(lower, v, 0.0) for v in (value, pltpu.roll(value, LANES // 2, 1))]

    for level in range(3):
        m, w = sz.main[level], sz.ly[level]
        for lo, hi in ((0, m), (m, w)):
            n = take(rn, sz.xp_pieces, level, lo, hi)
            p = take(rp, sz.xn_pieces, level, lo, hi)

            def add(s, xb, q, value):
                g.at(level, s, xb, q)[lo:hi] += value

            if level == 0:
                for q in range(4):
                    add(l1 - 1, 0, q, -RHO * n[q])
                    add(l1 - 1, 1, q, n[q])
                    add(0, 0, q, p[q])
                    add(0, 1, q, RHO * p[q])
            elif level == 1:
                for q in range(2):
                    h0, h1 = n[q], n[2 + q]
                    add(l2 - 2, 0, q, -RHO * h0)
                    add(l2 - 2, 1, q, h0)
                    add(l2 - 1, 0, q, KAPPA * h0 - RHO * h1)
                    add(l2 - 1, 1, q, h1)
                    add(0, 0, q, p[q])
                    add(0, 1, q, p[2 + q])
                    add(1, 0, q, p[4 + q])
                    add(1, 1, q, RHO * p[4 + q])
            else:
                n, p = [halves(v) for v in n], [halves(v) for v in p]
                for q in range(2):
                    add(l3 - 2, 0, q, -RHO * n[0][q])
                    add(l3 - 2, 1, q, n[0][q])
                    add(l3 - 1, 0, q, n[1][q])
                    add(l3 - 1, 1, q, n[2][q])
                    add(0, 0, q, p[0][q])
                    add(0, 1, q, p[1][q])
                    add(1, 0, q, p[2][q])
                    add(1, 1, q, RHO * p[2][q])


def pack_y(sz, g, mp, mn):
    k1, k2, k3 = sz.ly
    at_p = at_n = 4 * sz.lx[0]
    for s in range(sz.lx[1]):
        for xb in range(2):
            mp[at_p : at_p + 2] = g.at(1, s, xb, 1)[0:2]
            mn[at_n : at_n + 2] = g.at(1, s, xb, 0)[k2 - 2 : k2]
            mn[at_n + 2 : at_n + 3] = g.at(1, s, xb, 1)[k2 - 2 : k2 - 1]
            at_p += 2
            at_n += 3
    for s in range(sz.lx[2]):
        for xb in range(2):
            mp[at_p : at_p + 2] = g.at(2, s, xb, 1)[0:2]
            mp[at_p + 2 : at_p + 3] = g.at(2, s, xb, 0)[1:2]
            mn[at_n : at_n + 2] = g.at(2, s, xb, 0)[k3 - 2 : k3]
            mn[at_n + 2 : at_n + 3] = g.at(2, s, xb, 1)[k3 - 2 : k3 - 1]
            at_p += 3
            at_n += 3
    if at_p < sz.yp:
        mp[at_p:] = jnp.zeros((sz.yp - at_p, LANES), jnp.float32)
    if at_n < sz.yn:
        mn[at_n:] = jnp.zeros((sz.yn - at_n, LANES), jnp.float32)


def fix_y_fine(sz, g, rn, rp, rows):
    last = sz.ly[0] - 1
    for s in rows:
        for xb in range(2):
            for tb in range(2):
                at = (2 * tb + xb) * sz.lx[0] + s
                high, low = rn[at : at + 1], rp[at : at + 1]
                g.at(0, s, xb, tb)[last : last + 1] += -RHO * high
                g.at(0, s, xb, 2 + tb)[last : last + 1] += high
                g.at(0, s, xb, tb)[0:1] += low
                g.at(0, s, xb, 2 + tb)[0:1] += RHO * low


def fix_y_coarse(sz, g, rn, rp):
    k1, k2, k3 = sz.ly
    at_p = at_n = 4 * sz.lx[0]

    for level in (1, 2):
        k = sz.ly[level]
        for s in range(sz.lx[level]):
            for xb in range(2):

                def add(q, row, value):
                    g.at(level, s, xb, q)[row : row + 1] += value

                h0, h1 = rn[at_n : at_n + 1], rn[at_n + 1 : at_n + 2]
                if level == 1:
                    l1 = KAPPA * h0 - RHO * h1
                    at_n += 2
                else:
                    l1 = rn[at_n + 2 : at_n + 3]
                    at_n += 3
                add(0, k - 2, -RHO * h0)
                add(1, k - 2, h0)
                add(0, k - 1, l1)
                add(1, k - 1, h1)
                w0, w2, w1 = (rp[at_p + i : at_p + i + 1] for i in range(3))
                add(0, 0, w0)
                add(1, 0, w1)
                add(0, 1, w2)
                add(1, 1, RHO * w2)
                at_p += 3


def shrink(v):
    return v - jnp.clip(v, -THRESHOLD, THRESHOLD)


def y_synthesis(low, high, count, t_ref, v_ref, index, start):
    a = low + RHO * high
    b = RHO * low - high
    t_ref[...] = a
    a = t_ref[1 : 1 + count]
    b = b[:count]
    v_ref[index + (pl.ds(start, count, stride=2), slice(None))] = a - R3 * b
    v_ref[index + (pl.ds(start + 1, count, stride=2), slice(None))] = R3 * a + b


def lane_below(limit, shape):
    return lax.broadcasted_iota(jnp.int32, shape, 1) < limit


def level_1_columns(sz, details, s, xb, tb, coarse, ta, v1, index):
    low = coarse if coarse is not None else details(0, s, xb, tb, None)
    high = details(0, s, xb, 2 + tb, None)
    y_synthesis(low, high, sz.y // 2, ta.at[s, xb * 2 + tb, 0 : sz.py[0]], v1, index, 0)


def times_back(sz, v_low, v_high, i1):
    v = jnp.concatenate([v_low, v_high], axis=-1)
    return dot_parts(v.reshape(-1, sz.t), i1).reshape(v.shape)


def inner_inverse(sz, details, i1, va, ba, ta, v1):
    l1 = sz.lx[0]

    def rows(s, carry):
        level_1_columns(sz, details, s, 0, 1, None, ta, va, (s,))
        level_1_columns(sz, details, s, 1, 0, None, ta, v1, (s, 0))
        level_1_columns(sz, details, s, 1, 1, None, ta, v1, (s, 1))
        return carry

    lax.fori_loop(1, l1 - 1, rows, 0)
    step = 8
    for s0 in range(1, l1 - 1, step):
        n = min(step, l1 - 1 - s0)
        ba[s0 : s0 + n] = times_back(sz, v1[s0 : s0 + n, 0], v1[s0 : s0 + n, 1], i1)


def inverse(sz, details, emit, va, ba, i1, i2, i3, ta1, ta, v3, b3, v2, b2, v1, b1, ve):
    y, t = sz.y, sz.t
    p1, p2, p3 = sz.py
    l1, l2, l3 = sz.lx
    third = lane_below(t // 8, (p3, LANES))

    for e, s in enumerate((0, l1 - 1)):
        level_1_columns(sz, details, s, 0, 1, None, ta1, va, (s,))
        level_1_columns(sz, details, s, 1, 0, None, ta1, ve, (e, 0))
        level_1_columns(sz, details, s, 1, 1, None, ta1, ve, (e, 1))

    for s in range(l3):
        for xb in range(2):
            low = details(2, s, xb, 0, third if xb == 0 else None)
            high = details(2, s, xb, 1, None)
            y_synthesis(low, high, sz.ly[1] // 2, ta.at[1, s, xb, 0:p3], v3, (s, xb), 0)
    b3[...] = dot_parts(v3[...].reshape(l3 * 2 * p2, LANES), i3).reshape(l3, 2, p2, LANES)

    second = lane_below(t // 4, (p2, LANES))
    for p in range(l2 // 2):
        even, odd = lattice_t(b3[p + 1, 0], b3[p + 1, 1], b3[p, 0], b3[p, 1])
        for s, coarse in ((2 * p, even), (2 * p + 1, odd)):
            for xb in range(2):
                low = details(1, s, xb, 0, None)
                if xb == 0:
                    low = jnp.where(second, coarse, low)
                high = details(1, s, xb, 1, None)
                y_synthesis(low, high, (sz.ly[0] + 1) // 2, ta.at[0, s, xb, 0:p2], v2, (s, xb), 7)
    b2[...] = dot_parts(v2[:, :, 8 : 8 + p1, :].reshape(l2 * 2 * p1, LANES), i2).reshape(l2, 2, p1, LANES)

    edge = times_back(sz, ve[:, 0], ve[:, 1], i1)
    ba[0] = edge[0]
    ba[l1 - 1] = edge[1]

    def coarse_rows(p):
        return lattice_t(b2[p + 1, 0], b2[p + 1, 1], b2[p, 0], b2[p, 1])

    level_1_columns(sz, details, 0, 0, 0, coarse_rows(0)[1], ta1, v1, (0,))

    def pair_1(p, carry):
        even, odd = coarse_rows(p)
        level_1_columns(sz, details, 2 * p - 1, 0, 0, even, ta1, v1, (2 * p - 1,))
        level_1_columns(sz, details, 2 * p, 0, 0, odd, ta1, v1, (2 * p,))
        return carry

    lax.fori_loop(1, l2 - 1, pair_1, 0)

    step = 9
    for s0 in range(0, l1, step):
        n = min(step, l1 - s0)
        b1[s0 : s0 + n] = times_back(sz, v1[s0 : s0 + n], va[s0 : s0 + n], i1)

    def rows_x(p, carry):
        even, odd = lattice_t(b1[p + 1], ba[p + 1], b1[p], ba[p])
        emit(p, even, odd)
        return carry

    return rows_x


def border(sz, u):
    zeros = jnp.zeros((2 * sz.y, LANES), jnp.float32)
    for h in range(2):
        u[h, 0 : 2 * sz.y, :] = zeros
        u[h, (sz.x + 2) * sz.y :, :] = zeros


def store_u(sz, u, x, value):
    for h in range(2):
        u[h, u_rows(u, x + 2, sz.y), :] = value[:, h * LANES : (h + 1) * LANES]


def first_kernel(sz, c, w_ref, ga, g2, g3, mp, mn, u, zh, f1, f2, f3, i1, i2, i3, *scratch):
    border(sz, u)
    for level, (f, i) in enumerate(((f1, i1), (f2, i2), (f3, i3))):
        for m, transposed in ((f, False), (i, True)):
            m[0], m[1] = split(time_matrix(sz.t >> level, m.shape[1], transposed))

    def rows(x, carry):
        value = c[x].astype(jnp.float32) * (1.0 / 64.0)
        weight = 1.0 / (1.0 + jnp.abs(value))
        w_ref[x] = weight
        store_u(sz, u, x, weight * value)
        return carry

    lax.fori_loop(0, sz.x, rows, 0)
    forward_coarse(sz, u, f1, f2, f3, Bands(ga, None, g2, g3), zh, mp, mn, *scratch)


def edge_kernel(sz, gai, gbi, g2i, g3i, rn, rp, ga, gb, g2, g3, mp, mn):
    g = Bands(ga, gb, g2, g3)
    fix_y_coarse(sz, g, rn, rp)
    fix_y_fine(sz, g, rn, rp, (0, sz.lx[0] - 1))
    pack_x(sz, g, mp, mn)


def first_details(g):
    def details(level, s, xb, q, approx_lanes):
        value = g.at(level, s, xb, q)[...]
        small = shrink(value)
        return small if approx_lanes is None else jnp.where(approx_lanes, value, small)

    return details


def second_details(g, q_bands):
    def details(level, s, xb, q, approx_lanes):
        first = g.at(level, s, xb, q)[...]
        second = q_bands.at(level, s, xb, q)[...]
        small = shrink(shrink(first) + (first - second))
        if approx_lanes is None:
            return small
        return jnp.where(approx_lanes, first + (first - second), small)

    return details


def inner_first_kernel(sz, gai, gbi, rn, rp, i1, ga, gb, va, ba, ta, v1):
    g = Bands(ga, gb, None, None)
    fix_y_fine(sz, g, rn, rp, range(1, sz.lx[0] - 1))
    inner_inverse(sz, first_details(g), i1, va, ba, ta, v1)


def inner_last_kernel(sz, qai, qbi, rn, rp, i1, ga, gb, qa, qb, va, ba, ta, v1):
    q = Bands(qa, qb, None, None)
    fix_y_fine(sz, q, rn, rp, range(1, sz.lx[0] - 1))
    inner_inverse(sz, second_details(Bands(ga, gb, None, None), q), i1, va, ba, ta, v1)


def middle_kernel(sz, gai, gbi, g2i, g3i, vai, bai, rn, rp, w_ref, f1, f2, f3, i1, i2, i3,
                  ga, gb, g2, g3, va, ba, qa, q2, q3, mp, mn, u, zh, ta1, ta, v3, b3, v2, b2, v1, b1, ve, *scratch):
    g = Bands(ga, gb, g2, g3)
    fix_x(sz, g, rn, rp)
    border(sz, u)

    def emit(p, even, odd):
        store_u(sz, u, 2 * p, w_ref[2 * p] * even)
        store_u(sz, u, 2 * p + 1, w_ref[2 * p + 1] * odd)

    rows = inverse(sz, first_details(g), emit, va, ba, i1, i2, i3, ta1, ta, v3, b3, v2, b2, v1, b1, ve)
    lax.fori_loop(0, sz.x // 2, rows, 0)
    forward_coarse(sz, u, f1, f2, f3, Bands(qa, None, q2, q3), zh, mp, mn, *scratch)


def last_kernel(sz, qai, qbi, q2i, q3i, vai, bai, rn, rp, ga, gb, g2, g3, i1, i2, i3,
                qa, qb, q2, q3, va, ba, out_hbm, out, sems, ta1, ta, v3, b3, v2, b2, v1, b1, ve):
    q = Bands(qa, qb, q2, q3)
    fix_x(sz, q, rn, rp)

    def emit(p, even, odd):
        out[2 * p] = even
        out[2 * p + 1] = odd

    details = second_details(Bands(ga, gb, g2, g3), q)
    rows = inverse(sz, details, emit, va, ba, i1, i2, i3, ta1, ta, v3, b3, v2, b2, v1, b1, ve)
    step = 8
    copies = []
    for i, x0 in enumerate(range(0, sz.x, step)):
        lax.fori_loop(x0 // 2, (x0 + step) // 2, rows, 0)
        copies.append(pltpu.make_async_copy(out.at[x0 : x0 + step], out_hbm.at[x0 : x0 + step], sems.at[i]))
        copies[-1].start()
    for copy in copies:
        copy.wait()


VMEM = pltpu.MemorySpace.VMEM
HBM = pltpu.MemorySpace.HBM


def call(kernel, sz, outs, scratch, aliases, *args, outs_hbm=(), flops=0):
    def specs(n, in_hbm):
        return [pl.BlockSpec(memory_space=HBM if k in in_hbm else VMEM) for k in range(n)]

    outs = [s if isinstance(s, jax.ShapeDtypeStruct) else jax.ShapeDtypeStruct(s, jnp.float32) for s in outs]
    return pl.pallas_call(
        functools.partial(kernel, sz),
        out_shape=outs,
        in_specs=specs(len(args), ()),
        out_specs=specs(len(outs), outs_hbm),
        scratch_shapes=scratch,
        input_output_aliases=aliases,
        cost_estimate=pl.CostEstimate(flops=flops, bytes_accessed=flops // 100, transcendentals=0) if flops else None,
        compiler_params=pltpu.CompilerParams(vmem_limit_bytes=36 * 2**20),
    )(*args)


def on_device(counts):
    sz = Sizes(*counts.shape)
    x, y, t = counts.shape
    l1, l2, l3 = sz.lx
    p1, p2, p3 = sz.py

    def f32(*shapes):
        return [pltpu.VMEM(s, jnp.float32) for s in shapes]

    parts = [jax.ShapeDtypeStruct((2, n, n), jnp.bfloat16) for n in (t, LANES, LANES)]
    u, zh = (2, (x + 4) * y, LANES), (l1, sz.zrows[0], LANES)
    sems = [pltpu.SemaphoreType.DMA((x // 8,))]
    fw = f32((2, l1, y, LANES), (l1, sz.zrows[0], LANES), (l2, 2, p1, LANES), (l2, 2, sz.zrows[1], LANES),
             (l3, 2, p2, LANES), (l3, 2, sz.zrows[2], LANES))
    fine = f32((sz.zrows[0], LANES), (2, l1, y, LANES), (l1, 2, sz.zrows[0], LANES))
    ta1 = f32((l1, 4, p1 + 8, LANES))
    bw = ta1 + f32((2, l2, 2, p2 + 8, LANES), (l3, 2, p2, LANES), (l3, 2, p2, LANES), (l2, 2, p1 + 8, LANES),
                   (l2, 2, p1, LANES), (l1, y, LANES), (l1, y, t), (2, 2, y, LANES))
    to_prev, to_next = (sz.xp, LANES), (sz.xn, LANES)
    messages = [(sz.yp, LANES), (sz.yn, LANES)]
    halves = [(l1, y, LANES), (l1, y, t)]
    inner = ta1 + f32((l1, 2, y, LANES))
    work = 6 * l1 * y * t * t
    ga, gb, g2, g3 = sz.g

    def exchange(ga, g2, g3, mp, mn, u, zh, f1):
        rn, rp = shifted(mp, "gy", -1), shifted(mn, "gy", 1)
        (gb,) = call(forward_fine_kernel, sz, [sz.g[1]], fine, {}, u, zh, f1, flops=work)
        *g, mp, mn = call(edge_kernel, sz, sz.g + [to_prev, to_next], [], {k: k for k in range(4)},
                          ga, gb, g2, g3, rn, rp)
        return g, (rn, rp), shifted(mp, "gx", -1), shifted(mn, "gx", 1)

    weight, *rest = call(first_kernel, sz, [(x, y, t), ga, g2, g3] + messages + [u, zh] + parts + parts,
                         fw, {}, counts)
    g_a, g_2, g_3, mp, mn, *rest = rest
    f, i = rest[2:5], rest[5:8]
    g, ry, rn, rp = exchange(g_a, g_2, g_3, mp, mn, *rest[:3])
    *kept, va, ba = call(inner_first_kernel, sz, [ga, gb] + halves, inner, {0: 0, 1: 1}, g[0], g[1], *ry, i[0], flops=work)
    same = {k: k for k in range(6)}
    *rest, q_a, q_2, q_3, mp, mn, u_, zh_ = call(
        middle_kernel, sz, sz.g + halves + [ga, g2, g3] + messages + [u, zh], bw + fw, same,
        *kept, g[2], g[3], va, ba, rn, rp, weight, *f, *i)
    g = rest[:4]
    q, ry, rn, rp = exchange(q_a, q_2, q_3, mp, mn, u_, zh_, f[0])
    *kept, va, ba = call(inner_last_kernel, sz, [ga, gb] + halves, inner, {0: 0, 1: 1}, q[0], q[1], *ry, i[0], g[0], g[1],
                         flops=work)
    return call(last_kernel, sz, sz.g + halves + [(x, y, t)], f32((x, y, t)) + sems + bw, same,
                *kept, q[2], q[3], va, ba, rn, rp, *g, *i, outs_hbm=(6,))[6]


def solution(mesh):
    spec = P(("grp", "gx"), "gy", None)
    return jax.shard_map(on_device, mesh=mesh, in_specs=(spec,), out_specs=spec, check_vma=False)
```

time: 46.1 us -> 42.6 us (0.924)
  waiting for transfers between devices: 15 us -> 11.8 us
  local copies, waits for them, and re-layouts: 2.59 us -> 1.59 us
  Pallas kernels: 16.1 us -> 16.8 us
    ppermute x8, waiting for transfers between devices: 15 us -> 11.8 us  [shifted(): return lax.ppermute(x, axis, [(i, (i + by) % count) for i in range(count)])]
    unnamed x6 -> x2, local copies, waits for them, and re-layouts: 2.59 us -> 1.59 us
    pallas_call x7 -> x9, Pallas kernels: 16.1 us -> 16.8 us  [call(): pl.pallas_call(functools.partial(kernel, sz), out_shape=outs, in_specs=sp...]
  transfers between devices with their start and end apart: 8 -> 8, of which waited for: 5 -> 5; matrix products, arithmetic and copies ran while one was open for 0% -> 0% of each run, Pallas kernels for 5% -> 13%
where the time goes in v2:
time: 42.6 us; the launch traced here: 42.4 us
  Pallas kernels  16.8 us (39%)
  starting transfers between devices  12.2 us (29%)
  waiting for transfers between devices  11.8 us (28%)
  local copies, waits for them, and re-layouts  1.59 us (4%)
    pallas_call x9, Pallas kernels, call(): pl.pallas_call(functools.partial(kernel, sz), out_shape=outs, in_specs=sp...  16.8 us
    ppermute x8, starting transfers between devices, shifted(): return lax.ppermute(x, axis, [(i, (i + by) % count) for i in range(count)])  12.2 us
    ppermute x8, waiting for transfers between devices, shifted(): return lax.ppermute(x, axis, [(i, (i + by) % count) for i in range(count)])  11.8 us
    unnamed x2, local copies, waits for them, and re-layouts  1.59 us
  transfers between devices with their start and end apart: 8, of which 5 were waited for; matrix products, arithmetic and copies ran while one was open for 0% of the time, Pallas kernels for 13%

profile of v2, /device:TPU:0, one launch (start us, length us, event | category | flops | bytes accessed | tf_op | source)
XLA Modules:
  0.0 42.4 jit_solution(13212923963907086782)
XLA Ops:
  0.0 0.0 copy-start
  0.0 1.6 %copy-done = s32[32,64,256]{2,1,0:T(8,128)S(1)} copy-done((s32[32,64,256]{2,1,0:T(8,128)S(1)}, s32[32,64,256]{2,1,0:T(8,128)}, u32[]{:S(2)}) %copy-start) | copy-done | bytes 2097176
  1.6 3.2 %shard_map.17 = (f32[32,64,256]{2,1,0:T(8,128)S(1)}, f32[17,2,40,128]{3,2,1,0:T(8,128)S(1)}, f32[10,2,2,24,128]{4,3,2,1,0:T(8,128)S(1)}, f32[6,2,2,16,128]{4,3,2...) custom-call(s32[32,64,256]{2,1,0:T(8,128)S(1)} %copy-done), custom_call_target="tpu_custom_call" | custom-call | tf_op jit(solution)/shard_map/pallas_call | solution.py:592
  4.8 0.5 %collective-permute-start.1 = (f32[168,128]{1,0:T(8,128)S(1)}, f32[168,128]{1,0:T(8,128)S(1)}, u32[]{:S(2)}, u32[]{:S(2)}) collective-permute-start(f32[168,128]{1,0:T(8,128)S(1)} %get-tuple-element.58), channel_id=1, source_target_pairs={{0,1},{1,2},{2,3},{3,0},{4,5},{5,6},{6,7},{7,4},{8,9},{9,10},{10,1... | collective-permute-start | bytes 258056 | tf_op jit(solution)/shard_map/ppermute | solution.py:23
  5.3 2.0 %collective-permute-start = (f32[144,128]{1,0:T(8,128)S(1)}, f32[144,128]{1,0:T(8,128)S(1)}, u32[]{:S(2)}, u32[]{:S(2)}) collective-permute-start(f32[144,128]{1,0:T(8,128)S(1)} %get-tuple-element.57), channel_id=1, source_target_pairs={{0,3},{1,0},{2,1},{3,2},{4,7},{5,4},{6,5},{7,6},{8,11},{9,8},{10,9... | collective-permute-start | bytes 221192 | tf_op jit(solution)/shard_map/ppermute | solution.py:23
  7.3 1.5 %shard_map.18.gbi = f32[17,3,2,40,128]{4,3,2,1,0:T(8,128)S(1)} custom-call(f32[2,2304,128]{2,1,0:T(8,128)S(1)} %get-tuple-element.52.u, f32[17,88,128]{2,1,0:T(8,128)S(1)} %get-tuple-element.53.zh, bf16[2,256,256]{2,1,0:T(8,128)(2,1)S(1)} %get-tuple-element.54.f1), custom_call_target="tpu_custom_call" | custom-call | flops 427819008 | bytes 4278190 | tf_op jit(solution)/shard_map/pallas_call | solution.py:592
  8.8 1.1 %collective-permute-done.rn = f32[144,128]{1,0:T(8,128)S(1)} collective-permute-done((f32[144,128]{1,0:T(8,128)S(1)}, f32[144,128]{1,0:T(8,128)S(1)}, u32[]{:S(2)}, u32[]{:S(2)}) %collective-permute-start) | collective-permute-done | bytes 73760 | tf_op jit(solution)/shard_map/ppermute | solution.py:23
  10.0 0.0 collective-permute-done.1.rp
  10.0 0.2 shard_map.19
  10.2 1.9 %collective-permute-start.3 = (f32[272,128]{1,0:T(8,128)S(1)}, f32[272,128]{1,0:T(8,128)S(1)}, u32[]{:S(2)}, u32[]{:S(2)}) collective-permute-start(f32[272,128]{1,0:T(8,128)S(1)} %get-tuple-element.69), channel_id=1, source_target_pairs={{0,4},{4,8},{8,12},{12,0},{1,5},{5,9},{9,13},{13,1},{2,6},{6,10},{... | collective-permute-start | bytes 417800 | tf_op jit(solution)/shard_map/ppermute | solution.py:23
  12.1 2.1 %collective-permute-start.2 = (f32[240,128]{1,0:T(8,128)S(1)}, f32[240,128]{1,0:T(8,128)S(1)}, u32[]{:S(2)}, u32[]{:S(2)}) collective-permute-start(f32[240,128]{1,0:T(8,128)S(1)} %get-tuple-element.68), channel_id=1, source_target_pairs={{0,12},{4,0},{8,4},{12,8},{1,13},{5,1},{9,5},{13,9},{2,14},{6,2},{... | collective-permute-start | bytes 368648 | tf_op jit(solution)/shard_map/ppermute | solution.py:23
  14.1 1.2 %shard_map.20 = (f32[17,2,40,128]{3,2,1,0:T(8,128)S(1)}, f32[17,3,2,40,128]{4,3,2,1,0:T(8,128)S(1)}, f32[17,64,128]{2,1,0:T(8,128)S(1)}, f32[17,64,256]{2,1,0:T(8,128)S(1)}) custom-call(f32[17,2,40,128]{3,2,1,0:T(8,128)S(1)} %get-tuple-element.59.gai, ...), custom_call_target="tpu_custom_call", output_to_operand_aliasing={{0}: (0, {}), {1}: (1, {})} | custom-call | flops 427819008 | bytes 4278190 | tf_op jit(solution)/shard_map/pallas_call | solution.py:592
  15.4 5.8 %collective-permute-done.2.rn = f32[240,128]{1,0:T(8,128)S(1)} collective-permute-done((f32[240,128]{1,0:T(8,128)S(1)}, f32[240,128]{1,0:T(8,128)S(1)}, u32[]{:S(2)}, u32[]{:S(2)}) %collective-permute-start.2) | collective-permute-done | bytes 122912 | tf_op jit(solution)/shard_map/ppermute | solution.py:23
  21.2 0.0 collective-permute-done.3.rp
  21.2 4.2 %shard_map.21 = (f32[17,2,40,128]{3,2,1,0:T(8,128)S(1)}, f32[17,3,2,40,128]{4,3,2,1,0:T(8,128)S(1)}, f32[10,2,2,24,128]{4,3,2,1,0:T(8,128)S(1)}, f32[6,2,2,16,12...) custom-call(f32[17,2,40,128]{3,2,1,0:T(8,128)S(1)} %get-tuple-elemen, ...), custom_call_target="tpu_custom_call", output_to_operand_aliasing={{0}: (0, {}), {1}: (1, {}), {2}: (2, {}), {3}: (3, {}), {4}... | custom-call | tf_op jit(solution)/shard_map/pallas_call | solution.py:592
  25.5 0.2 collective-permute-start.5
  25.6 1.6 %collective-permute-start.4 = (f32[144,128]{1,0:T(8,128)S(1)}, f32[144,128]{1,0:T(8,128)S(1)}, u32[]{:S(2)}, u32[]{:S(2)}) collective-permute-start(f32[144,128]{1,0:T(8,128)S(1)} %get-tuple-element.80), channel_id=1, source_target_pairs={{0,3},{1,0},{2,1},{3,2},{4,7},{5,4},{6,5},{7,6},{8,11},{9,8},{10,9... | collective-permute-start | bytes 221192 | tf_op jit(solution)/shard_map/ppermute | solution.py:23
  27.3 1.5 %shard_map.22.gbi = f32[17,3,2,40,128]{4,3,2,1,0:T(8,128)S(1)} custom-call(f32[2,2304,128]{2,1,0:T(8,128)S(1)} %get-tuple-element.76.u, f32[17,88,128]{2,1,0:T(8,128)S(1)} %get-tuple-element.77.zh, bf16[2,256,256]{2,1,0:T(8,128)(2,1)S(1)} %get-tuple-element.54.f1), custom_call_target="tpu_custom_call" | custom-call | flops 427819008 | bytes 4278190 | tf_op jit(solution)/shard_map/pallas_call | solution.py:592
  28.8 0.5 %collective-permute-done.4.rn = f32[144,128]{1,0:T(8,128)S(1)} collective-permute-done((f32[144,128]{1,0:T(8,128)S(1)}, f32[144,128]{1,0:T(8,128)S(1)}, u32[]{:S(2)}, u32[]{:S(2)}) %collective-permute-start.4) | collective-permute-done | bytes 73760 | tf_op jit(solution)/shard_map/ppermute | solution.py:23
  29.3 0.2 collective-permute-done.5.rp
  29.4 0.2 shard_map.23
  29.6 0.6 %collective-permute-start.7 = (f32[272,128]{1,0:T(8,128)S(1)}, f32[272,128]{1,0:T(8,128)S(1)}, u32[]{:S(2)}, u32[]{:S(2)}) collective-permute-start(f32[272,128]{1,0:T(8,128)S(1)} %get-tuple-element.93), channel_id=1, source_target_pairs={{0,4},{4,8},{8,12},{12,0},{1,5},{5,9},{9,13},{13,1},{2,6},{6,10},{... | collective-permute-start | bytes 417800 | tf_op jit(solution)/shard_map/ppermute | solution.py:23
  30.2 3.3 %collective-permute-start.6 = (f32[240,128]{1,0:T(8,128)S(1)}, f32[240,128]{1,0:T(8,128)S(1)}, u32[]{:S(2)}, u32[]{:S(2)}) collective-permute-start(f32[240,128]{1,0:T(8,128)S(1)} %get-tuple-element.92), channel_id=1, source_target_pairs={{0,12},{4,0},{8,4},{12,8},{1,13},{5,1},{9,5},{13,9},{2,14},{6,2},{... | collective-permute-start | bytes 368648 | tf_op jit(solution)/shard_map/ppermute | solution.py:23
  33.5 1.4 %shard_map.24 = (f32[17,2,40,128]{3,2,1,0:T(8,128)S(1)}, f32[17,3,2,40,128]{4,3,2,1,0:T(8,128)S(1)}, f32[17,64,128]{2,1,0:T(8,128)S(1)}, f32[17,64,256]{2,1,0:T(8,128)S(1)}) custom-call(f32[17,2,40,128]{3,2,1,0:T(8,128)S(1)} %get-tuple-element.82.qai, ...), custom_call_target="tpu_custom_call", output_to_operand_aliasing={{0}: (0, {}), {1}: (1, {})} | custom-call | flops 427819008 | bytes 4278190 | tf_op jit(solution)/shard_map/pallas_call | solution.py:592
  34.9 4.2 %collective-permute-done.6.rn = f32[240,128]{1,0:T(8,128)S(1)} collective-permute-done((f32[240,128]{1,0:T(8,128)S(1)}, f32[240,128]{1,0:T(8,128)S(1)}, u32[]{:S(2)}, u32[]{:S(2)}) %collective-permute-start.6) | collective-permute-done | bytes 122912 | tf_op jit(solution)/shard_map/ppermute | solution.py:23
  39.1 0.0 collective-permute-done.7.rp
  39.1 3.3 %shard_map.25 = (f32[17,2,40,128]{3,2,1,0:T(8,128)S(1)}, f32[17,3,2,40,128]{4,3,2,1,0:T(8,128)S(1)}, f32[10,2,2,24,128]{4,3,2,1,0:T(8,128)S(1)}, f32[6,2,2,16,12...) custom-call(f32[17,2,40,128]{3,2,1,0:T(8,128)S(1)} %get-tuple-elemen, ...), custom_call_target="tpu_custom_call", output_to_operand_aliasing={{0}: (0, {}), {1}: (1, {}), {2}: (2, {}), {3}: (3, {}), {4}... | custom-call | tf_op jit(solution)/shard_map/pallas_call | solution.py:592
Async XLA Ops:
  0.0 1.6 %copy-start = (s32[32,64,256]{2,1,0:T(8,128)S(1)}, s32[32,64,256]{2,1,0:T(8,128)}, u32[]{:S(2)}) copy-start(s32[32,64,256]{2,1,0:T(8,128)} %c.1) | copy-start | bytes 6291460
  4.8 5.2 %collective-permute-start.1 = (f32[168,128]{1,0:T(8,128)S(1)}, f32[168,128]{1,0:T(8,128)S(1)}, u32[]{:S(2)}, u32[]{:S(2)}) collective-permute-start(f32[168,128]{1,0:T(8,128)S(1)} %get-tuple-element.58), channel_id=1, source_target_pairs={{0,1},{1,2},{2,3},{3,0},{4,5},{5,6},{6,7},{7,4},{8,9},{9,10},{10,1... | collective-permute-start | bytes 258056 | tf_op jit(solution)/shard_map/ppermute | solution.py:23
  5.3 4.6 %collective-permute-start = (f32[144,128]{1,0:T(8,128)S(1)}, f32[144,128]{1,0:T(8,128)S(1)}, u32[]{:S(2)}, u32[]{:S(2)}) collective-permute-start(f32[144,128]{1,0:T(8,128)S(1)} %get-tuple-element.57), channel_id=1, source_target_pairs={{0,3},{1,0},{2,1},{3,2},{4,7},{5,4},{6,5},{7,6},{8,11},{9,8},{10,9... | collective-permute-start | bytes 221192 | tf_op jit(solution)/shard_map/ppermute | solution.py:23
  10.2 11.1 %collective-permute-start.3 = (f32[272,128]{1,0:T(8,128)S(1)}, f32[272,128]{1,0:T(8,128)S(1)}, u32[]{:S(2)}, u32[]{:S(2)}) collective-permute-start(f32[272,128]{1,0:T(8,128)S(1)} %get-tuple-element.69), channel_id=1, source_target_pairs={{0,4},{4,8},{8,12},{12,0},{1,5},{5,9},{9,13},{13,1},{2,6},{6,10},{... | collective-permute-start | bytes 417800 | tf_op jit(solution)/shard_map/ppermute | solution.py:23
  12.1 9.2 %collective-permute-start.2 = (f32[240,128]{1,0:T(8,128)S(1)}, f32[240,128]{1,0:T(8,128)S(1)}, u32[]{:S(2)}, u32[]{:S(2)}) collective-permute-start(f32[240,128]{1,0:T(8,128)S(1)} %get-tuple-element.68), channel_id=1, source_target_pairs={{0,12},{4,0},{8,4},{12,8},{1,13},{5,1},{9,5},{13,9},{2,14},{6,2},{... | collective-permute-start | bytes 368648 | tf_op jit(solution)/shard_map/ppermute | solution.py:23
  25.5 4.0 %collective-permute-start.5 = (f32[168,128]{1,0:T(8,128)S(1)}, f32[168,128]{1,0:T(8,128)S(1)}, u32[]{:S(2)}, u32[]{:S(2)}) collective-permute-start(f32[168,128]{1,0:T(8,128)S(1)} %get-tuple-element.81), channel_id=1, source_target_pairs={{0,1},{1,2},{2,3},{3,0},{4,5},{5,6},{6,7},{7,4},{8,9},{9,10},{10,1... | collective-permute-start | bytes 258056 | tf_op jit(solution)/shard_map/ppermute | solution.py:23
  25.6 3.6 %collective-permute-start.4 = (f32[144,128]{1,0:T(8,128)S(1)}, f32[144,128]{1,0:T(8,128)S(1)}, u32[]{:S(2)}, u32[]{:S(2)}) collective-permute-start(f32[144,128]{1,0:T(8,128)S(1)} %get-tuple-element.80), channel_id=1, source_target_pairs={{0,3},{1,0},{2,1},{3,2},{4,7},{5,4},{6,5},{7,6},{8,11},{9,8},{10,9... | collective-permute-start | bytes 221192 | tf_op jit(solution)/shard_map/ppermute | solution.py:23
  29.6 9.5 %collective-permute-start.7 = (f32[272,128]{1,0:T(8,128)S(1)}, f32[272,128]{1,0:T(8,128)S(1)}, u32[]{:S(2)}, u32[]{:S(2)}) collective-permute-start(f32[272,128]{1,0:T(8,128)S(1)} %get-tuple-element.93), channel_id=1, source_target_pairs={{0,4},{4,8},{8,12},{12,0},{1,5},{5,9},{9,13},{13,1},{2,6},{6,10},{... | collective-permute-start | bytes 417800 | tf_op jit(solution)/shard_map/ppermute | solution.py:23
  30.2 8.8 %collective-permute-start.6 = (f32[240,128]{1,0:T(8,128)S(1)}, f32[240,128]{1,0:T(8,128)S(1)}, u32[]{:S(2)}, u32[]{:S(2)}) collective-permute-start(f32[240,128]{1,0:T(8,128)S(1)} %get-tuple-element.92), channel_id=1, source_target_pairs={{0,12},{4,0},{8,4},{12,8},{1,13},{5,1},{9,5},{13,9},{2,14},{6,2},{... | collective-permute-start | bytes 368648 | tf_op jit(solution)/shard_map/ppermute | solution.py:23

commit v3 on v2

--- a/solution.py
+++ b/solution.py
@@ -43,8 +43,12 @@
 
 def dot_parts(x, m_ref):
     high, low = split(x)
-    dot = functools.partial(jnp.dot, preferred_element_type=jnp.float32)
-    return dot(high, m_ref[0]) + (dot(low, m_ref[0]) + dot(high, m_ref[1]))
+    return jnp.dot(jnp.concatenate([high, low, high], axis=-1), m_ref[...], preferred_element_type=jnp.float32)
+
+
+def each(first, end, body):
+    for i in range(first, end):
+        body(i)
 
 
 def ceil8(n):
@@ -126,7 +130,7 @@
 
 
 def u_rows(u, x, y):
-    return pl.ds(pl.multiple_of(x * y, 8), y)
+    return pl.ds(x * y, y)
 
 
 def x_lattice_rows(u, h, s, y):
@@ -143,12 +147,11 @@
     x, y, t = sz.x, sz.y, sz.t
     l1 = sz.lx[0]
 
-    def rows_x(s, carry):
+    def rows_x(s):
         for h in range(2):
             a1[h, s] = x_lattice_rows(u, h, s, y)[0]
-        return carry
-
-    lax.fori_loop(0, l1, rows_x, 0)
+
+    each(0, l1, rows_x)
 
     step = 9
     for s0 in range(0, l1, step):
@@ -158,12 +161,11 @@
         z1[s0 : s0 + n, 8 : 8 + y, :] = out[..., :LANES]
         zh[s0 : s0 + n, 8 : 8 + y, :] = out[..., LANES:]
 
-    def cols_1(s, carry):
+    def cols_1(s):
         pad_z(z1, (s,), 8, 8 + y, sz.zrows[0])
         y_analysis(z1.at[s], sz.zbase[0], sz.py[0], g.at(0, s, 0, 0), g.at(0, s, 0, 2))
-        return carry
-
-    lax.fori_loop(0, l1, cols_1, 0)
+
+    each(0, l1, cols_1)
 
     def column(h, j, col):
         return u[h, pl.ds(j * y + col, l1, stride=2 * y), :]
@@ -204,12 +206,11 @@
     x, y, t = sz.x, sz.y, sz.t
     l1 = sz.lx[0]
 
-    def rows_x(s, carry):
+    def rows_x(s):
         for h in range(2):
             a1[h, s] = x_lattice_rows(u, h, s, y)[1]
-        return carry
-
-    lax.fori_loop(0, l1, rows_x, 0)
+
+    each(0, l1, rows_x)
 
     step = 9
     for s0 in range(0, l1, step):
@@ -219,16 +220,15 @@
         z1[s0 : s0 + n, 0, 8 : 8 + y, :] = out[..., :LANES]
         z1[s0 : s0 + n, 1, 8 : 8 + y, :] = out[..., LANES:]
 
-    def cols_1(s, carry):
+    def cols_1(s):
         zl[8 : 8 + y] = zh[s, 8 : 8 + y, :]
         y_analysis(zl, sz.zbase[0], sz.py[0], gb.at[s, 0, 0], gb.at[s, 0, 1])
         for tb in range(2):
             pad_z(z1, (s, tb), 8, 8 + y, sz.zrows[0])
             y_analysis(z1.at[s, tb], sz.zbase[0], sz.py[0], gb.at[s, 1 + tb, 0], gb.at[s, 1 + tb, 1])
-        return carry
 
     pad_z(zl, (), 8, 8 + y, sz.zrows[0])
-    lax.fori_loop(0, l1, cols_1, 0)
+    each(0, l1, cols_1)
 
 
 def pack_x(sz, g, mp, mn):
@@ -402,20 +402,19 @@
 def inner_inverse(sz, details, i1, va, ba, ta, v1):
     l1 = sz.lx[0]
 
-    def rows(s, carry):
+    def rows(s):
         level_1_columns(sz, details, s, 0, 1, None, ta, va, (s,))
         level_1_columns(sz, details, s, 1, 0, None, ta, v1, (s, 0))
         level_1_columns(sz, details, s, 1, 1, None, ta, v1, (s, 1))
-        return carry
-
-    lax.fori_loop(1, l1 - 1, rows, 0)
-    step = 8
+
+    each(1, l1 - 1, rows)
+    step = 15
     for s0 in range(1, l1 - 1, step):
         n = min(step, l1 - 1 - s0)
         ba[s0 : s0 + n] = times_back(sz, v1[s0 : s0 + n, 0], v1[s0 : s0 + n, 1], i1)
 
 
-def inverse(sz, details, emit, va, ba, i1, i2, i3, ta1, ta, v3, b3, v2, b2, v1, b1, ve):
+def inverse(sz, details, emit, done, groups, va, ba, i1, i2, i3, ta1, ta, v3, b3, v2, b2, v1, b1, ve):
     y, t = sz.y, sz.t
     p1, p2, p3 = sz.py
     l1, l2, l3 = sz.lx
@@ -452,27 +451,23 @@
     def coarse_rows(p):
         return lattice_t(b2[p + 1, 0], b2[p + 1, 1], b2[p, 0], b2[p, 1])
 
-    level_1_columns(sz, details, 0, 0, 0, coarse_rows(0)[1], ta1, v1, (0,))
-
-    def pair_1(p, carry):
+    def pair_1(p):
         even, odd = coarse_rows(p)
         level_1_columns(sz, details, 2 * p - 1, 0, 0, even, ta1, v1, (2 * p - 1,))
         level_1_columns(sz, details, 2 * p, 0, 0, odd, ta1, v1, (2 * p,))
-        return carry
-
-    lax.fori_loop(1, l2 - 1, pair_1, 0)
-
-    step = 9
-    for s0 in range(0, l1, step):
-        n = min(step, l1 - s0)
-        b1[s0 : s0 + n] = times_back(sz, v1[s0 : s0 + n], va[s0 : s0 + n], i1)
-
-    def rows_x(p, carry):
+
+    def rows_x(p):
         even, odd = lattice_t(b1[p + 1], ba[p + 1], b1[p], ba[p])
         emit(p, even, odd)
-        return carry
-
-    return rows_x
+
+    level_1_columns(sz, details, 0, 0, 0, coarse_rows(0)[1], ta1, v1, (0,))
+    step = sz.x // groups
+    for x0 in range(0, sz.x, step):
+        each(x0 // 4 + 1, (x0 + step) // 4 + 1, pair_1)
+        s0, s1 = (x0 // 2 + 1 if x0 else 0), (x0 + step) // 2 + 1
+        b1[s0:s1] = times_back(sz, v1[s0:s1], va[s0:s1], i1)
+        each(x0 // 2, (x0 + step) // 2, rows_x)
+        done(x0, step)
 
 
 def border(sz, u):
@@ -487,20 +482,26 @@
         u[h, u_rows(u, x + 2, sz.y), :] = value[:, h * LANES : (h + 1) * LANES]
 
 
-def first_kernel(sz, c, w_ref, ga, g2, g3, mp, mn, u, zh, f1, f2, f3, i1, i2, i3, *scratch):
-    border(sz, u)
+def matrix_kernel(sz, f1, f2, f3, i1, i2, i3):
     for level, (f, i) in enumerate(((f1, i1), (f2, i2), (f3, i3))):
         for m, transposed in ((f, False), (i, True)):
-            m[0], m[1] = split(time_matrix(sz.t >> level, m.shape[1], transposed))
-
-    def rows(x, carry):
+            n = m.shape[1]
+            high, low = split(time_matrix(sz.t >> level, n, transposed))
+            m[0:n] = high
+            m[n : 2 * n] = high
+            m[2 * n :] = low
+
+
+def first_kernel(sz, c, f1, f2, f3, w_ref, ga, g2, g3, mp, mn, u, zh, *scratch):
+    border(sz, u)
+
+    def rows(x):
         value = c[x].astype(jnp.float32) * (1.0 / 64.0)
         weight = 1.0 / (1.0 + jnp.abs(value))
         w_ref[x] = weight
         store_u(sz, u, x, weight * value)
-        return carry
-
-    lax.fori_loop(0, sz.x, rows, 0)
+
+    each(0, sz.x, rows)
     forward_coarse(sz, u, f1, f2, f3, Bands(ga, None, g2, g3), zh, mp, mn, *scratch)
 
 
@@ -554,8 +555,7 @@
         store_u(sz, u, 2 * p, w_ref[2 * p] * even)
         store_u(sz, u, 2 * p + 1, w_ref[2 * p + 1] * odd)
 
-    rows = inverse(sz, first_details(g), emit, va, ba, i1, i2, i3, ta1, ta, v3, b3, v2, b2, v1, b1, ve)
-    lax.fori_loop(0, sz.x // 2, rows, 0)
+    inverse(sz, first_details(g), emit, lambda x0, n: None, 2, va, ba, i1, i2, i3, ta1, ta, v3, b3, v2, b2, v1, b1, ve)
     forward_coarse(sz, u, f1, f2, f3, Bands(qa, None, q2, q3), zh, mp, mn, *scratch)
 
 
@@ -569,13 +569,13 @@
         out[2 * p + 1] = odd
 
     details = second_details(Bands(ga, gb, g2, g3), q)
-    rows = inverse(sz, details, emit, va, ba, i1, i2, i3, ta1, ta, v3, b3, v2, b2, v1, b1, ve)
-    step = 8
     copies = []
-    for i, x0 in enumerate(range(0, sz.x, step)):
-        lax.fori_loop(x0 // 2, (x0 + step) // 2, rows, 0)
-        copies.append(pltpu.make_async_copy(out.at[x0 : x0 + step], out_hbm.at[x0 : x0 + step], sems.at[i]))
+
+    def done(x0, n):
+        copies.append(pltpu.make_async_copy(out.at[x0 : x0 + n], out_hbm.at[x0 : x0 + n], sems.at[len(copies)]))
         copies[-1].start()
+
+    inverse(sz, details, emit, done, sz.x // 4, va, ba, i1, i2, i3, ta1, ta, v3, b3, v2, b2, v1, b1, ve)
     for copy in copies:
         copy.wait()
 
@@ -610,9 +610,9 @@
     def f32(*shapes):
         return [pltpu.VMEM(s, jnp.float32) for s in shapes]
 
-    parts = [jax.ShapeDtypeStruct((2, n, n), jnp.bfloat16) for n in (t, LANES, LANES)]
+    parts = [jax.ShapeDtypeStruct((3 * n, n), jnp.bfloat16) for n in (t, LANES, LANES)]
     u, zh = (2, (x + 4) * y, LANES), (l1, sz.zrows[0], LANES)
-    sems = [pltpu.SemaphoreType.DMA((x // 8,))]
+    sems = [pltpu.SemaphoreType.DMA((x // 4,))]
     fw = f32((2, l1, y, LANES), (l1, sz.zrows[0], LANES), (l2, 2, p1, LANES), (l2, 2, sz.zrows[1], LANES),
              (l3, 2, p2, LANES), (l3, 2, sz.zrows[2], LANES))
     fine = f32((sz.zrows[0], LANES), (2, l1, y, LANES), (l1, 2, sz.zrows[0], LANES))
@@ -633,11 +633,10 @@
                           ga, gb, g2, g3, rn, rp)
         return g, (rn, rp), shifted(mp, "gx", -1), shifted(mn, "gx", 1)
 
-    weight, *rest = call(first_kernel, sz, [(x, y, t), ga, g2, g3] + messages + [u, zh] + parts + parts,
-                         fw, {}, counts)
-    g_a, g_2, g_3, mp, mn, *rest = rest
-    f, i = rest[2:5], rest[5:8]
-    g, ry, rn, rp = exchange(g_a, g_2, g_3, mp, mn, *rest[:3])
+    matrices = call(matrix_kernel, sz, parts + parts, [], {}, flops=x * y * t)
+    f, i = matrices[:3], matrices[3:]
+    weight, *rest = call(first_kernel, sz, [(x, y, t), ga, g2, g3] + messages + [u, zh], fw, {}, counts, *f)
+    g, ry, rn, rp = exchange(*rest, f[0])
     *kept, va, ba = call(inner_first_kernel, sz, [ga, gb] + halves, inner, {0: 0, 1: 1}, g[0], g[1], *ry, i[0], flops=work)
     same = {k: k for k in range(6)}
     *rest, q_a, q_2, q_3, mp, mn, u_, zh_ = call(

time: 42.6 us -> 39.8 us (0.934)
  Pallas kernels: 16.8 us -> 12.9 us
  waiting for transfers between devices: 11.8 us -> 13 us
    pallas_call x9 -> x10, Pallas kernels: 16.8 us -> 12.9 us  [call(): pl.pallas_call(functools.partial(kernel, sz), out_shape=outs, in_specs=sp...]
    ppermute x8, waiting for transfers between devices: 11.8 us -> 13 us  [shifted(): return lax.ppermute(x, axis, [(i, (i + by) % count) for i in range(count)])]
  transfers between devices with their start and end apart: 8 -> 8, of which waited for: 5 -> 5; matrix products, arithmetic and copies ran while one was open for 0% -> 0% of each run, Pallas kernels for 13% -> 11%
where the time goes in v3:
time: 39.8 us; the launch traced here: 39.6 us
  waiting for transfers between devices  13 us (33%)
  Pallas kernels  12.9 us (32%)
  starting transfers between devices  12.1 us (30%)
  local copies, waits for them, and re-layouts  1.59 us (4%)
    ppermute x8, waiting for transfers between devices, shifted(): return lax.ppermute(x, axis, [(i, (i + by) % count) for i in range(count)])  13 us
    pallas_call x10, Pallas kernels, call(): pl.pallas_call(functools.partial(kernel, sz), out_shape=outs, in_specs=sp...  12.9 us
    ppermute x8, starting transfers between devices, shifted(): return lax.ppermute(x, axis, [(i, (i + by) % count) for i in range(count)])  12.1 us
    unnamed x2, local copies, waits for them, and re-layouts  1.59 us
  transfers between devices with their start and end apart: 8, of which 5 were waited for; matrix products, arithmetic and copies ran while one was open for 0% of the time, Pallas kernels for 11%

profile of v3, /device:TPU:0, one launch (start us, length us, event | category | flops | bytes accessed | tf_op | source)
XLA Modules:
  0.0 39.6 jit_solution(17744194203369306687)
XLA Ops:
  0.0 0.4 %shard_map.17 = (bf16[768,256]{1,0:T(8,128)(2,1)S(1)}, bf16[384,128]{1,0:T(8,128)(2,1)S(1)}, bf16[384,128]{1,0:T(8,128)(2,1)S(1)}, bf16[768,256]{1,0:T(8,128)(2,...) custom-call(), custom_call_target="tpu_custom_call" | custom-call | flops 524288 | bytes 5242 | tf_op jit(solution)/shard_map/pallas_call | solution.py:592
  0.4 0.0 copy-start
  0.5 1.6 %copy-done = s32[32,64,256]{2,1,0:T(8,128)S(1)} copy-done((s32[32,64,256]{2,1,0:T(8,128)S(1)}, s32[32,64,256]{2,1,0:T(8,128)}, u32[]{:S(2)}) %copy-start) | copy-done | bytes 2097176
  2.0 1.9 %shard_map.18 = (f32[32,64,256]{2,1,0:T(8,128)S(1)}, f32[17,2,40,128]{3,2,1,0:T(8,128)S(1)}, f32[10,2,2,24,128]{4,3,2,1,0:T(8,128)S(1)}, f32[6,2,2,16,128]{4,3,2...) custom-call(s32[32,64,256]{2,1,0:T(8,128)S(1)} %copy-done, ...), custom_call_target="tpu_custom_call" | custom-call | tf_op jit(solution)/shard_map/pallas_call | solution.py:592
  3.9 0.5 %collective-permute-start.1 = (f32[168,128]{1,0:T(8,128)S(1)}, f32[168,128]{1,0:T(8,128)S(1)}, u32[]{:S(2)}, u32[]{:S(2)}) collective-permute-start(f32[168,128]{1,0:T(8,128)S(1)} %get-tuple-element.60), channel_id=1, source_target_pairs={{0,1},{1,2},{2,3},{3,0},{4,5},{5,6},{6,7},{7,4},{8,9},{9,10},{10,1... | collective-permute-start | bytes 258056 | tf_op jit(solution)/shard_map/ppermute | solution.py:23
  4.4 2.0 %collective-permute-start = (f32[144,128]{1,0:T(8,128)S(1)}, f32[144,128]{1,0:T(8,128)S(1)}, u32[]{:S(2)}, u32[]{:S(2)}) collective-permute-start(f32[144,128]{1,0:T(8,128)S(1)} %get-tuple-element.59), channel_id=1, source_target_pairs={{0,3},{1,0},{2,1},{3,2},{4,7},{5,4},{6,5},{7,6},{8,11},{9,8},{10,9... | collective-permute-start | bytes 221192 | tf_op jit(solution)/shard_map/ppermute | solution.py:23
  6.4 1.1 %shard_map.19.gbi = f32[17,3,2,40,128]{4,3,2,1,0:T(8,128)S(1)} custom-call(f32[2,2304,128]{2,1,0:T(8,128)S(1)} %get-tuple-element.55.u, f32[17,88,128]{2,1,0:T(8,128)S(1)} %get-tuple-element.56.zh, bf16[768,256]{1,0:T(8,128)(2,1)S(1)} %get-tuple-element.51.f1), custom_call_target="tpu_custom_call" | custom-call | flops 427819008 | bytes 4278190 | tf_op jit(solution)/shard_map/pallas_call | solution.py:592
  7.5 1.5 %collective-permute-done.rn = f32[144,128]{1,0:T(8,128)S(1)} collective-permute-done((f32[144,128]{1,0:T(8,128)S(1)}, f32[144,128]{1,0:T(8,128)S(1)}, u32[]{:S(2)}, u32[]{:S(2)}) %collective-permute-start) | collective-permute-done | bytes 73760 | tf_op jit(solution)/shard_map/ppermute | solution.py:23
  9.1 0.0 collective-permute-done.1.rp
  9.1 0.2 shard_map.20
  9.3 1.9 %collective-permute-start.3 = (f32[272,128]{1,0:T(8,128)S(1)}, f32[272,128]{1,0:T(8,128)S(1)}, u32[]{:S(2)}, u32[]{:S(2)}) collective-permute-start(f32[272,128]{1,0:T(8,128)S(1)} %get-tuple-element.71), channel_id=1, source_target_pairs={{0,4},{4,8},{8,12},{12,0},{1,5},{5,9},{9,13},{13,1},{2,6},{6,10},{... | collective-permute-start | bytes 417800 | tf_op jit(solution)/shard_map/ppermute | solution.py:23
  11.1 2.1 %collective-permute-start.2 = (f32[240,128]{1,0:T(8,128)S(1)}, f32[240,128]{1,0:T(8,128)S(1)}, u32[]{:S(2)}, u32[]{:S(2)}) collective-permute-start(f32[240,128]{1,0:T(8,128)S(1)} %get-tuple-element.70), channel_id=1, source_target_pairs={{0,12},{4,0},{8,4},{12,8},{1,13},{5,1},{9,5},{13,9},{2,14},{6,2},{... | collective-permute-start | bytes 368648 | tf_op jit(solution)/shard_map/ppermute | solution.py:23
  13.2 1.0 %shard_map.21 = (f32[17,2,40,128]{3,2,1,0:T(8,128)S(1)}, f32[17,3,2,40,128]{4,3,2,1,0:T(8,128)S(1)}, f32[17,64,128]{2,1,0:T(8,128)S(1)}, f32[17,64,256]{2,1,0:T(8,128)S(1)}) custom-call(f32[17,2,40,128]{3,2,1,0:T(8,128)S(1)} %get-tuple-element.61.gai, ...), custom_call_target="tpu_custom_call", output_to_operand_aliasing={{0}: (0, {}), {1}: (1, {})} | custom-call | flops 427819008 | bytes 4278190 | tf_op jit(solution)/shard_map/pallas_call | solution.py:592
  14.2 6.0 %collective-permute-done.2.rn = f32[240,128]{1,0:T(8,128)S(1)} collective-permute-done((f32[240,128]{1,0:T(8,128)S(1)}, f32[240,128]{1,0:T(8,128)S(1)}, u32[]{:S(2)}, u32[]{:S(2)}) %collective-permute-start.2) | collective-permute-done | bytes 122912 | tf_op jit(solution)/shard_map/ppermute | solution.py:23
  20.2 0.0 collective-permute-done.3.rp
  20.2 3.1 %shard_map.22 = (f32[17,2,40,128]{3,2,1,0:T(8,128)S(1)}, f32[17,3,2,40,128]{4,3,2,1,0:T(8,128)S(1)}, f32[10,2,2,24,128]{4,3,2,1,0:T(8,128)S(1)}, f32[6,2,2,16,12...) custom-call(f32[17,2,40,128]{3,2,1,0:T(8,128)S(1)} %get-tuple-elemen, ...), custom_call_target="tpu_custom_call", output_to_operand_aliasing={{0}: (0, {}), {1}: (1, {}), {2}: (2, {}), {3}: (3, {}), {4}... | custom-call | tf_op jit(solution)/shard_map/pallas_call | solution.py:592
  23.3 0.2 collective-permute-start.5
  23.5 1.6 %collective-permute-start.4 = (f32[144,128]{1,0:T(8,128)S(1)}, f32[144,128]{1,0:T(8,128)S(1)}, u32[]{:S(2)}, u32[]{:S(2)}) collective-permute-start(f32[144,128]{1,0:T(8,128)S(1)} %get-tuple-element.80), channel_id=1, source_target_pairs={{0,3},{1,0},{2,1},{3,2},{4,7},{5,4},{6,5},{7,6},{8,11},{9,8},{10,9... | collective-permute-start | bytes 221192 | tf_op jit(solution)/shard_map/ppermute | solution.py:23
  25.1 1.1 %shard_map.23.gbi = f32[17,3,2,40,128]{4,3,2,1,0:T(8,128)S(1)} custom-call(f32[2,2304,128]{2,1,0:T(8,128)S(1)} %get-tuple-element.76.u, f32[17,88,128]{2,1,0:T(8,128)S(1)} %get-tuple-element.77.zh, bf16[768,256]{1,0:T(8,128)(2,1)S(1)} %get-tuple-element.51.f1), custom_call_target="tpu_custom_call" | custom-call | flops 427819008 | bytes 4278190 | tf_op jit(solution)/shard_map/pallas_call | solution.py:592
  26.2 0.9 %collective-permute-done.4.rn = f32[144,128]{1,0:T(8,128)S(1)} collective-permute-done((f32[144,128]{1,0:T(8,128)S(1)}, f32[144,128]{1,0:T(8,128)S(1)}, u32[]{:S(2)}, u32[]{:S(2)}) %collective-permute-start.4) | collective-permute-done | bytes 73760 | tf_op jit(solution)/shard_map/ppermute | solution.py:23
  27.1 0.2 collective-permute-done.5.rp
  27.3 0.2 shard_map.24
  27.5 0.7 %collective-permute-start.7 = (f32[272,128]{1,0:T(8,128)S(1)}, f32[272,128]{1,0:T(8,128)S(1)}, u32[]{:S(2)}, u32[]{:S(2)}) collective-permute-start(f32[272,128]{1,0:T(8,128)S(1)} %get-tuple-element.93), channel_id=1, source_target_pairs={{0,4},{4,8},{8,12},{12,0},{1,5},{5,9},{9,13},{13,1},{2,6},{6,10},{... | collective-permute-start | bytes 417800 | tf_op jit(solution)/shard_map/ppermute | solution.py:23
  28.1 3.2 %collective-permute-start.6 = (f32[240,128]{1,0:T(8,128)S(1)}, f32[240,128]{1,0:T(8,128)S(1)}, u32[]{:S(2)}, u32[]{:S(2)}) collective-permute-start(f32[240,128]{1,0:T(8,128)S(1)} %get-tuple-element.92), channel_id=1, source_target_pairs={{0,12},{4,0},{8,4},{12,8},{1,13},{5,1},{9,5},{13,9},{2,14},{6,2},{... | collective-permute-start | bytes 368648 | tf_op jit(solution)/shard_map/ppermute | solution.py:23
  31.4 1.2 %shard_map.25 = (f32[17,2,40,128]{3,2,1,0:T(8,128)S(1)}, f32[17,3,2,40,128]{4,3,2,1,0:T(8,128)S(1)}, f32[17,64,128]{2,1,0:T(8,128)S(1)}, f32[17,64,256]{2,1,0:T(8,128)S(1)}) custom-call(f32[17,2,40,128]{3,2,1,0:T(8,128)S(1)} %get-tuple-element.82.qai, ...), custom_call_target="tpu_custom_call", output_to_operand_aliasing={{0}: (0, {}), {1}: (1, {})} | custom-call | flops 427819008 | bytes 4278190 | tf_op jit(solution)/shard_map/pallas_call | solution.py:592
  32.6 4.4 %collective-permute-done.6.rn = f32[240,128]{1,0:T(8,128)S(1)} collective-permute-done((f32[240,128]{1,0:T(8,128)S(1)}, f32[240,128]{1,0:T(8,128)S(1)}, u32[]{:S(2)}, u32[]{:S(2)}) %collective-permute-start.6) | collective-permute-done | bytes 122912 | tf_op jit(solution)/shard_map/ppermute | solution.py:23
  37.0 0.0 collective-permute-done.7.rp
  37.0 2.6 %shard_map.26 = (f32[17,2,40,128]{3,2,1,0:T(8,128)S(1)}, f32[17,3,2,40,128]{4,3,2,1,0:T(8,128)S(1)}, f32[10,2,2,24,128]{4,3,2,1,0:T(8,128)S(1)}, f32[6,2,2,16,12...) custom-call(f32[17,2,40,128]{3,2,1,0:T(8,128)S(1)} %get-tuple-elemen, ...), custom_call_target="tpu_custom_call", output_to_operand_aliasing={{0}: (0, {}), {1}: (1, {}), {2}: (2, {}), {3}: (3, {}), {4}... | custom-call | tf_op jit(solution)/shard_map/pallas_call | solution.py:592
Async XLA Ops:
  0.4 1.6 %copy-start = (s32[32,64,256]{2,1,0:T(8,128)S(1)}, s32[32,64,256]{2,1,0:T(8,128)}, u32[]{:S(2)}) copy-start(s32[32,64,256]{2,1,0:T(8,128)} %c.1) | copy-start | bytes 6291460
  3.9 5.2 %collective-permute-start.1 = (f32[168,128]{1,0:T(8,128)S(1)}, f32[168,128]{1,0:T(8,128)S(1)}, u32[]{:S(2)}, u32[]{:S(2)}) collective-permute-start(f32[168,128]{1,0:T(8,128)S(1)} %get-tuple-element.60), channel_id=1, source_target_pairs={{0,1},{1,2},{2,3},{3,0},{4,5},{5,6},{6,7},{7,4},{8,9},{9,10},{10,1... | collective-permute-start | bytes 258056 | tf_op jit(solution)/shard_map/ppermute | solution.py:23
  4.4 4.6 %collective-permute-start = (f32[144,128]{1,0:T(8,128)S(1)}, f32[144,128]{1,0:T(8,128)S(1)}, u32[]{:S(2)}, u32[]{:S(2)}) collective-permute-start(f32[144,128]{1,0:T(8,128)S(1)} %get-tuple-element.59), channel_id=1, source_target_pairs={{0,3},{1,0},{2,1},{3,2},{4,7},{5,4},{6,5},{7,6},{8,11},{9,8},{10,9... | collective-permute-start | bytes 221192 | tf_op jit(solution)/shard_map/ppermute | solution.py:23
  9.3 11.0 %collective-permute-start.3 = (f32[272,128]{1,0:T(8,128)S(1)}, f32[272,128]{1,0:T(8,128)S(1)}, u32[]{:S(2)}, u32[]{:S(2)}) collective-permute-start(f32[272,128]{1,0:T(8,128)S(1)} %get-tuple-element.71), channel_id=1, source_target_pairs={{0,4},{4,8},{8,12},{12,0},{1,5},{5,9},{9,13},{13,1},{2,6},{6,10},{... | collective-permute-start | bytes 417800 | tf_op jit(solution)/shard_map/ppermute | solution.py:23
  11.1 9.1 %collective-permute-start.2 = (f32[240,128]{1,0:T(8,128)S(1)}, f32[240,128]{1,0:T(8,128)S(1)}, u32[]{:S(2)}, u32[]{:S(2)}) collective-permute-start(f32[240,128]{1,0:T(8,128)S(1)} %get-tuple-element.70), channel_id=1, source_target_pairs={{0,12},{4,0},{8,4},{12,8},{1,13},{5,1},{9,5},{13,9},{2,14},{6,2},{... | collective-permute-start | bytes 368648 | tf_op jit(solution)/shard_map/ppermute | solution.py:23
  23.3 4.0 %collective-permute-start.5 = (f32[168,128]{1,0:T(8,128)S(1)}, f32[168,128]{1,0:T(8,128)S(1)}, u32[]{:S(2)}, u32[]{:S(2)}) collective-permute-start(f32[168,128]{1,0:T(8,128)S(1)} %get-tuple-element.81), channel_id=1, source_target_pairs={{0,1},{1,2},{2,3},{3,0},{4,5},{5,6},{6,7},{7,4},{8,9},{9,10},{10,1... | collective-permute-start | bytes 258056 | tf_op jit(solution)/shard_map/ppermute | solution.py:23
  23.5 3.6 %collective-permute-start.4 = (f32[144,128]{1,0:T(8,128)S(1)}, f32[144,128]{1,0:T(8,128)S(1)}, u32[]{:S(2)}, u32[]{:S(2)}) collective-permute-start(f32[144,128]{1,0:T(8,128)S(1)} %get-tuple-element.80), channel_id=1, source_target_pairs={{0,3},{1,0},{2,1},{3,2},{4,7},{5,4},{6,5},{7,6},{8,11},{9,8},{10,9... | collective-permute-start | bytes 221192 | tf_op jit(solution)/shard_map/ppermute | solution.py:23
  27.5 9.6 %collective-permute-start.7 = (f32[272,128]{1,0:T(8,128)S(1)}, f32[272,128]{1,0:T(8,128)S(1)}, u32[]{:S(2)}, u32[]{:S(2)}) collective-permute-start(f32[272,128]{1,0:T(8,128)S(1)} %get-tuple-element.93), channel_id=1, source_target_pairs={{0,4},{4,8},{8,12},{12,0},{1,5},{5,9},{9,13},{13,1},{2,6},{6,10},{... | collective-permute-start | bytes 417800 | tf_op jit(solution)/shard_map/ppermute | solution.py:23
  28.1 8.9 %collective-permute-start.6 = (f32[240,128]{1,0:T(8,128)S(1)}, f32[240,128]{1,0:T(8,128)S(1)}, u32[]{:S(2)}, u32[]{:S(2)}) collective-permute-start(f32[240,128]{1,0:T(8,128)S(1)} %get-tuple-element.92), channel_id=1, source_target_pairs={{0,12},{4,0},{8,4},{12,8},{1,13},{5,1},{9,5},{13,9},{2,14},{6,2},{... | collective-permute-start | bytes 368648 | tf_op jit(solution)/shard_map/ppermute | solution.py:23

commit v4 on v3

--- a/solution.py
+++ b/solution.py
@@ -482,7 +482,18 @@
         u[h, u_rows(u, x + 2, sz.y), :] = value[:, h * LANES : (h + 1) * LANES]
 
 
-def matrix_kernel(sz, f1, f2, f3, i1, i2, i3):
+def scaled_and_weight(c):
+    value = c.astype(jnp.float32) * (1.0 / 64.0)
+    return value, 1.0 / (1.0 + jnp.abs(value))
+
+
+def first_kernel(sz, c_hbm, ga, g2, g3, mp, mn, zh, f1, f2, f3, i1, i2, i3, c, sems, u, *scratch):
+    step = 4
+    copies = [pltpu.make_async_copy(c_hbm.at[x0 : x0 + step], c.at[x0 : x0 + step], sems.at[x0 // step])
+              for x0 in range(0, sz.x, step)]
+    for copy in copies:
+        copy.start()
+    border(sz, u)
     for level, (f, i) in enumerate(((f1, i1), (f2, i2), (f3, i3))):
         for m, transposed in ((f, False), (i, True)):
             n = m.shape[1]
@@ -490,19 +501,20 @@
             m[0:n] = high
             m[n : 2 * n] = high
             m[2 * n :] = low
-
-
-def first_kernel(sz, c, f1, f2, f3, w_ref, ga, g2, g3, mp, mn, u, zh, *scratch):
+    for x in range(sz.x):
+        if x % step == 0:
+            copies[x // step].wait()
+        value, weight = scaled_and_weight(c[x])
+        store_u(sz, u, x, weight * value)
+    forward_coarse(sz, u, f1, f2, f3, Bands(ga, None, g2, g3), zh, mp, mn, *scratch)
+
+
+def forward_fine_first_kernel(sz, c, zh, f1, gb, u, zl, a1, z1):
     border(sz, u)
-
-    def rows(x):
-        value = c[x].astype(jnp.float32) * (1.0 / 64.0)
-        weight = 1.0 / (1.0 + jnp.abs(value))
-        w_ref[x] = weight
+    for x in range(sz.x):
+        value, weight = scaled_and_weight(c[x])
         store_u(sz, u, x, weight * value)
-
-    each(0, sz.x, rows)
-    forward_coarse(sz, u, f1, f2, f3, Bands(ga, None, g2, g3), zh, mp, mn, *scratch)
+    forward_fine_kernel(sz, u, zh, f1, gb, zl, a1, z1)
 
 
 def edge_kernel(sz, gai, gbi, g2i, g3i, rn, rp, ga, gb, g2, g3, mp, mn):
@@ -533,7 +545,9 @@
     return details
 
 
-def inner_first_kernel(sz, gai, gbi, rn, rp, i1, ga, gb, va, ba, ta, v1):
+def inner_first_kernel(sz, gai, gbi, rn, rp, i1, c, ga, gb, va, ba, w_ref, ta, v1):
+    for x in range(sz.x):
+        w_ref[x] = scaled_and_weight(c[x])[1]
     g = Bands(ga, gb, None, None)
     fix_y_fine(sz, g, rn, rp, range(1, sz.lx[0] - 1))
     inner_inverse(sz, first_details(g), i1, va, ba, ta, v1)
@@ -584,7 +598,7 @@
 HBM = pltpu.MemorySpace.HBM
 
 
-def call(kernel, sz, outs, scratch, aliases, *args, outs_hbm=(), flops=0):
+def call(kernel, sz, outs, scratch, aliases, *args, ins_hbm=(), outs_hbm=(), flops=0, limit=36):
     def specs(n, in_hbm):
         return [pl.BlockSpec(memory_space=HBM if k in in_hbm else VMEM) for k in range(n)]
 
@@ -592,12 +606,12 @@
     return pl.pallas_call(
         functools.partial(kernel, sz),
         out_shape=outs,
-        in_specs=specs(len(args), ()),
+        in_specs=specs(len(args), ins_hbm),
         out_specs=specs(len(outs), outs_hbm),
         scratch_shapes=scratch,
         input_output_aliases=aliases,
         cost_estimate=pl.CostEstimate(flops=flops, bytes_accessed=flops // 100, transcendentals=0) if flops else None,
-        compiler_params=pltpu.CompilerParams(vmem_limit_bytes=36 * 2**20),
+        compiler_params=pltpu.CompilerParams(vmem_limit_bytes=limit * 2**20),
     )(*args)
 
 
@@ -626,24 +640,26 @@
     work = 6 * l1 * y * t * t
     ga, gb, g2, g3 = sz.g
 
-    def exchange(ga, g2, g3, mp, mn, u, zh, f1):
+    def exchange(ga, g2, g3, mp, mn, fine_kernel, fine_scratch, source, zh, f1):
         rn, rp = shifted(mp, "gy", -1), shifted(mn, "gy", 1)
-        (gb,) = call(forward_fine_kernel, sz, [sz.g[1]], fine, {}, u, zh, f1, flops=work)
+        (gb,) = call(fine_kernel, sz, [sz.g[1]], fine_scratch, {}, source, zh, f1, flops=work)
         *g, mp, mn = call(edge_kernel, sz, sz.g + [to_prev, to_next], [], {k: k for k in range(4)},
                           ga, gb, g2, g3, rn, rp)
         return g, (rn, rp), shifted(mp, "gx", -1), shifted(mn, "gx", 1)
 
-    matrices = call(matrix_kernel, sz, parts + parts, [], {}, flops=x * y * t)
-    f, i = matrices[:3], matrices[3:]
-    weight, *rest = call(first_kernel, sz, [(x, y, t), ga, g2, g3] + messages + [u, zh], fw, {}, counts, *f)
-    g, ry, rn, rp = exchange(*rest, f[0])
-    *kept, va, ba = call(inner_first_kernel, sz, [ga, gb] + halves, inner, {0: 0, 1: 1}, g[0], g[1], *ry, i[0], flops=work)
+    *rest, z_, f1, f2, f3, i1, i2, i3 = call(
+        first_kernel, sz, [ga, g2, g3] + messages + [zh] + parts + parts,
+        [pltpu.VMEM((x, y, t), jnp.int32)] + sems + f32(u) + fw, {}, counts, ins_hbm=(0,), limit=50)
+    f, i = [f1, f2, f3], [i1, i2, i3]
+    g, ry, rn, rp = exchange(*rest, forward_fine_first_kernel, f32(u) + fine, counts, z_, f1)
+    *kept, va, ba, weight = call(inner_first_kernel, sz, [ga, gb] + halves + [(x, y, t)], inner, {0: 0, 1: 1},
+                                 g[0], g[1], *ry, i1, counts, flops=work)
     same = {k: k for k in range(6)}
     *rest, q_a, q_2, q_3, mp, mn, u_, zh_ = call(
         middle_kernel, sz, sz.g + halves + [ga, g2, g3] + messages + [u, zh], bw + fw, same,
         *kept, g[2], g[3], va, ba, rn, rp, weight, *f, *i)
     g = rest[:4]
-    q, ry, rn, rp = exchange(q_a, q_2, q_3, mp, mn, u_, zh_, f[0])
+    q, ry, rn, rp = exchange(q_a, q_2, q_3, mp, mn, forward_fine_kernel, fine, u_, zh_, f1)
     *kept, va, ba = call(inner_last_kernel, sz, [ga, gb] + halves, inner, {0: 0, 1: 1}, q[0], q[1], *ry, i[0], g[0], g[1],
                          flops=work)
     return call(last_kernel, sz, sz.g + halves + [(x, y, t)], f32((x, y, t)) + sems + bw, same,

time: 39.8 us -> 39.2 us (0.985)
  local copies, waits for them, and re-layouts: 1.59 us -> 0.01 us
  Pallas kernels: 12.9 us -> 14.4 us
  waiting for transfers between devices: 13 us -> 12.3 us
    unnamed x2, local copies, waits for them, and re-layouts: 1.59 us -> 0.01 us
    pallas_call x10 -> x9, Pallas kernels: 12.9 us -> 14.4 us  [call(): pl.pallas_call(functools.partial(kernel, sz), out_shape=outs, in_specs=sp...]
    ppermute x8, waiting for transfers between devices: 13 us -> 12.3 us  [shifted(): return lax.ppermute(x, axis, [(i, (i + by) % count) for i in range(count)])]
  transfers between devices with their start and end apart: 8 -> 8, of which waited for: 5 -> 5; matrix products, arithmetic and copies ran while one was open for 0% -> 0% of each run, Pallas kernels for 11% -> 13%
where the time goes in v4:
time: 39.2 us; the launch traced here: 39.1 us
  Pallas kernels  14.4 us (37%)
  waiting for transfers between devices  12.3 us (31%)
  starting transfers between devices  12.1 us (31%)
    pallas_call x9, Pallas kernels, call(): pl.pallas_call(functools.partial(kernel, sz), out_shape=outs, in_specs=sp...  14.4 us
    ppermute x8, waiting for transfers between devices, shifted(): return lax.ppermute(x, axis, [(i, (i + by) % count) for i in range(count)])  12.3 us
    ppermute x8, starting transfers between devices, shifted(): return lax.ppermute(x, axis, [(i, (i + by) % count) for i in range(count)])  12.1 us
  transfers between devices with their start and end apart: 8, of which 5 were waited for; matrix products, arithmetic and copies ran while one was open for 0% of the time, Pallas kernels for 13%

profile of v4, /device:TPU:0, one launch (start us, length us, event | category | flops | bytes accessed | tf_op | source)
XLA Modules:
  0.0 39.1 jit_solution(2069083674444286721)
XLA Ops:
  0.0 0.0 copy-start
  0.0 3.2 %shard_map.17 = (f32[17,2,40,128]{3,2,1,0:T(8,128)S(1)}, f32[10,2,2,24,128]{4,3,2,1,0:T(8,128)S(1)}, f32[6,2,2,16,128]{4,3,2,1,0:T(8,128)S(1)}, f32[144,128]{1,0...) custom-call(s32[32,64,256]{2,1,0:T(8,128)} %c.3), custom_call_target="tpu_custom_call" | custom-call | tf_op jit(solution)/shard_map/pallas_call | solution.py:606
  3.2 0.5 %collective-permute-start.1 = (f32[168,128]{1,0:T(8,128)S(1)}, f32[168,128]{1,0:T(8,128)S(1)}, u32[]{:S(2)}, u32[]{:S(2)}) collective-permute-start(f32[168,128]{1,0:T(8,128)S(1)} %get-tuple-element.56), channel_id=1, source_target_pairs={{0,1},{1,2},{2,3},{3,0},{4,5},{5,6},{6,7},{7,4},{8,9},{9,10},{10,1... | collective-permute-start | bytes 258056 | tf_op jit(solution)/shard_map/ppermute | solution.py:23
  3.7 2.0 %collective-permute-start = (f32[144,128]{1,0:T(8,128)S(1)}, f32[144,128]{1,0:T(8,128)S(1)}, u32[]{:S(2)}, u32[]{:S(2)}) collective-permute-start(f32[144,128]{1,0:T(8,128)S(1)} %get-tuple-element.55), channel_id=1, source_target_pairs={{0,3},{1,0},{2,1},{3,2},{4,7},{5,4},{6,5},{7,6},{8,11},{9,8},{10,9... | collective-permute-start | bytes 221192 | tf_op jit(solution)/shard_map/ppermute | solution.py:23
  5.7 0.0 copy-done
  5.7 1.4 %shard_map.18.gbi = f32[17,3,2,40,128]{4,3,2,1,0:T(8,128)S(1)} custom-call(s32[32,64,256]{2,1,0:T(8,128)S(1)} %copy-done, f32[17,88,128]{2,1,0:T(8,128)S(1)} %get-tuple-element.51.zh, bf16[768,256]{1,0:T(8,128)(2,1)S(1)} %get-tuple-element.52.f1), custom_call_target="tpu_custom_call" | custom-call | flops 427819008 | bytes 4278190 | tf_op jit(solution)/shard_map/pallas_call | solution.py:606
  7.2 1.2 %collective-permute-done.rn = f32[144,128]{1,0:T(8,128)S(1)} collective-permute-done((f32[144,128]{1,0:T(8,128)S(1)}, f32[144,128]{1,0:T(8,128)S(1)}, u32[]{:S(2)}, u32[]{:S(2)}) %collective-permute-start) | collective-permute-done | bytes 73760 | tf_op jit(solution)/shard_map/ppermute | solution.py:23
  8.4 0.0 collective-permute-done.1.rp
  8.4 0.2 shard_map.19
  8.6 1.9 %collective-permute-start.3 = (f32[272,128]{1,0:T(8,128)S(1)}, f32[272,128]{1,0:T(8,128)S(1)}, u32[]{:S(2)}, u32[]{:S(2)}) collective-permute-start(f32[272,128]{1,0:T(8,128)S(1)} %get-tuple-element.67), channel_id=1, source_target_pairs={{0,4},{4,8},{8,12},{12,0},{1,5},{5,9},{9,13},{13,1},{2,6},{6,10},{... | collective-permute-start | bytes 417800 | tf_op jit(solution)/shard_map/ppermute | solution.py:23
  10.5 2.1 %collective-permute-start.2 = (f32[240,128]{1,0:T(8,128)S(1)}, f32[240,128]{1,0:T(8,128)S(1)}, u32[]{:S(2)}, u32[]{:S(2)}) collective-permute-start(f32[240,128]{1,0:T(8,128)S(1)} %get-tuple-element.66), channel_id=1, source_target_pairs={{0,12},{4,0},{8,4},{12,8},{1,13},{5,1},{9,5},{13,9},{2,14},{6,2},{... | collective-permute-start | bytes 368648 | tf_op jit(solution)/shard_map/ppermute | solution.py:23
  12.6 1.3 %shard_map.20 = (f32[17,2,40,128]{3,2,1,0:T(8,128)S(1)}, f32[17,3,2,40,128]{4,3,2,1,0:T(8,128)S(1)}, f32[17,64,128]{2,1,0:T(8,128)S(1)}, f32[17,64,256]{2,1,0:T(8,128)S(1)}, f32[32,64,256]{2,1,0:T(8,128)S(1)}) custom-call(f32[17,2,40,128]{3,2,1,0:T(8,128)S(1)} %get-tuple-element.57.gai, ...), custom_call_target="tpu_custom_call", output_to_operand_aliasing={{0}: (0, {}), {1}: (1, {})} | custom-call | flops 427819008 | bytes 4278190 | tf_op jit(solution)/shard_map/pallas_call | solution.py:606
  13.9 5.6 %collective-permute-done.2.rn = f32[240,128]{1,0:T(8,128)S(1)} collective-permute-done((f32[240,128]{1,0:T(8,128)S(1)}, f32[240,128]{1,0:T(8,128)S(1)}, u32[]{:S(2)}, u32[]{:S(2)}) %collective-permute-start.2) | collective-permute-done | bytes 122912 | tf_op jit(solution)/shard_map/ppermute | solution.py:23
  19.5 0.0 collective-permute-done.3.rp
  19.5 3.1 %shard_map.21 = (f32[17,2,40,128]{3,2,1,0:T(8,128)S(1)}, f32[17,3,2,40,128]{4,3,2,1,0:T(8,128)S(1)}, f32[10,2,2,24,128]{4,3,2,1,0:T(8,128)S(1)}, f32[6,2,2,16,12...) custom-call(f32[17,2,40,128]{3,2,1,0:T(8,128)S(1)} %get-tuple-elemen, ...), custom_call_target="tpu_custom_call", output_to_operand_aliasing={{0}: (0, {}), {1}: (1, {}), {2}: (2, {}), {3}: (3, {}), {4}... | custom-call | tf_op jit(solution)/shard_map/pallas_call | solution.py:606
  22.6 0.2 collective-permute-start.5
  22.8 1.6 %collective-permute-start.4 = (f32[144,128]{1,0:T(8,128)S(1)}, f32[144,128]{1,0:T(8,128)S(1)}, u32[]{:S(2)}, u32[]{:S(2)}) collective-permute-start(f32[144,128]{1,0:T(8,128)S(1)} %get-tuple-element.78), channel_id=1, source_target_pairs={{0,3},{1,0},{2,1},{3,2},{4,7},{5,4},{6,5},{7,6},{8,11},{9,8},{10,9... | collective-permute-start | bytes 221192 | tf_op jit(solution)/shard_map/ppermute | solution.py:23
  24.4 1.1 %shard_map.22.gbi = f32[17,3,2,40,128]{4,3,2,1,0:T(8,128)S(1)} custom-call(f32[2,2304,128]{2,1,0:T(8,128)S(1)} %get-tuple-element.74.u, f32[17,88,128]{2,1,0:T(8,128)S(1)} %get-tuple-element.75.zh, bf16[768,256]{1,0:T(8,128)(2,1)S(1)} %get-tuple-element.52.f1), custom_call_target="tpu_custom_call" | custom-call | flops 427819008 | bytes 4278190 | tf_op jit(solution)/shard_map/pallas_call | solution.py:606
  25.5 0.9 %collective-permute-done.4.rn = f32[144,128]{1,0:T(8,128)S(1)} collective-permute-done((f32[144,128]{1,0:T(8,128)S(1)}, f32[144,128]{1,0:T(8,128)S(1)}, u32[]{:S(2)}, u32[]{:S(2)}) %collective-permute-start.4) | collective-permute-done | bytes 73760 | tf_op jit(solution)/shard_map/ppermute | solution.py:23
  26.4 0.2 collective-permute-done.5.rp
  26.6 0.2 shard_map.23
  26.8 0.7 %collective-permute-start.7 = (f32[272,128]{1,0:T(8,128)S(1)}, f32[272,128]{1,0:T(8,128)S(1)}, u32[]{:S(2)}, u32[]{:S(2)}) collective-permute-start(f32[272,128]{1,0:T(8,128)S(1)} %get-tuple-element.91), channel_id=1, source_target_pairs={{0,4},{4,8},{8,12},{12,0},{1,5},{5,9},{9,13},{13,1},{2,6},{6,10},{... | collective-permute-start | bytes 417800 | tf_op jit(solution)/shard_map/ppermute | solution.py:23
  27.5 3.2 %collective-permute-start.6 = (f32[240,128]{1,0:T(8,128)S(1)}, f32[240,128]{1,0:T(8,128)S(1)}, u32[]{:S(2)}, u32[]{:S(2)}) collective-permute-start(f32[240,128]{1,0:T(8,128)S(1)} %get-tuple-element.90), channel_id=1, source_target_pairs={{0,12},{4,0},{8,4},{12,8},{1,13},{5,1},{9,5},{13,9},{2,14},{6,2},{... | collective-permute-start | bytes 368648 | tf_op jit(solution)/shard_map/ppermute | solution.py:23
  30.7 1.3 %shard_map.24 = (f32[17,2,40,128]{3,2,1,0:T(8,128)S(1)}, f32[17,3,2,40,128]{4,3,2,1,0:T(8,128)S(1)}, f32[17,64,128]{2,1,0:T(8,128)S(1)}, f32[17,64,256]{2,1,0:T(8,128)S(1)}) custom-call(f32[17,2,40,128]{3,2,1,0:T(8,128)S(1)} %get-tuple-element.80.qai, ...), custom_call_target="tpu_custom_call", output_to_operand_aliasing={{0}: (0, {}), {1}: (1, {})} | custom-call | flops 427819008 | bytes 4278190 | tf_op jit(solution)/shard_map/pallas_call | solution.py:606
  31.9 4.4 %collective-permute-done.6.rn = f32[240,128]{1,0:T(8,128)S(1)} collective-permute-done((f32[240,128]{1,0:T(8,128)S(1)}, f32[240,128]{1,0:T(8,128)S(1)}, u32[]{:S(2)}, u32[]{:S(2)}) %collective-permute-start.6) | collective-permute-done | bytes 122912 | tf_op jit(solution)/shard_map/ppermute | solution.py:23
  36.3 0.0 collective-permute-done.7.rp
  36.3 2.6 %shard_map.25 = (f32[17,2,40,128]{3,2,1,0:T(8,128)S(1)}, f32[17,3,2,40,128]{4,3,2,1,0:T(8,128)S(1)}, f32[10,2,2,24,128]{4,3,2,1,0:T(8,128)S(1)}, f32[6,2,2,16,12...) custom-call(f32[17,2,40,128]{3,2,1,0:T(8,128)S(1)} %get-tuple-elemen, ...), custom_call_target="tpu_custom_call", output_to_operand_aliasing={{0}: (0, {}), {1}: (1, {}), {2}: (2, {}), {3}: (3, {}), {4}... | custom-call | tf_op jit(solution)/shard_map/pallas_call | solution.py:606
Async XLA Ops:
  0.0 5.7 %copy-start = (s32[32,64,256]{2,1,0:T(8,128)S(1)}, s32[32,64,256]{2,1,0:T(8,128)}, u32[]{:S(2)}) copy-start(s32[32,64,256]{2,1,0:T(8,128)} %c.3) | copy-start | bytes 6291460
  3.2 5.2 %collective-permute-start.1 = (f32[168,128]{1,0:T(8,128)S(1)}, f32[168,128]{1,0:T(8,128)S(1)}, u32[]{:S(2)}, u32[]{:S(2)}) collective-permute-start(f32[168,128]{1,0:T(8,128)S(1)} %get-tuple-element.56), channel_id=1, source_target_pairs={{0,1},{1,2},{2,3},{3,0},{4,5},{5,6},{6,7},{7,4},{8,9},{9,10},{10,1... | collective-permute-start | bytes 258056 | tf_op jit(solution)/shard_map/ppermute | solution.py:23
  3.7 4.7 %collective-permute-start = (f32[144,128]{1,0:T(8,128)S(1)}, f32[144,128]{1,0:T(8,128)S(1)}, u32[]{:S(2)}, u32[]{:S(2)}) collective-permute-start(f32[144,128]{1,0:T(8,128)S(1)} %get-tuple-element.55), channel_id=1, source_target_pairs={{0,3},{1,0},{2,1},{3,2},{4,7},{5,4},{6,5},{7,6},{8,11},{9,8},{10,9... | collective-permute-start | bytes 221192 | tf_op jit(solution)/shard_map/ppermute | solution.py:23
  8.6 11.0 %collective-permute-start.3 = (f32[272,128]{1,0:T(8,128)S(1)}, f32[272,128]{1,0:T(8,128)S(1)}, u32[]{:S(2)}, u32[]{:S(2)}) collective-permute-start(f32[272,128]{1,0:T(8,128)S(1)} %get-tuple-element.67), channel_id=1, source_target_pairs={{0,4},{4,8},{8,12},{12,0},{1,5},{5,9},{9,13},{13,1},{2,6},{6,10},{... | collective-permute-start | bytes 417800 | tf_op jit(solution)/shard_map/ppermute | solution.py:23
  10.5 9.1 %collective-permute-start.2 = (f32[240,128]{1,0:T(8,128)S(1)}, f32[240,128]{1,0:T(8,128)S(1)}, u32[]{:S(2)}, u32[]{:S(2)}) collective-permute-start(f32[240,128]{1,0:T(8,128)S(1)} %get-tuple-element.66), channel_id=1, source_target_pairs={{0,12},{4,0},{8,4},{12,8},{1,13},{5,1},{9,5},{13,9},{2,14},{6,2},{... | collective-permute-start | bytes 368648 | tf_op jit(solution)/shard_map/ppermute | solution.py:23
  22.6 4.0 %collective-permute-start.5 = (f32[168,128]{1,0:T(8,128)S(1)}, f32[168,128]{1,0:T(8,128)S(1)}, u32[]{:S(2)}, u32[]{:S(2)}) collective-permute-start(f32[168,128]{1,0:T(8,128)S(1)} %get-tuple-element.79), channel_id=1, source_target_pairs={{0,1},{1,2},{2,3},{3,0},{4,5},{5,6},{6,7},{7,4},{8,9},{9,10},{10,1... | collective-permute-start | bytes 258056 | tf_op jit(solution)/shard_map/ppermute | solution.py:23
  22.8 3.6 %collective-permute-start.4 = (f32[144,128]{1,0:T(8,128)S(1)}, f32[144,128]{1,0:T(8,128)S(1)}, u32[]{:S(2)}, u32[]{:S(2)}) collective-permute-start(f32[144,128]{1,0:T(8,128)S(1)} %get-tuple-element.78), channel_id=1, source_target_pairs={{0,3},{1,0},{2,1},{3,2},{4,7},{5,4},{6,5},{7,6},{8,11},{9,8},{10,9... | collective-permute-start | bytes 221192 | tf_op jit(solution)/shard_map/ppermute | solution.py:23
  26.8 9.5 %collective-permute-start.7 = (f32[272,128]{1,0:T(8,128)S(1)}, f32[272,128]{1,0:T(8,128)S(1)}, u32[]{:S(2)}, u32[]{:S(2)}) collective-permute-start(f32[272,128]{1,0:T(8,128)S(1)} %get-tuple-element.91), channel_id=1, source_target_pairs={{0,4},{4,8},{8,12},{12,0},{1,5},{5,9},{9,13},{13,1},{2,6},{6,10},{... | collective-permute-start | bytes 417800 | tf_op jit(solution)/shard_map/ppermute | solution.py:23
  27.5 8.9 %collective-permute-start.6 = (f32[240,128]{1,0:T(8,128)S(1)}, f32[240,128]{1,0:T(8,128)S(1)}, u32[]{:S(2)}, u32[]{:S(2)}) collective-permute-start(f32[240,128]{1,0:T(8,128)S(1)} %get-tuple-element.90), channel_id=1, source_target_pairs={{0,12},{4,0},{8,4},{12,8},{1,13},{5,1},{9,5},{13,9},{2,14},{6,2},{... | collective-permute-start | bytes 368648 | tf_op jit(solution)/shard_map/ppermute | solution.py:23

commit v5 on v4

--- a/solution.py
+++ b/solution.py
@@ -49,6 +49,11 @@
 def each(first, end, body):
     for i in range(first, end):
         body(i)
+
+
+def dot_parts_narrow(x, m_ref):
+    out = jnp.dot(jnp.concatenate(split(x), axis=-1), m_ref[...], preferred_element_type=jnp.float32)
+    return out[:, :LANES] + out[:, LANES:]
 
 
 def ceil8(n):
@@ -193,7 +198,7 @@
             low, high = x_lattice_static(rows, (p_in, LANES))
             a[s, 0] = low
             a[s, 1] = high
-        out = dot_parts(a[...].reshape(count * 2 * p_in, LANES), f)
+        out = dot_parts_narrow(a[...].reshape(count * 2 * p_in, LANES), f)
         z[:, :, 8 : 8 + p_in, :] = out.reshape(count, 2, p_in, LANES)
         for s in range(count):
             for xb in range(2):
@@ -389,7 +394,7 @@
 
 
 def level_1_columns(sz, details, s, xb, tb, coarse, ta, v1, index):
-    low = coarse if coarse is not None else details(0, s, xb, tb, None)
+    low = details(0, s, xb, tb, None) if coarse is None else coarse
     high = details(0, s, xb, 2 + tb, None)
     y_synthesis(low, high, sz.y // 2, ta.at[s, xb * 2 + tb, 0 : sz.py[0]], v1, index, 0)
 
@@ -399,38 +404,33 @@
     return dot_parts(v.reshape(-1, sz.t), i1).reshape(v.shape)
 
 
-def inner_inverse(sz, details, i1, va, ba, ta, v1):
+def inner_inverse(sz, details, i1, ba, ta, v1):
     l1 = sz.lx[0]
 
     def rows(s):
-        level_1_columns(sz, details, s, 0, 1, None, ta, va, (s,))
-        level_1_columns(sz, details, s, 1, 0, None, ta, v1, (s, 0))
-        level_1_columns(sz, details, s, 1, 1, None, ta, v1, (s, 1))
+        for xb in range(2):
+            for tb in range(2):
+                coarse = 0.0 if xb == 0 and tb == 0 else None
+                level_1_columns(sz, details, s, xb, tb, coarse, ta, v1, (tb, s, xb))
 
     each(1, l1 - 1, rows)
-    step = 15
-    for s0 in range(1, l1 - 1, step):
-        n = min(step, l1 - 1 - s0)
-        ba[s0 : s0 + n] = times_back(sz, v1[s0 : s0 + n, 0], v1[s0 : s0 + n, 1], i1)
-
-
-def inverse(sz, details, emit, done, groups, va, ba, i1, i2, i3, ta1, ta, v3, b3, v2, b2, v1, b1, ve):
+    for s0 in range(1, l1 - 1, 15):
+        n = min(15, l1 - 1 - s0)
+        ba[s0 : s0 + n] = times_back(sz, v1[0, s0 : s0 + n], v1[1, s0 : s0 + n], i1)
+
+
+def inverse(sz, details, emit, done, groups, ba, i1, i2, i3, ta1, ta, v3, b3, v2, b2, v1, b1, ve):
     y, t = sz.y, sz.t
     p1, p2, p3 = sz.py
     l1, l2, l3 = sz.lx
     third = lane_below(t // 8, (p3, LANES))
-
-    for e, s in enumerate((0, l1 - 1)):
-        level_1_columns(sz, details, s, 0, 1, None, ta1, va, (s,))
-        level_1_columns(sz, details, s, 1, 0, None, ta1, ve, (e, 0))
-        level_1_columns(sz, details, s, 1, 1, None, ta1, ve, (e, 1))
 
     for s in range(l3):
         for xb in range(2):
             low = details(2, s, xb, 0, third if xb == 0 else None)
             high = details(2, s, xb, 1, None)
             y_synthesis(low, high, sz.ly[1] // 2, ta.at[1, s, xb, 0:p3], v3, (s, xb), 0)
-    b3[...] = dot_parts(v3[...].reshape(l3 * 2 * p2, LANES), i3).reshape(l3, 2, p2, LANES)
+    b3[...] = dot_parts_narrow(v3[...].reshape(l3 * 2 * p2, LANES), i3).reshape(l3, 2, p2, LANES)
 
     second = lane_below(t // 4, (p2, LANES))
     for p in range(l2 // 2):
@@ -442,30 +442,43 @@
                     low = jnp.where(second, coarse, low)
                 high = details(1, s, xb, 1, None)
                 y_synthesis(low, high, (sz.ly[0] + 1) // 2, ta.at[0, s, xb, 0:p2], v2, (s, xb), 7)
-    b2[...] = dot_parts(v2[:, :, 8 : 8 + p1, :].reshape(l2 * 2 * p1, LANES), i2).reshape(l2, 2, p1, LANES)
-
-    edge = times_back(sz, ve[:, 0], ve[:, 1], i1)
-    ba[0] = edge[0]
-    ba[l1 - 1] = edge[1]
+    b2[...] = dot_parts_narrow(v2[:, :, 8 : 8 + p1, :].reshape(l2 * 2 * p1, LANES), i2).reshape(l2, 2, p1, LANES)
 
     def coarse_rows(p):
         return lattice_t(b2[p + 1, 0], b2[p + 1, 1], b2[p, 0], b2[p, 1])
 
+    n = t // 2
+    half = jnp.concatenate([i1[0:n], i1[t : t + n], i1[2 * t : 2 * t + n]], axis=0)
+
+    def coarse_columns(s, low):
+        y_synthesis(low, 0.0, y // 2, ta1.at[s, 0, 0:p1], v1, (s,), 0)
+
     def pair_1(p):
         even, odd = coarse_rows(p)
-        level_1_columns(sz, details, 2 * p - 1, 0, 0, even, ta1, v1, (2 * p - 1,))
-        level_1_columns(sz, details, 2 * p, 0, 0, odd, ta1, v1, (2 * p,))
+        coarse_columns(2 * p - 1, even)
+        if p < l2 - 2:
+            coarse_columns(2 * p, odd)
+        else:
+            ends.append(odd)
 
     def rows_x(p):
-        even, odd = lattice_t(b1[p + 1], ba[p + 1], b1[p], ba[p])
+        even, odd = lattice_t(b1[p + 1] + ba[p + 1, 0], ba[p + 1, 1], b1[p] + ba[p, 0], ba[p, 1])
         emit(p, even, odd)
 
-    level_1_columns(sz, details, 0, 0, 0, coarse_rows(0)[1], ta1, v1, (0,))
+    ends = [coarse_rows(0)[1]]
     step = sz.x // groups
     for x0 in range(0, sz.x, step):
         each(x0 // 4 + 1, (x0 + step) // 4 + 1, pair_1)
-        s0, s1 = (x0 // 2 + 1 if x0 else 0), (x0 + step) // 2 + 1
-        b1[s0:s1] = times_back(sz, v1[s0:s1], va[s0:s1], i1)
+        s0, s1 = x0 // 2 + 1, min((x0 + step) // 2 + 1, l1 - 1)
+        b1[s0:s1] = dot_parts(v1[s0:s1].reshape(-1, LANES), half).reshape(s1 - s0, y, t)
+        if x0 == 0 or x0 + step == sz.x:
+            e, s = (0, 0) if x0 == 0 else (1, l1 - 1)
+            for xb in range(2):
+                for tb in range(2):
+                    coarse = ends[e] if xb == 0 and tb == 0 else None
+                    level_1_columns(sz, details, s, xb, tb, coarse, ta1, ve, (tb, e, xb))
+            ba[s] = times_back(sz, ve[0, e], ve[1, e], i1)
+            b1[s] = jnp.zeros((y, t), jnp.float32)
         each(x0 // 2, (x0 + step) // 2, rows_x)
         done(x0, step)
 
@@ -496,11 +509,15 @@
     border(sz, u)
     for level, (f, i) in enumerate(((f1, i1), (f2, i2), (f3, i3))):
         for m, transposed in ((f, False), (i, True)):
-            n = m.shape[1]
+            n = LANES if level else sz.t
             high, low = split(time_matrix(sz.t >> level, n, transposed))
-            m[0:n] = high
-            m[n : 2 * n] = high
-            m[2 * n :] = low
+            m[0:n, 0:n] = high
+            m[n : 2 * n, 0:n] = high
+            if level:
+                m[0:n, n:] = low
+                m[n:, n:] = jnp.zeros_like(low)
+            else:
+                m[2 * n :] = low
     for x in range(sz.x):
         if x % step == 0:
             copies[x // step].wait()
@@ -545,22 +562,22 @@
     return details
 
 
-def inner_first_kernel(sz, gai, gbi, rn, rp, i1, c, ga, gb, va, ba, w_ref, ta, v1):
+def inner_first_kernel(sz, gai, gbi, rn, rp, i1, c, ga, gb, ba, w_ref, ta, v1):
     for x in range(sz.x):
         w_ref[x] = scaled_and_weight(c[x])[1]
     g = Bands(ga, gb, None, None)
     fix_y_fine(sz, g, rn, rp, range(1, sz.lx[0] - 1))
-    inner_inverse(sz, first_details(g), i1, va, ba, ta, v1)
-
-
-def inner_last_kernel(sz, qai, qbi, rn, rp, i1, ga, gb, qa, qb, va, ba, ta, v1):
+    inner_inverse(sz, first_details(g), i1, ba, ta, v1)
+
+
+def inner_last_kernel(sz, qai, qbi, rn, rp, i1, ga, gb, qa, qb, ba, ta, v1):
     q = Bands(qa, qb, None, None)
     fix_y_fine(sz, q, rn, rp, range(1, sz.lx[0] - 1))
-    inner_inverse(sz, second_details(Bands(ga, gb, None, None), q), i1, va, ba, ta, v1)
-
-
-def middle_kernel(sz, gai, gbi, g2i, g3i, vai, bai, rn, rp, w_ref, f1, f2, f3, i1, i2, i3,
-                  ga, gb, g2, g3, va, ba, qa, q2, q3, mp, mn, u, zh, ta1, ta, v3, b3, v2, b2, v1, b1, ve, *scratch):
+    inner_inverse(sz, second_details(Bands(ga, gb, None, None), q), i1, ba, ta, v1)
+
+
+def middle_kernel(sz, gai, gbi, g2i, g3i, bai, rn, rp, w_ref, f1, f2, f3, i1, i2, i3,
+                  ga, gb, g2, g3, ba, qa, q2, q3, mp, mn, u, zh, ta1, ta, v3, b3, v2, b2, v1, b1, ve, *scratch):
     g = Bands(ga, gb, g2, g3)
     fix_x(sz, g, rn, rp)
     border(sz, u)
@@ -569,12 +586,12 @@
         store_u(sz, u, 2 * p, w_ref[2 * p] * even)
         store_u(sz, u, 2 * p + 1, w_ref[2 * p + 1] * odd)
 
-    inverse(sz, first_details(g), emit, lambda x0, n: None, 2, va, ba, i1, i2, i3, ta1, ta, v3, b3, v2, b2, v1, b1, ve)
+    inverse(sz, first_details(g), emit, lambda x0, n: None, 2, ba, i1, i2, i3, ta1, ta, v3, b3, v2, b2, v1, b1, ve)
     forward_coarse(sz, u, f1, f2, f3, Bands(qa, None, q2, q3), zh, mp, mn, *scratch)
 
 
-def last_kernel(sz, qai, qbi, q2i, q3i, vai, bai, rn, rp, ga, gb, g2, g3, i1, i2, i3,
-                qa, qb, q2, q3, va, ba, out_hbm, out, sems, ta1, ta, v3, b3, v2, b2, v1, b1, ve):
+def last_kernel(sz, qai, qbi, q2i, q3i, bai, rn, rp, ga, gb, g2, g3, i1, i2, i3,
+                qa, qb, q2, q3, ba, out_hbm, out, sems, ta1, ta, v3, b3, v2, b2, v1, b1, ve):
     q = Bands(qa, qb, q2, q3)
     fix_x(sz, q, rn, rp)
 
@@ -589,7 +606,7 @@
         copies.append(pltpu.make_async_copy(out.at[x0 : x0 + n], out_hbm.at[x0 : x0 + n], sems.at[len(copies)]))
         copies[-1].start()
 
-    inverse(sz, details, emit, done, sz.x // 4, va, ba, i1, i2, i3, ta1, ta, v3, b3, v2, b2, v1, b1, ve)
+    inverse(sz, details, emit, done, sz.x // 4, ba, i1, i2, i3, ta1, ta, v3, b3, v2, b2, v1, b1, ve)
     for copy in copies:
         copy.wait()
 
@@ -624,7 +641,7 @@
     def f32(*shapes):
         return [pltpu.VMEM(s, jnp.float32) for s in shapes]
 
-    parts = [jax.ShapeDtypeStruct((3 * n, n), jnp.bfloat16) for n in (t, LANES, LANES)]
+    parts = [jax.ShapeDtypeStruct(s, jnp.bfloat16) for s in ((3 * t, t), (2 * LANES,) * 2, (2 * LANES,) * 2)]
     u, zh = (2, (x + 4) * y, LANES), (l1, sz.zrows[0], LANES)
     sems = [pltpu.SemaphoreType.DMA((x // 4,))]
     fw = f32((2, l1, y, LANES), (l1, sz.zrows[0], LANES), (l2, 2, p1, LANES), (l2, 2, sz.zrows[1], LANES),
@@ -632,11 +649,11 @@
     fine = f32((sz.zrows[0], LANES), (2, l1, y, LANES), (l1, 2, sz.zrows[0], LANES))
     ta1 = f32((l1, 4, p1 + 8, LANES))
     bw = ta1 + f32((2, l2, 2, p2 + 8, LANES), (l3, 2, p2, LANES), (l3, 2, p2, LANES), (l2, 2, p1 + 8, LANES),
-                   (l2, 2, p1, LANES), (l1, y, LANES), (l1, y, t), (2, 2, y, LANES))
+                   (l2, 2, p1, LANES), (l1, y, LANES), (l1, y, t), (2, 2, 2, y, LANES))
     to_prev, to_next = (sz.xp, LANES), (sz.xn, LANES)
     messages = [(sz.yp, LANES), (sz.yn, LANES)]
-    halves = [(l1, y, LANES), (l1, y, t)]
-    inner = ta1 + f32((l1, 2, y, LANES))
+    halves = [(l1, 2, y, t)]
+    inner = ta1 + f32((2, l1, 2, y, LANES))
     work = 6 * l1 * y * t * t
     ga, gb, g2, g3 = sz.g
 
@@ -652,18 +669,18 @@
         [pltpu.VMEM((x, y, t), jnp.int32)] + sems + f32(u) + fw, {}, counts, ins_hbm=(0,), limit=50)
     f, i = [f1, f2, f3], [i1, i2, i3]
     g, ry, rn, rp = exchange(*rest, forward_fine_first_kernel, f32(u) + fine, counts, z_, f1)
-    *kept, va, ba, weight = call(inner_first_kernel, sz, [ga, gb] + halves + [(x, y, t)], inner, {0: 0, 1: 1},
+    *kept, ba, weight = call(inner_first_kernel, sz, [ga, gb] + halves + [(x, y, t)], inner, {0: 0, 1: 1},
                                  g[0], g[1], *ry, i1, counts, flops=work)
-    same = {k: k for k in range(6)}
+    same = {k: k for k in range(5)}
     *rest, q_a, q_2, q_3, mp, mn, u_, zh_ = call(
         middle_kernel, sz, sz.g + halves + [ga, g2, g3] + messages + [u, zh], bw + fw, same,
-        *kept, g[2], g[3], va, ba, rn, rp, weight, *f, *i)
+        *kept, g[2], g[3], ba, rn, rp, weight, *f, *i)
     g = rest[:4]
     q, ry, rn, rp = exchange(q_a, q_2, q_3, mp, mn, forward_fine_kernel, fine, u_, zh_, f1)
-    *kept, va, ba = call(inner_last_kernel, sz, [ga, gb] + halves, inner, {0: 0, 1: 1}, q[0], q[1], *ry, i[0], g[0], g[1],
+    *kept, ba = call(inner_last_kernel, sz, [ga, gb] + halves, inner, {0: 0, 1: 1}, q[0], q[1], *ry, i[0], g[0], g[1],
                          flops=work)
     return call(last_kernel, sz, sz.g + halves + [(x, y, t)], f32((x, y, t)) + sems + bw, same,
-                *kept, q[2], q[3], va, ba, rn, rp, *g, *i, outs_hbm=(6,))[6]
+                *kept, q[2], q[3], ba, rn, rp, *g, *i, outs_hbm=(5,))[5]
 
 
 def solution(mesh):

time: 39.2 us -> 38.8 us (0.990)
  waiting for transfers between devices: 12.3 us -> 11.5 us
  Pallas kernels: 14.4 us -> 14.8 us
    ppermute x8, waiting for transfers between devices: 12.3 us -> 11.5 us  [shifted(): return lax.ppermute(x, axis, [(i, (i + by) % count) for i in range(count)])]
  transfers between devices with their start and end apart: 8 -> 8, of which waited for: 5 -> 5; matrix products, arithmetic and copies ran while one was open for 0% -> 0% of each run, Pallas kernels for 13% -> 15%
where the time goes in v5:
time: 38.8 us; the launch traced here: 38.7 us
  Pallas kernels  14.8 us (38%)
  starting transfers between devices  12.1 us (31%)
  waiting for transfers between devices  11.5 us (30%)
    pallas_call x9, Pallas kernels, call(): pl.pallas_call(functools.partial(kernel, sz), out_shape=outs, in_specs=sp...  14.8 us
    ppermute x8, starting transfers between devices, shifted(): return lax.ppermute(x, axis, [(i, (i + by) % count) for i in range(count)])  12.1 us
    ppermute x8, waiting for transfers between devices, shifted(): return lax.ppermute(x, axis, [(i, (i + by) % count) for i in range(count)])  11.5 us
  transfers between devices with their start and end apart: 8, of which 5 were waited for; matrix products, arithmetic and copies ran while one was open for 0% of the time, Pallas kernels for 15%

profile of v5, /device:TPU:0, one launch (start us, length us, event | category | flops | bytes accessed | tf_op | source)
XLA Modules:
  0.0 38.7 jit_solution(1153103876602787603)
XLA Ops:
  0.0 0.0 copy-start
  0.0 3.3 %shard_map.17 = (f32[17,2,40,128]{3,2,1,0:T(8,128)S(1)}, f32[10,2,2,24,128]{4,3,2,1,0:T(8,128)S(1)}, f32[6,2,2,16,128]{4,3,2,1,0:T(8,128)S(1)}, f32[144,128]{1,0...) custom-call(s32[32,64,256]{2,1,0:T(8,128)} %c.3), custom_call_target="tpu_custom_call" | custom-call | tf_op jit(solution)/shard_map/pallas_call | solution.py:623
  3.3 0.5 %collective-permute-start.1 = (f32[168,128]{1,0:T(8,128)S(1)}, f32[168,128]{1,0:T(8,128)S(1)}, u32[]{:S(2)}, u32[]{:S(2)}) collective-permute-start(f32[168,128]{1,0:T(8,128)S(1)} %get-tuple-element.54), channel_id=1, source_target_pairs={{0,1},{1,2},{2,3},{3,0},{4,5},{5,6},{6,7},{7,4},{8,9},{9,10},{10,1... | collective-permute-start | bytes 258056 | tf_op jit(solution)/shard_map/ppermute | solution.py:23
  3.8 2.0 %collective-permute-start = (f32[144,128]{1,0:T(8,128)S(1)}, f32[144,128]{1,0:T(8,128)S(1)}, u32[]{:S(2)}, u32[]{:S(2)}) collective-permute-start(f32[144,128]{1,0:T(8,128)S(1)} %get-tuple-element.53), channel_id=1, source_target_pairs={{0,3},{1,0},{2,1},{3,2},{4,7},{5,4},{6,5},{7,6},{8,11},{9,8},{10,9... | collective-permute-start | bytes 221192 | tf_op jit(solution)/shard_map/ppermute | solution.py:23
  5.8 0.0 copy-done
  5.8 1.4 %shard_map.18.gbi = f32[17,3,2,40,128]{4,3,2,1,0:T(8,128)S(1)} custom-call(s32[32,64,256]{2,1,0:T(8,128)S(1)} %copy-done, f32[17,88,128]{2,1,0:T(8,128)S(1)} %get-tuple-element.49.zh, bf16[768,256]{1,0:T(8,128)(2,1)S(1)} %get-tuple-element.50.f1), custom_call_target="tpu_custom_call" | custom-call | flops 427819008 | bytes 4278190 | tf_op jit(solution)/shard_map/pallas_call | solution.py:623
  7.3 1.2 %collective-permute-done.rn = f32[144,128]{1,0:T(8,128)S(1)} collective-permute-done((f32[144,128]{1,0:T(8,128)S(1)}, f32[144,128]{1,0:T(8,128)S(1)}, u32[]{:S(2)}, u32[]{:S(2)}) %collective-permute-start) | collective-permute-done | bytes 73760 | tf_op jit(solution)/shard_map/ppermute | solution.py:23
  8.5 0.0 collective-permute-done.1.rp
  8.5 0.2 shard_map.19
  8.7 1.9 %collective-permute-start.3 = (f32[272,128]{1,0:T(8,128)S(1)}, f32[272,128]{1,0:T(8,128)S(1)}, u32[]{:S(2)}, u32[]{:S(2)}) collective-permute-start(f32[272,128]{1,0:T(8,128)S(1)} %get-tuple-element.64), channel_id=1, source_target_pairs={{0,4},{4,8},{8,12},{12,0},{1,5},{5,9},{9,13},{13,1},{2,6},{6,10},{... | collective-permute-start | bytes 417800 | tf_op jit(solution)/shard_map/ppermute | solution.py:23
  10.5 2.1 %collective-permute-start.2 = (f32[240,128]{1,0:T(8,128)S(1)}, f32[240,128]{1,0:T(8,128)S(1)}, u32[]{:S(2)}, u32[]{:S(2)}) collective-permute-start(f32[240,128]{1,0:T(8,128)S(1)} %get-tuple-element.63), channel_id=1, source_target_pairs={{0,12},{4,0},{8,4},{12,8},{1,13},{5,1},{9,5},{13,9},{2,14},{6,2},{... | collective-permute-start | bytes 368648 | tf_op jit(solution)/shard_map/ppermute | solution.py:23
  12.6 1.7 %shard_map.20 = (f32[17,2,40,128]{3,2,1,0:T(8,128)S(1)}, f32[17,3,2,40,128]{4,3,2,1,0:T(8,128)S(1)}, f32[17,2,64,256]{3,2,1,0:T(8,128)S(1)}, f32[32,64,256]{2,1,0:T(8,128)S(1)}) custom-call(f32[17,2,40,128]{3,2,1,0:T(8,128)S(1)} %get-tuple-element.55.gai, ...), custom_call_target="tpu_custom_call", output_to_operand_aliasing={{0}: (0, {}), {1}: (1, {})} | custom-call | flops 427819008 | bytes 4278190 | tf_op jit(solution)/shard_map/pallas_call | solution.py:623
  14.3 5.3 %collective-permute-done.2.rn = f32[240,128]{1,0:T(8,128)S(1)} collective-permute-done((f32[240,128]{1,0:T(8,128)S(1)}, f32[240,128]{1,0:T(8,128)S(1)}, u32[]{:S(2)}, u32[]{:S(2)}) %collective-permute-start.2) | collective-permute-done | bytes 122912 | tf_op jit(solution)/shard_map/ppermute | solution.py:23
  19.6 0.0 collective-permute-done.3.rp
  19.6 2.9 %shard_map.21 = (f32[17,2,40,128]{3,2,1,0:T(8,128)S(1)}, f32[17,3,2,40,128]{4,3,2,1,0:T(8,128)S(1)}, f32[10,2,2,24,128]{4,3,2,1,0:T(8,128)S(1)}, f32[6,2,2,16,12...) custom-call(f32[17,2,40,128]{3,2,1,0:T(8,128)S(1)} %get-tuple-elemen, ...), custom_call_target="tpu_custom_call", output_to_operand_aliasing={{0}: (0, {}), {1}: (1, {}), {2}: (2, {}), {3}: (3, {}), {4}... | custom-call | tf_op jit(solution)/shard_map/pallas_call | solution.py:623
  22.5 0.2 collective-permute-start.5
  22.6 1.6 %collective-permute-start.4 = (f32[144,128]{1,0:T(8,128)S(1)}, f32[144,128]{1,0:T(8,128)S(1)}, u32[]{:S(2)}, u32[]{:S(2)}) collective-permute-start(f32[144,128]{1,0:T(8,128)S(1)} %get-tuple-element.75), channel_id=1, source_target_pairs={{0,3},{1,0},{2,1},{3,2},{4,7},{5,4},{6,5},{7,6},{8,11},{9,8},{10,9... | collective-permute-start | bytes 221192 | tf_op jit(solution)/shard_map/ppermute | solution.py:23
  24.3 1.1 %shard_map.22.gbi = f32[17,3,2,40,128]{4,3,2,1,0:T(8,128)S(1)} custom-call(f32[2,2304,128]{2,1,0:T(8,128)S(1)} %get-tuple-element.71.u, f32[17,88,128]{2,1,0:T(8,128)S(1)} %get-tuple-element.72.zh, bf16[768,256]{1,0:T(8,128)(2,1)S(1)} %get-tuple-element.50.f1), custom_call_target="tpu_custom_call" | custom-call | flops 427819008 | bytes 4278190 | tf_op jit(solution)/shard_map/pallas_call | solution.py:623
  25.4 0.9 %collective-permute-done.4.rn = f32[144,128]{1,0:T(8,128)S(1)} collective-permute-done((f32[144,128]{1,0:T(8,128)S(1)}, f32[144,128]{1,0:T(8,128)S(1)}, u32[]{:S(2)}, u32[]{:S(2)}) %collective-permute-start.4) | collective-permute-done | bytes 73760 | tf_op jit(solution)/shard_map/ppermute | solution.py:23
  26.3 0.2 collective-permute-done.5.rp
  26.4 0.2 shard_map.23
  26.6 0.7 %collective-permute-start.7 = (f32[272,128]{1,0:T(8,128)S(1)}, f32[272,128]{1,0:T(8,128)S(1)}, u32[]{:S(2)}, u32[]{:S(2)}) collective-permute-start(f32[272,128]{1,0:T(8,128)S(1)} %get-tuple-element.87), channel_id=1, source_target_pairs={{0,4},{4,8},{8,12},{12,0},{1,5},{5,9},{9,13},{13,1},{2,6},{6,10},{... | collective-permute-start | bytes 417800 | tf_op jit(solution)/shard_map/ppermute | solution.py:23
  27.3 3.2 %collective-permute-start.6 = (f32[240,128]{1,0:T(8,128)S(1)}, f32[240,128]{1,0:T(8,128)S(1)}, u32[]{:S(2)}, u32[]{:S(2)}) collective-permute-start(f32[240,128]{1,0:T(8,128)S(1)} %get-tuple-element.86), channel_id=1, source_target_pairs={{0,12},{4,0},{8,4},{12,8},{1,13},{5,1},{9,5},{13,9},{2,14},{6,2},{... | collective-permute-start | bytes 368648 | tf_op jit(solution)/shard_map/ppermute | solution.py:23
  30.5 1.7 %shard_map.24 = (f32[17,2,40,128]{3,2,1,0:T(8,128)S(1)}, f32[17,3,2,40,128]{4,3,2,1,0:T(8,128)S(1)}, f32[17,2,64,256]{3,2,1,0:T(8,128)S(1)}) custom-call(f32[17,2,40,128]{3,2,1,0:T(8,128)S(1)} %get-tuple-element.77.qai, f32[17,3,2,40,128]{4,3,2,1,0:T(8,128)S(1)} %get-tuple-element.78.qbi, ...), custom_call_target="tpu_custom_call", output_to_operand_aliasing={{0}: (0, {}), {1}: (1, {})} | custom-call | flops 427819008 | bytes 4278190 | tf_op jit(solution)/shard_map/pallas_call | solution.py:623
  32.2 4.0 %collective-permute-done.6.rn = f32[240,128]{1,0:T(8,128)S(1)} collective-permute-done((f32[240,128]{1,0:T(8,128)S(1)}, f32[240,128]{1,0:T(8,128)S(1)}, u32[]{:S(2)}, u32[]{:S(2)}) %collective-permute-start.6) | collective-permute-done | bytes 122912 | tf_op jit(solution)/shard_map/ppermute | solution.py:23
  36.2 0.0 collective-permute-done.7.rp
  36.2 2.3 %shard_map.25 = (f32[17,2,40,128]{3,2,1,0:T(8,128)S(1)}, f32[17,3,2,40,128]{4,3,2,1,0:T(8,128)S(1)}, f32[10,2,2,24,128]{4,3,2,1,0:T(8,128)S(1)}, f32[6,2,2,16,12...) custom-call(f32[17,2,40,128]{3,2,1,0:T(8,128)S(1)} %get-tuple-elemen, ...), custom_call_target="tpu_custom_call", output_to_operand_aliasing={{0}: (0, {}), {1}: (1, {}), {2}: (2, {}), {3}: (3, {}), {4}... | custom-call | tf_op jit(solution)/shard_map/pallas_call | solution.py:623
Async XLA Ops:
  0.0 5.8 %copy-start = (s32[32,64,256]{2,1,0:T(8,128)S(1)}, s32[32,64,256]{2,1,0:T(8,128)}, u32[]{:S(2)}) copy-start(s32[32,64,256]{2,1,0:T(8,128)} %c.3) | copy-start | bytes 6291460
  3.3 5.2 %collective-permute-start.1 = (f32[168,128]{1,0:T(8,128)S(1)}, f32[168,128]{1,0:T(8,128)S(1)}, u32[]{:S(2)}, u32[]{:S(2)}) collective-permute-start(f32[168,128]{1,0:T(8,128)S(1)} %get-tuple-element.54), channel_id=1, source_target_pairs={{0,1},{1,2},{2,3},{3,0},{4,5},{5,6},{6,7},{7,4},{8,9},{9,10},{10,1... | collective-permute-start | bytes 258056 | tf_op jit(solution)/shard_map/ppermute | solution.py:23
  3.8 4.6 %collective-permute-start = (f32[144,128]{1,0:T(8,128)S(1)}, f32[144,128]{1,0:T(8,128)S(1)}, u32[]{:S(2)}, u32[]{:S(2)}) collective-permute-start(f32[144,128]{1,0:T(8,128)S(1)} %get-tuple-element.53), channel_id=1, source_target_pairs={{0,3},{1,0},{2,1},{3,2},{4,7},{5,4},{6,5},{7,6},{8,11},{9,8},{10,9... | collective-permute-start | bytes 221192 | tf_op jit(solution)/shard_map/ppermute | solution.py:23
  8.7 11.0 %collective-permute-start.3 = (f32[272,128]{1,0:T(8,128)S(1)}, f32[272,128]{1,0:T(8,128)S(1)}, u32[]{:S(2)}, u32[]{:S(2)}) collective-permute-start(f32[272,128]{1,0:T(8,128)S(1)} %get-tuple-element.64), channel_id=1, source_target_pairs={{0,4},{4,8},{8,12},{12,0},{1,5},{5,9},{9,13},{13,1},{2,6},{6,10},{... | collective-permute-start | bytes 417800 | tf_op jit(solution)/shard_map/ppermute | solution.py:23
  10.5 9.1 %collective-permute-start.2 = (f32[240,128]{1,0:T(8,128)S(1)}, f32[240,128]{1,0:T(8,128)S(1)}, u32[]{:S(2)}, u32[]{:S(2)}) collective-permute-start(f32[240,128]{1,0:T(8,128)S(1)} %get-tuple-element.63), channel_id=1, source_target_pairs={{0,12},{4,0},{8,4},{12,8},{1,13},{5,1},{9,5},{13,9},{2,14},{6,2},{... | collective-permute-start | bytes 368648 | tf_op jit(solution)/shard_map/ppermute | solution.py:23
  22.5 4.0 %collective-permute-start.5 = (f32[168,128]{1,0:T(8,128)S(1)}, f32[168,128]{1,0:T(8,128)S(1)}, u32[]{:S(2)}, u32[]{:S(2)}) collective-permute-start(f32[168,128]{1,0:T(8,128)S(1)} %get-tuple-element.76), channel_id=1, source_target_pairs={{0,1},{1,2},{2,3},{3,0},{4,5},{5,6},{6,7},{7,4},{8,9},{9,10},{10,1... | collective-permute-start | bytes 258056 | tf_op jit(solution)/shard_map/ppermute | solution.py:23
  22.6 3.6 %collective-permute-start.4 = (f32[144,128]{1,0:T(8,128)S(1)}, f32[144,128]{1,0:T(8,128)S(1)}, u32[]{:S(2)}, u32[]{:S(2)}) collective-permute-start(f32[144,128]{1,0:T(8,128)S(1)} %get-tuple-element.75), channel_id=1, source_target_pairs={{0,3},{1,0},{2,1},{3,2},{4,7},{5,4},{6,5},{7,6},{8,11},{9,8},{10,9... | collective-permute-start | bytes 221192 | tf_op jit(solution)/shard_map/ppermute | solution.py:23
  26.6 9.6 %collective-permute-start.7 = (f32[272,128]{1,0:T(8,128)S(1)}, f32[272,128]{1,0:T(8,128)S(1)}, u32[]{:S(2)}, u32[]{:S(2)}) collective-permute-start(f32[272,128]{1,0:T(8,128)S(1)} %get-tuple-element.87), channel_id=1, source_target_pairs={{0,4},{4,8},{8,12},{12,0},{1,5},{5,9},{9,13},{13,1},{2,6},{6,10},{... | collective-permute-start | bytes 417800 | tf_op jit(solution)/shard_map/ppermute | solution.py:23
  27.3 8.9 %collective-permute-start.6 = (f32[240,128]{1,0:T(8,128)S(1)}, f32[240,128]{1,0:T(8,128)S(1)}, u32[]{:S(2)}, u32[]{:S(2)}) collective-permute-start(f32[240,128]{1,0:T(8,128)S(1)} %get-tuple-element.86), channel_id=1, source_target_pairs={{0,12},{4,0},{8,4},{12,8},{1,13},{5,1},{9,5},{13,9},{2,14},{6,2},{... | collective-permute-start | bytes 368648 | tf_op jit(solution)/shard_map/ppermute | solution.py:23

commit v6 on v5

--- a/solution.py
+++ b/solution.py
@@ -71,15 +71,17 @@
                   (self.lx[2], 2, 2, p3, LANES)]
         self.zin = [y, p1, p2]
         self.zbase = [6, 5, 6]
-        self.zrows = [ceil8(2 * (p - 1) + 4 + b) for p, b in zip(self.py, self.zbase)]
+        self.zfill = [ceil8(2 * (p - 1) + 4 + b) for p, b in zip(self.py, self.zbase)]
+        self.zrows = [n + 8 for n in self.zfill]
+        self.vrows = [2 * ceil8(self.ly[1] // 2), 8 + 2 * ceil8((self.ly[0] + 1) // 2)]
         self.main = [y // 2, y // 4, y // 8]
         self.xp_pieces = [4, 4, 3]
         self.xn_pieces = [4, 6, 3]
         self.xp = self.x_rows(self.xp_pieces)
         self.xn = self.x_rows(self.xn_pieces)
         n1, n2, n3 = self.lx[0] * 4, self.lx[1] * 2, self.lx[2] * 2
-        self.yp = ceil8(n1 + 2 * n2 + 3 * n3)
-        self.yn = ceil8(n1 + 3 * n2 + 3 * n3)
+        self.yp = ceil8(n1 + 2 * n2 + 3 * n3) + 8
+        self.yn = ceil8(n1 + 3 * n2 + 3 * n3) + 8
 
 
     def x_rows(self, pieces):
@@ -167,13 +169,15 @@
         zh[s0 : s0 + n, 8 : 8 + y, :] = out[..., LANES:]
 
     def cols_1(s):
-        pad_z(z1, (s,), 8, 8 + y, sz.zrows[0])
+        pad_z(z1, (s,), 8, 8 + y, sz.zfill[0])
         y_analysis(z1.at[s], sz.zbase[0], sz.py[0], g.at(0, s, 0, 0), g.at(0, s, 0, 2))
 
     each(0, l1, cols_1)
 
     def column(h, j, col):
-        return u[h, pl.ds(j * y + col, l1, stride=2 * y), :]
+        last = (2 * (l1 - 1) + j) * y + col
+        return jnp.concatenate(
+            [u[h, pl.ds(j * y + col, l1 - 1, stride=2 * y), :], u[h, last : last + 1, :]], axis=0)
 
     edges = []
     for c0, c1, w0, w1 in ((0, 1, R3, -1.0), (y - 2, y - 1, 1.0, R3)):
@@ -202,7 +206,7 @@
         z[:, :, 8 : 8 + p_in, :] = out.reshape(count, 2, p_in, LANES)
         for s in range(count):
             for xb in range(2):
-                pad_z(z, (s, xb), 8, 8 + p_in, sz.zrows[level])
+                pad_z(z, (s, xb), 8, 8 + p_in, sz.zfill[level])
                 y_analysis(z.at[s, xb], sz.zbase[level], p_out, g.at(level, s, xb, 0), g.at(level, s, xb, 1))
     pack_y(sz, g, mp, mn)
 
@@ -229,10 +233,10 @@
         zl[8 : 8 + y] = zh[s, 8 : 8 + y, :]
         y_analysis(zl, sz.zbase[0], sz.py[0], gb.at[s, 0, 0], gb.at[s, 0, 1])
         for tb in range(2):
-            pad_z(z1, (s, tb), 8, 8 + y, sz.zrows[0])
+            pad_z(z1, (s, tb), 8, 8 + y, sz.zfill[0])
             y_analysis(z1.at[s, tb], sz.zbase[0], sz.py[0], gb.at[s, 1 + tb, 0], gb.at[s, 1 + tb, 1])
 
-    pad_z(zl, (), 8, 8 + y, sz.zrows[0])
+    pad_z(zl, (), 8, 8 + y, sz.zfill[0])
     each(0, l1, cols_1)
 
 
@@ -247,14 +251,22 @@
                 value = item[0][lo:hi]
                 if level == 2:
                     value = jnp.where(lower, value, pltpu.roll(item[1][lo:hi], LANES // 2, 1))
-                ref[at : at + hi - lo] = value
-
+                if lo == 0:
+                    ref[at : at + hi] = value
+                else:
+                    tails[ref is mn].append(value)
+
+    tails = [], []
     put(mp, sz.xp_pieces, 0, [[g.at(0, 0, 1, q)] for q in range(4)])
     put(mn, sz.xn_pieces, 0, [[g.at(0, l1 - 1, 0, q)] for q in range(4)])
     put(mp, sz.xp_pieces, 1, [[g.at(1, s, 1, q)] for s in (0, 1) for q in (0, 1)])
     put(mn, sz.xn_pieces, 1, [[g.at(1, s, b, q)] for s, b in ((l2 - 2, 0), (l2 - 2, 1), (l2 - 1, 0)) for q in (0, 1)])
     put(mp, sz.xp_pieces, 2, [[g.at(2, s, b, q) for q in (0, 1)] for s, b in ((0, 1), (1, 0), (1, 1))])
     put(mn, sz.xn_pieces, 2, [[g.at(2, s, b, q) for q in (0, 1)] for s, b in ((l3 - 2, 0), (l3 - 2, 1), (l3 - 1, 0))])
+    for ref, tail, pieces in ((mp, tails[0], sz.xp_pieces), (mn, tails[1], sz.xn_pieces)):
+        at = sz.x_offsets(pieces)[0][0][1]
+        rest = ref.shape[0] - at - sum(v.shape[0] for v in tail)
+        ref[at:] = jnp.concatenate(tail + ([jnp.zeros((rest, LANES), jnp.float32)] if rest else []), axis=0)
 
 
 def fix_x(sz, g, rn, rp):
@@ -262,8 +274,12 @@
     lower = lane_below(LANES // 2, (1, LANES))
 
     def take(ref, pieces, level, lo, hi):
-        part = 0 if lo == 0 else 1
-        return [ref[at[part] : at[part] + hi - lo] for at in sz.x_offsets(pieces)[level]]
+        offsets = sz.x_offsets(pieces)
+        if lo == 0:
+            return [ref[at : at + hi] for at, _ in offsets[level]]
+        first = offsets[0][0][1]
+        tail = ref[first:]
+        return [tail[at - first : at - first + hi - lo] for _, at in offsets[level]]
 
     def halves(value):
         return [jnp.where(lower, v, 0.0) for v in (value, pltpu.roll(value, LANES // 2, 1))]
@@ -353,8 +369,8 @@
         for s in range(sz.lx[level]):
             for xb in range(2):
 
-                def add(q, row, value):
-                    g.at(level, s, xb, q)[row : row + 1] += value
+                def add(q, row, first, second):
+                    g.at(level, s, xb, q)[row : row + 2] += jnp.concatenate([first, second], axis=0)
 
                 h0, h1 = rn[at_n : at_n + 1], rn[at_n + 1 : at_n + 2]
                 if level == 1:
@@ -363,15 +379,11 @@
                 else:
                     l1 = rn[at_n + 2 : at_n + 3]
                     at_n += 3
-                add(0, k - 2, -RHO * h0)
-                add(1, k - 2, h0)
-                add(0, k - 1, l1)
-                add(1, k - 1, h1)
+                add(0, k - 2, -RHO * h0, l1)
+                add(1, k - 2, h0, h1)
                 w0, w2, w1 = (rp[at_p + i : at_p + i + 1] for i in range(3))
-                add(0, 0, w0)
-                add(1, 0, w1)
-                add(0, 1, w2)
-                add(1, 1, RHO * w2)
+                add(0, 0, w0, w2)
+                add(1, 0, w1, RHO * w2)
                 at_p += 3
 
 
@@ -382,7 +394,7 @@
 def y_synthesis(low, high, count, t_ref, v_ref, index, start):
     a = low + RHO * high
     b = RHO * low - high
-    t_ref[...] = a
+    t_ref[0 : a.shape[0]] = a
     a = t_ref[1 : 1 + count]
     b = b[:count]
     v_ref[index + (pl.ds(start, count, stride=2), slice(None))] = a - R3 * b
@@ -396,7 +408,7 @@
 def level_1_columns(sz, details, s, xb, tb, coarse, ta, v1, index):
     low = details(0, s, xb, tb, None) if coarse is None else coarse
     high = details(0, s, xb, 2 + tb, None)
-    y_synthesis(low, high, sz.y // 2, ta.at[s, xb * 2 + tb, 0 : sz.py[0]], v1, index, 0)
+    y_synthesis(low, high, sz.y // 2, ta.at[s, xb * 2 + tb], v1, index, 0)
 
 
 def times_back(sz, v_low, v_high, i1):
@@ -429,8 +441,8 @@
         for xb in range(2):
             low = details(2, s, xb, 0, third if xb == 0 else None)
             high = details(2, s, xb, 1, None)
-            y_synthesis(low, high, sz.ly[1] // 2, ta.at[1, s, xb, 0:p3], v3, (s, xb), 0)
-    b3[...] = dot_parts_narrow(v3[...].reshape(l3 * 2 * p2, LANES), i3).reshape(l3, 2, p2, LANES)
+            y_synthesis(low, high, sz.ly[1] // 2, ta.at[1, s, xb], v3, (s, xb), 0)
+    b3[...] = dot_parts_narrow(v3[:, :, :p2].reshape(l3 * 2 * p2, LANES), i3).reshape(l3, 2, p2, LANES)
 
     second = lane_below(t // 4, (p2, LANES))
     for p in range(l2 // 2):
@@ -441,7 +453,7 @@
                 if xb == 0:
                     low = jnp.where(second, coarse, low)
                 high = details(1, s, xb, 1, None)
-                y_synthesis(low, high, (sz.ly[0] + 1) // 2, ta.at[0, s, xb, 0:p2], v2, (s, xb), 7)
+                y_synthesis(low, high, (sz.ly[0] + 1) // 2, ta.at[0, s, xb], v2, (s, xb), 7)
     b2[...] = dot_parts_narrow(v2[:, :, 8 : 8 + p1, :].reshape(l2 * 2 * p1, LANES), i2).reshape(l2, 2, p1, LANES)
 
     def coarse_rows(p):
@@ -451,7 +463,7 @@
     half = jnp.concatenate([i1[0:n], i1[t : t + n], i1[2 * t : 2 * t + n]], axis=0)
 
     def coarse_columns(s, low):
-        y_synthesis(low, 0.0, y // 2, ta1.at[s, 0, 0:p1], v1, (s,), 0)
+        y_synthesis(low, 0.0, y // 2, ta1.at[s, 0], v1, (s,), 0)
 
     def pair_1(p):
         even, odd = coarse_rows(p)
@@ -648,7 +660,7 @@
              (l3, 2, p2, LANES), (l3, 2, sz.zrows[2], LANES))
     fine = f32((sz.zrows[0], LANES), (2, l1, y, LANES), (l1, 2, sz.zrows[0], LANES))
     ta1 = f32((l1, 4, p1 + 8, LANES))
-    bw = ta1 + f32((2, l2, 2, p2 + 8, LANES), (l3, 2, p2, LANES), (l3, 2, p2, LANES), (l2, 2, p1 + 8, LANES),
+    bw = ta1 + f32((2, l2, 2, p2 + 8, LANES), (l3, 2, sz.vrows[0], LANES), (l3, 2, p2, LANES), (l2, 2, sz.vrows[1], LANES),
                    (l2, 2, p1, LANES), (l1, y, LANES), (l1, y, t), (2, 2, 2, y, LANES))
     to_prev, to_next = (sz.xp, LANES), (sz.xn, LANES)
     messages = [(sz.yp, LANES), (sz.yn, LANES)]

time: 38.8 us -> 39 us (level)
  transfers between devices with their start and end apart: 8 -> 8, of which waited for: 5 -> 5; matrix products, arithmetic and copies ran while one was open for 0% -> 0% of each run, Pallas kernels for 15% -> 16%
where the time goes in v6:
time: 39 us; the launch traced here: 38.8 us
  Pallas kernels  14.9 us (38%)
  starting transfers between devices  12.1 us (31%)
  waiting for transfers between devices  11.6 us (30%)
    pallas_call x9, Pallas kernels, call(): pl.pallas_call(functools.partial(kernel, sz), out_shape=outs, in_specs=sp...  14.9 us
    ppermute x8, starting transfers between devices, shifted(): return lax.ppermute(x, axis, [(i, (i + by) % count) for i in range(count)])  12.1 us
    ppermute x8, waiting for transfers between devices, shifted(): return lax.ppermute(x, axis, [(i, (i + by) % count) for i in range(count)])  11.6 us
  transfers between devices with their start and end apart: 8, of which 5 were waited for; matrix products, arithmetic and copies ran while one was open for 0% of the time, Pallas kernels for 16%

profile of v6, /device:TPU:0, one launch (start us, length us, event | category | flops | bytes accessed | tf_op | source)
XLA Modules:
  0.0 38.8 jit_solution(11466376822212067383)
XLA Ops:
  0.0 0.0 copy-start
  0.0 3.3 %shard_map.17 = (f32[17,2,40,128]{3,2,1,0:T(8,128)S(1)}, f32[10,2,2,24,128]{4,3,2,1,0:T(8,128)S(1)}, f32[6,2,2,16,128]{4,3,2,1,0:T(8,128)S(1)}, f32[152,128]{1,0...) custom-call(s32[32,64,256]{2,1,0:T(8,128)} %c.3), custom_call_target="tpu_custom_call" | custom-call | tf_op jit(solution)/shard_map/pallas_call | solution.py:635
  3.3 0.5 %collective-permute-start.1 = (f32[176,128]{1,0:T(8,128)S(1)}, f32[176,128]{1,0:T(8,128)S(1)}, u32[]{:S(2)}, u32[]{:S(2)}) collective-permute-start(f32[176,128]{1,0:T(8,128)S(1)} %get-tuple-element.54), channel_id=1, source_target_pairs={{0,1},{1,2},{2,3},{3,0},{4,5},{5,6},{6,7},{7,4},{8,9},{9,10},{10,1... | collective-permute-start | bytes 270344 | tf_op jit(solution)/shard_map/ppermute | solution.py:23
  3.8 2.0 %collective-permute-start = (f32[152,128]{1,0:T(8,128)S(1)}, f32[152,128]{1,0:T(8,128)S(1)}, u32[]{:S(2)}, u32[]{:S(2)}) collective-permute-start(f32[152,128]{1,0:T(8,128)S(1)} %get-tuple-element.53), channel_id=1, source_target_pairs={{0,3},{1,0},{2,1},{3,2},{4,7},{5,4},{6,5},{7,6},{8,11},{9,8},{10,9... | collective-permute-start | bytes 233480 | tf_op jit(solution)/shard_map/ppermute | solution.py:23
  5.8 0.0 copy-done
  5.8 1.5 %shard_map.18.gbi = f32[17,3,2,40,128]{4,3,2,1,0:T(8,128)S(1)} custom-call(s32[32,64,256]{2,1,0:T(8,128)S(1)} %copy-done, f32[17,96,128]{2,1,0:T(8,128)S(1)} %get-tuple-element.49.zh, bf16[768,256]{1,0:T(8,128)(2,1)S(1)} %get-tuple-element.50.f1), custom_call_target="tpu_custom_call" | custom-call | flops 427819008 | bytes 4278190 | tf_op jit(solution)/shard_map/pallas_call | solution.py:635
  7.3 1.3 %collective-permute-done.rn = f32[152,128]{1,0:T(8,128)S(1)} collective-permute-done((f32[152,128]{1,0:T(8,128)S(1)}, f32[152,128]{1,0:T(8,128)S(1)}, u32[]{:S(2)}, u32[]{:S(2)}) %collective-permute-start) | collective-permute-done | bytes 77856 | tf_op jit(solution)/shard_map/ppermute | solution.py:23
  8.6 0.0 collective-permute-done.1.rp
  8.6 0.2 shard_map.19
  8.7 1.8 %collective-permute-start.3 = (f32[272,128]{1,0:T(8,128)S(1)}, f32[272,128]{1,0:T(8,128)S(1)}, u32[]{:S(2)}, u32[]{:S(2)}) collective-permute-start(f32[272,128]{1,0:T(8,128)S(1)} %get-tuple-element.64), channel_id=1, source_target_pairs={{0,4},{4,8},{8,12},{12,0},{1,5},{5,9},{9,13},{13,1},{2,6},{6,10},{... | collective-permute-start | bytes 417800 | tf_op jit(solution)/shard_map/ppermute | solution.py:23
  10.6 2.1 %collective-permute-start.2 = (f32[240,128]{1,0:T(8,128)S(1)}, f32[240,128]{1,0:T(8,128)S(1)}, u32[]{:S(2)}, u32[]{:S(2)}) collective-permute-start(f32[240,128]{1,0:T(8,128)S(1)} %get-tuple-element.63), channel_id=1, source_target_pairs={{0,12},{4,0},{8,4},{12,8},{1,13},{5,1},{9,5},{13,9},{2,14},{6,2},{... | collective-permute-start | bytes 368648 | tf_op jit(solution)/shard_map/ppermute | solution.py:23
  12.7 1.7 %shard_map.20 = (f32[17,2,40,128]{3,2,1,0:T(8,128)S(1)}, f32[17,3,2,40,128]{4,3,2,1,0:T(8,128)S(1)}, f32[17,2,64,256]{3,2,1,0:T(8,128)S(1)}, f32[32,64,256]{2,1,0:T(8,128)S(1)}) custom-call(f32[17,2,40,128]{3,2,1,0:T(8,128)S(1)} %get-tuple-element.55.gai, ...), custom_call_target="tpu_custom_call", output_to_operand_aliasing={{0}: (0, {}), {1}: (1, {})} | custom-call | flops 427819008 | bytes 4278190 | tf_op jit(solution)/shard_map/pallas_call | solution.py:635
  14.4 5.2 %collective-permute-done.2.rn = f32[240,128]{1,0:T(8,128)S(1)} collective-permute-done((f32[240,128]{1,0:T(8,128)S(1)}, f32[240,128]{1,0:T(8,128)S(1)}, u32[]{:S(2)}, u32[]{:S(2)}) %collective-permute-start.2) | collective-permute-done | bytes 122912 | tf_op jit(solution)/shard_map/ppermute | solution.py:23
  19.7 0.0 collective-permute-done.3.rp
  19.7 2.9 %shard_map.21 = (f32[17,2,40,128]{3,2,1,0:T(8,128)S(1)}, f32[17,3,2,40,128]{4,3,2,1,0:T(8,128)S(1)}, f32[10,2,2,24,128]{4,3,2,1,0:T(8,128)S(1)}, f32[6,2,2,16,12...) custom-call(f32[17,2,40,128]{3,2,1,0:T(8,128)S(1)} %get-tuple-elemen, ...), custom_call_target="tpu_custom_call", output_to_operand_aliasing={{0}: (0, {}), {1}: (1, {}), {2}: (2, {}), {3}: (3, {}), {4}... | custom-call | tf_op jit(solution)/shard_map/pallas_call | solution.py:635
  22.5 0.2 collective-permute-start.5
  22.7 1.6 %collective-permute-start.4 = (f32[152,128]{1,0:T(8,128)S(1)}, f32[152,128]{1,0:T(8,128)S(1)}, u32[]{:S(2)}, u32[]{:S(2)}) collective-permute-start(f32[152,128]{1,0:T(8,128)S(1)} %get-tuple-element.75), channel_id=1, source_target_pairs={{0,3},{1,0},{2,1},{3,2},{4,7},{5,4},{6,5},{7,6},{8,11},{9,8},{10,9... | collective-permute-start | bytes 233480 | tf_op jit(solution)/shard_map/ppermute | solution.py:23
  24.3 1.1 %shard_map.22.gbi = f32[17,3,2,40,128]{4,3,2,1,0:T(8,128)S(1)} custom-call(f32[2,2304,128]{2,1,0:T(8,128)S(1)} %get-tuple-element.71.u, f32[17,96,128]{2,1,0:T(8,128)S(1)} %get-tuple-element.72.zh, bf16[768,256]{1,0:T(8,128)(2,1)S(1)} %get-tuple-element.50.f1), custom_call_target="tpu_custom_call" | custom-call | flops 427819008 | bytes 4278190 | tf_op jit(solution)/shard_map/pallas_call | solution.py:635
  25.4 0.9 %collective-permute-done.4.rn = f32[152,128]{1,0:T(8,128)S(1)} collective-permute-done((f32[152,128]{1,0:T(8,128)S(1)}, f32[152,128]{1,0:T(8,128)S(1)}, u32[]{:S(2)}, u32[]{:S(2)}) %collective-permute-start.4) | collective-permute-done | bytes 77856 | tf_op jit(solution)/shard_map/ppermute | solution.py:23
  26.3 0.2 collective-permute-done.5.rp
  26.5 0.2 shard_map.23
  26.7 0.7 %collective-permute-start.7 = (f32[272,128]{1,0:T(8,128)S(1)}, f32[272,128]{1,0:T(8,128)S(1)}, u32[]{:S(2)}, u32[]{:S(2)}) collective-permute-start(f32[272,128]{1,0:T(8,128)S(1)} %get-tuple-element.87), channel_id=1, source_target_pairs={{0,4},{4,8},{8,12},{12,0},{1,5},{5,9},{9,13},{13,1},{2,6},{6,10},{... | collective-permute-start | bytes 417800 | tf_op jit(solution)/shard_map/ppermute | solution.py:23
  27.4 3.1 %collective-permute-start.6 = (f32[240,128]{1,0:T(8,128)S(1)}, f32[240,128]{1,0:T(8,128)S(1)}, u32[]{:S(2)}, u32[]{:S(2)}) collective-permute-start(f32[240,128]{1,0:T(8,128)S(1)} %get-tuple-element.86), channel_id=1, source_target_pairs={{0,12},{4,0},{8,4},{12,8},{1,13},{5,1},{9,5},{13,9},{2,14},{6,2},{... | collective-permute-start | bytes 368648 | tf_op jit(solution)/shard_map/ppermute | solution.py:23
  30.6 1.7 %shard_map.24 = (f32[17,2,40,128]{3,2,1,0:T(8,128)S(1)}, f32[17,3,2,40,128]{4,3,2,1,0:T(8,128)S(1)}, f32[17,2,64,256]{3,2,1,0:T(8,128)S(1)}) custom-call(f32[17,2,40,128]{3,2,1,0:T(8,128)S(1)} %get-tuple-element.77.qai, f32[17,3,2,40,128]{4,3,2,1,0:T(8,128)S(1)} %get-tuple-element.78.qbi, ...), custom_call_target="tpu_custom_call", output_to_operand_aliasing={{0}: (0, {}), {1}: (1, {})} | custom-call | flops 427819008 | bytes 4278190 | tf_op jit(solution)/shard_map/pallas_call | solution.py:635
  32.3 4.0 %collective-permute-done.6.rn = f32[240,128]{1,0:T(8,128)S(1)} collective-permute-done((f32[240,128]{1,0:T(8,128)S(1)}, f32[240,128]{1,0:T(8,128)S(1)}, u32[]{:S(2)}, u32[]{:S(2)}) %collective-permute-start.6) | collective-permute-done | bytes 122912 | tf_op jit(solution)/shard_map/ppermute | solution.py:23
  36.3 0.0 collective-permute-done.7.rp
  36.3 2.4 %shard_map.25 = (f32[17,2,40,128]{3,2,1,0:T(8,128)S(1)}, f32[17,3,2,40,128]{4,3,2,1,0:T(8,128)S(1)}, f32[10,2,2,24,128]{4,3,2,1,0:T(8,128)S(1)}, f32[6,2,2,16,12...) custom-call(f32[17,2,40,128]{3,2,1,0:T(8,128)S(1)} %get-tuple-elemen, ...), custom_call_target="tpu_custom_call", output_to_operand_aliasing={{0}: (0, {}), {1}: (1, {}), {2}: (2, {}), {3}: (3, {}), {4}... | custom-call | tf_op jit(solution)/shard_map/pallas_call | solution.py:635
Async XLA Ops:
  0.0 5.8 %copy-start = (s32[32,64,256]{2,1,0:T(8,128)S(1)}, s32[32,64,256]{2,1,0:T(8,128)}, u32[]{:S(2)}) copy-start(s32[32,64,256]{2,1,0:T(8,128)} %c.3) | copy-start | bytes 6291460
  3.3 5.2 %collective-permute-start.1 = (f32[176,128]{1,0:T(8,128)S(1)}, f32[176,128]{1,0:T(8,128)S(1)}, u32[]{:S(2)}, u32[]{:S(2)}) collective-permute-start(f32[176,128]{1,0:T(8,128)S(1)} %get-tuple-element.54), channel_id=1, source_target_pairs={{0,1},{1,2},{2,3},{3,0},{4,5},{5,6},{6,7},{7,4},{8,9},{9,10},{10,1... | collective-permute-start | bytes 270344 | tf_op jit(solution)/shard_map/ppermute | solution.py:23
  3.8 4.7 %collective-permute-start = (f32[152,128]{1,0:T(8,128)S(1)}, f32[152,128]{1,0:T(8,128)S(1)}, u32[]{:S(2)}, u32[]{:S(2)}) collective-permute-start(f32[152,128]{1,0:T(8,128)S(1)} %get-tuple-element.53), channel_id=1, source_target_pairs={{0,3},{1,0},{2,1},{3,2},{4,7},{5,4},{6,5},{7,6},{8,11},{9,8},{10,9... | collective-permute-start | bytes 233480 | tf_op jit(solution)/shard_map/ppermute | solution.py:23
  8.7 10.9 %collective-permute-start.3 = (f32[272,128]{1,0:T(8,128)S(1)}, f32[272,128]{1,0:T(8,128)S(1)}, u32[]{:S(2)}, u32[]{:S(2)}) collective-permute-start(f32[272,128]{1,0:T(8,128)S(1)} %get-tuple-element.64), channel_id=1, source_target_pairs={{0,4},{4,8},{8,12},{12,0},{1,5},{5,9},{9,13},{13,1},{2,6},{6,10},{... | collective-permute-start | bytes 417800 | tf_op jit(solution)/shard_map/ppermute | solution.py:23
  10.6 9.1 %collective-permute-start.2 = (f32[240,128]{1,0:T(8,128)S(1)}, f32[240,128]{1,0:T(8,128)S(1)}, u32[]{:S(2)}, u32[]{:S(2)}) collective-permute-start(f32[240,128]{1,0:T(8,128)S(1)} %get-tuple-element.63), channel_id=1, source_target_pairs={{0,12},{4,0},{8,4},{12,8},{1,13},{5,1},{9,5},{13,9},{2,14},{6,2},{... | collective-permute-start | bytes 368648 | tf_op jit(solution)/shard_map/ppermute | solution.py:23
  22.5 4.0 %collective-permute-start.5 = (f32[176,128]{1,0:T(8,128)S(1)}, f32[176,128]{1,0:T(8,128)S(1)}, u32[]{:S(2)}, u32[]{:S(2)}) collective-permute-start(f32[176,128]{1,0:T(8,128)S(1)} %get-tuple-element.76), channel_id=1, source_target_pairs={{0,1},{1,2},{2,3},{3,0},{4,5},{5,6},{6,7},{7,4},{8,9},{9,10},{10,1... | collective-permute-start | bytes 270344 | tf_op jit(solution)/shard_map/ppermute | solution.py:23
  22.7 3.7 %collective-permute-start.4 = (f32[152,128]{1,0:T(8,128)S(1)}, f32[152,128]{1,0:T(8,128)S(1)}, u32[]{:S(2)}, u32[]{:S(2)}) collective-permute-start(f32[152,128]{1,0:T(8,128)S(1)} %get-tuple-element.75), channel_id=1, source_target_pairs={{0,3},{1,0},{2,1},{3,2},{4,7},{5,4},{6,5},{7,6},{8,11},{9,8},{10,9... | collective-permute-start | bytes 233480 | tf_op jit(solution)/shard_map/ppermute | solution.py:23
  26.7 9.6 %collective-permute-start.7 = (f32[272,128]{1,0:T(8,128)S(1)}, f32[272,128]{1,0:T(8,128)S(1)}, u32[]{:S(2)}, u32[]{:S(2)}) collective-permute-start(f32[272,128]{1,0:T(8,128)S(1)} %get-tuple-element.87), channel_id=1, source_target_pairs={{0,4},{4,8},{8,12},{12,0},{1,5},{5,9},{9,13},{13,1},{2,6},{6,10},{... | collective-permute-start | bytes 417800 | tf_op jit(solution)/shard_map/ppermute | solution.py:23
  27.4 8.9 %collective-permute-start.6 = (f32[240,128]{1,0:T(8,128)S(1)}, f32[240,128]{1,0:T(8,128)S(1)}, u32[]{:S(2)}, u32[]{:S(2)}) collective-permute-start(f32[240,128]{1,0:T(8,128)S(1)} %get-tuple-element.86), channel_id=1, source_target_pairs={{0,12},{4,0},{8,4},{12,8},{1,13},{5,1},{9,5},{13,9},{2,14},{6,2},{... | collective-permute-start | bytes 368648 | tf_op jit(solution)/shard_map/ppermute | solution.py:23

commit v7 on v6

--- a/solution.py
+++ b/solution.py
@@ -150,7 +150,7 @@
         z[index + (slice(hi, total), slice(None))] = jnp.zeros((total - hi, LANES), jnp.float32)
 
 
-def forward_coarse(sz, u, f1, f2, f3, g, zh, mp, mn, a1, z1, a2, z2, a3, z3):
+def forward_coarse(sz, step, u, f1, f2, f3, g, zh, mp, mn, a1, z1, a2, z2, a3, z3):
     x, y, t = sz.x, sz.y, sz.t
     l1 = sz.lx[0]
 
@@ -160,7 +160,6 @@
 
     each(0, l1, rows_x)
 
-    step = 9
     for s0 in range(0, l1, step):
         n = min(step, l1 - s0)
         out = dot_parts(jnp.concatenate([a1[0, s0 : s0 + n], a1[1, s0 : s0 + n]], axis=-1).reshape(n * y, t), f1)
@@ -535,7 +534,7 @@
             copies[x // step].wait()
         value, weight = scaled_and_weight(c[x])
         store_u(sz, u, x, weight * value)
-    forward_coarse(sz, u, f1, f2, f3, Bands(ga, None, g2, g3), zh, mp, mn, *scratch)
+    forward_coarse(sz, sz.lx[0], u, f1, f2, f3, Bands(ga, None, g2, g3), zh, mp, mn, *scratch)
 
 
 def forward_fine_first_kernel(sz, c, zh, f1, gb, u, zl, a1, z1):
@@ -599,7 +598,7 @@
         store_u(sz, u, 2 * p + 1, w_ref[2 * p + 1] * odd)
 
     inverse(sz, first_details(g), emit, lambda x0, n: None, 2, ba, i1, i2, i3, ta1, ta, v3, b3, v2, b2, v1, b1, ve)
-    forward_coarse(sz, u, f1, f2, f3, Bands(qa, None, q2, q3), zh, mp, mn, *scratch)
+    forward_coarse(sz, 9, u, f1, f2, f3, Bands(qa, None, q2, q3), zh, mp, mn, *scratch)
 
 
 def last_kernel(sz, qai, qbi, q2i, q3i, bai, rn, rp, ga, gb, g2, g3, i1, i2, i3,

time: 39 us -> 38.8 us (level)
  no operation moved by 1% of the time
where the time goes in v7:
time: 38.8 us; the launch traced here: 38.7 us
  Pallas kernels  14.7 us (38%)
  starting transfers between devices  12.1 us (31%)
  waiting for transfers between devices  11.6 us (30%)
    pallas_call x9, Pallas kernels, call(): pl.pallas_call(functools.partial(kernel, sz), out_shape=outs, in_specs=sp...  14.7 us
    ppermute x8, starting transfers between devices, shifted(): return lax.ppermute(x, axis, [(i, (i + by) % count) for i in range(count)])  12.1 us
    ppermute x8, waiting for transfers between devices, shifted(): return lax.ppermute(x, axis, [(i, (i + by) % count) for i in range(count)])  11.6 us
  transfers between devices with their start and end apart: 8, of which 5 were waited for; matrix products, arithmetic and copies ran while one was open for 0% of the time, Pallas kernels for 16%

profile of v7, /device:TPU:0, one launch (start us, length us, event | category | flops | bytes accessed | tf_op | source)
XLA Modules:
  0.0 38.7 jit_solution(14405448019556601527)
XLA Ops:
  0.0 0.0 copy-start
  0.0 3.2 %shard_map.17 = (f32[17,2,40,128]{3,2,1,0:T(8,128)S(1)}, f32[10,2,2,24,128]{4,3,2,1,0:T(8,128)S(1)}, f32[6,2,2,16,128]{4,3,2,1,0:T(8,128)S(1)}, f32[152,128]{1,0...) custom-call(s32[32,64,256]{2,1,0:T(8,128)} %c.3), custom_call_target="tpu_custom_call" | custom-call | tf_op jit(solution)/shard_map/pallas_call | solution.py:634
  3.2 0.5 %collective-permute-start.1 = (f32[176,128]{1,0:T(8,128)S(1)}, f32[176,128]{1,0:T(8,128)S(1)}, u32[]{:S(2)}, u32[]{:S(2)}) collective-permute-start(f32[176,128]{1,0:T(8,128)S(1)} %get-tuple-element.54), channel_id=1, source_target_pairs={{0,1},{1,2},{2,3},{3,0},{4,5},{5,6},{6,7},{7,4},{8,9},{9,10},{10,1... | collective-permute-start | bytes 270344 | tf_op jit(solution)/shard_map/ppermute | solution.py:23
  3.7 2.0 %collective-permute-start = (f32[152,128]{1,0:T(8,128)S(1)}, f32[152,128]{1,0:T(8,128)S(1)}, u32[]{:S(2)}, u32[]{:S(2)}) collective-permute-start(f32[152,128]{1,0:T(8,128)S(1)} %get-tuple-element.53), channel_id=1, source_target_pairs={{0,3},{1,0},{2,1},{3,2},{4,7},{5,4},{6,5},{7,6},{8,11},{9,8},{10,9... | collective-permute-start | bytes 233480 | tf_op jit(solution)/shard_map/ppermute | solution.py:23
  5.7 0.0 copy-done
  5.7 1.5 %shard_map.18.gbi = f32[17,3,2,40,128]{4,3,2,1,0:T(8,128)S(1)} custom-call(s32[32,64,256]{2,1,0:T(8,128)S(1)} %copy-done, f32[17,96,128]{2,1,0:T(8,128)S(1)} %get-tuple-element.49.zh, bf16[768,256]{1,0:T(8,128)(2,1)S(1)} %get-tuple-element.50.f1), custom_call_target="tpu_custom_call" | custom-call | flops 427819008 | bytes 4278190 | tf_op jit(solution)/shard_map/pallas_call | solution.py:634
  7.2 1.3 %collective-permute-done.rn = f32[152,128]{1,0:T(8,128)S(1)} collective-permute-done((f32[152,128]{1,0:T(8,128)S(1)}, f32[152,128]{1,0:T(8,128)S(1)}, u32[]{:S(2)}, u32[]{:S(2)}) %collective-permute-start) | collective-permute-done | bytes 77856 | tf_op jit(solution)/shard_map/ppermute | solution.py:23
  8.4 0.0 collective-permute-done.1.rp
  8.4 0.2 shard_map.19
  8.6 1.8 %collective-permute-start.3 = (f32[272,128]{1,0:T(8,128)S(1)}, f32[272,128]{1,0:T(8,128)S(1)}, u32[]{:S(2)}, u32[]{:S(2)}) collective-permute-start(f32[272,128]{1,0:T(8,128)S(1)} %get-tuple-element.64), channel_id=1, source_target_pairs={{0,4},{4,8},{8,12},{12,0},{1,5},{5,9},{9,13},{13,1},{2,6},{6,10},{... | collective-permute-start | bytes 417800 | tf_op jit(solution)/shard_map/ppermute | solution.py:23
  10.4 2.1 %collective-permute-start.2 = (f32[240,128]{1,0:T(8,128)S(1)}, f32[240,128]{1,0:T(8,128)S(1)}, u32[]{:S(2)}, u32[]{:S(2)}) collective-permute-start(f32[240,128]{1,0:T(8,128)S(1)} %get-tuple-element.63), channel_id=1, source_target_pairs={{0,12},{4,0},{8,4},{12,8},{1,13},{5,1},{9,5},{13,9},{2,14},{6,2},{... | collective-permute-start | bytes 368648 | tf_op jit(solution)/shard_map/ppermute | solution.py:23
  12.5 1.7 %shard_map.20 = (f32[17,2,40,128]{3,2,1,0:T(8,128)S(1)}, f32[17,3,2,40,128]{4,3,2,1,0:T(8,128)S(1)}, f32[17,2,64,256]{3,2,1,0:T(8,128)S(1)}, f32[32,64,256]{2,1,0:T(8,128)S(1)}) custom-call(f32[17,2,40,128]{3,2,1,0:T(8,128)S(1)} %get-tuple-element.55.gai, ...), custom_call_target="tpu_custom_call", output_to_operand_aliasing={{0}: (0, {}), {1}: (1, {})} | custom-call | flops 427819008 | bytes 4278190 | tf_op jit(solution)/shard_map/pallas_call | solution.py:634
  14.3 5.2 %collective-permute-done.2.rn = f32[240,128]{1,0:T(8,128)S(1)} collective-permute-done((f32[240,128]{1,0:T(8,128)S(1)}, f32[240,128]{1,0:T(8,128)S(1)}, u32[]{:S(2)}, u32[]{:S(2)}) %collective-permute-start.2) | collective-permute-done | bytes 122912 | tf_op jit(solution)/shard_map/ppermute | solution.py:23
  19.5 0.0 collective-permute-done.3.rp
  19.5 2.9 %shard_map.21 = (f32[17,2,40,128]{3,2,1,0:T(8,128)S(1)}, f32[17,3,2,40,128]{4,3,2,1,0:T(8,128)S(1)}, f32[10,2,2,24,128]{4,3,2,1,0:T(8,128)S(1)}, f32[6,2,2,16,12...) custom-call(f32[17,2,40,128]{3,2,1,0:T(8,128)S(1)} %get-tuple-elemen, ...), custom_call_target="tpu_custom_call", output_to_operand_aliasing={{0}: (0, {}), {1}: (1, {}), {2}: (2, {}), {3}: (3, {}), {4}... | custom-call | tf_op jit(solution)/shard_map/pallas_call | solution.py:634
  22.4 0.2 collective-permute-start.5
  22.5 1.6 %collective-permute-start.4 = (f32[152,128]{1,0:T(8,128)S(1)}, f32[152,128]{1,0:T(8,128)S(1)}, u32[]{:S(2)}, u32[]{:S(2)}) collective-permute-start(f32[152,128]{1,0:T(8,128)S(1)} %get-tuple-element.75), channel_id=1, source_target_pairs={{0,3},{1,0},{2,1},{3,2},{4,7},{5,4},{6,5},{7,6},{8,11},{9,8},{10,9... | collective-permute-start | bytes 233480 | tf_op jit(solution)/shard_map/ppermute | solution.py:23
  24.2 1.1 %shard_map.22.gbi = f32[17,3,2,40,128]{4,3,2,1,0:T(8,128)S(1)} custom-call(f32[2,2304,128]{2,1,0:T(8,128)S(1)} %get-tuple-element.71.u, f32[17,96,128]{2,1,0:T(8,128)S(1)} %get-tuple-element.72.zh, bf16[768,256]{1,0:T(8,128)(2,1)S(1)} %get-tuple-element.50.f1), custom_call_target="tpu_custom_call" | custom-call | flops 427819008 | bytes 4278190 | tf_op jit(solution)/shard_map/pallas_call | solution.py:634
  25.3 0.9 %collective-permute-done.4.rn = f32[152,128]{1,0:T(8,128)S(1)} collective-permute-done((f32[152,128]{1,0:T(8,128)S(1)}, f32[152,128]{1,0:T(8,128)S(1)}, u32[]{:S(2)}, u32[]{:S(2)}) %collective-permute-start.4) | collective-permute-done | bytes 77856 | tf_op jit(solution)/shard_map/ppermute | solution.py:23
  26.2 0.2 collective-permute-done.5.rp
  26.4 0.2 shard_map.23
  26.5 0.7 %collective-permute-start.7 = (f32[272,128]{1,0:T(8,128)S(1)}, f32[272,128]{1,0:T(8,128)S(1)}, u32[]{:S(2)}, u32[]{:S(2)}) collective-permute-start(f32[272,128]{1,0:T(8,128)S(1)} %get-tuple-element.87), channel_id=1, source_target_pairs={{0,4},{4,8},{8,12},{12,0},{1,5},{5,9},{9,13},{13,1},{2,6},{6,10},{... | collective-permute-start | bytes 417800 | tf_op jit(solution)/shard_map/ppermute | solution.py:23
  27.3 3.1 %collective-permute-start.6 = (f32[240,128]{1,0:T(8,128)S(1)}, f32[240,128]{1,0:T(8,128)S(1)}, u32[]{:S(2)}, u32[]{:S(2)}) collective-permute-start(f32[240,128]{1,0:T(8,128)S(1)} %get-tuple-element.86), channel_id=1, source_target_pairs={{0,12},{4,0},{8,4},{12,8},{1,13},{5,1},{9,5},{13,9},{2,14},{6,2},{... | collective-permute-start | bytes 368648 | tf_op jit(solution)/shard_map/ppermute | solution.py:23
  30.4 1.7 %shard_map.24 = (f32[17,2,40,128]{3,2,1,0:T(8,128)S(1)}, f32[17,3,2,40,128]{4,3,2,1,0:T(8,128)S(1)}, f32[17,2,64,256]{3,2,1,0:T(8,128)S(1)}) custom-call(f32[17,2,40,128]{3,2,1,0:T(8,128)S(1)} %get-tuple-element.77.qai, f32[17,3,2,40,128]{4,3,2,1,0:T(8,128)S(1)} %get-tuple-element.78.qbi, ...), custom_call_target="tpu_custom_call", output_to_operand_aliasing={{0}: (0, {}), {1}: (1, {})} | custom-call | flops 427819008 | bytes 4278190 | tf_op jit(solution)/shard_map/pallas_call | solution.py:634
  32.2 4.0 %collective-permute-done.6.rn = f32[240,128]{1,0:T(8,128)S(1)} collective-permute-done((f32[240,128]{1,0:T(8,128)S(1)}, f32[240,128]{1,0:T(8,128)S(1)}, u32[]{:S(2)}, u32[]{:S(2)}) %collective-permute-start.6) | collective-permute-done | bytes 122912 | tf_op jit(solution)/shard_map/ppermute | solution.py:23
  36.2 0.0 collective-permute-done.7.rp
  36.2 2.4 %shard_map.25 = (f32[17,2,40,128]{3,2,1,0:T(8,128)S(1)}, f32[17,3,2,40,128]{4,3,2,1,0:T(8,128)S(1)}, f32[10,2,2,24,128]{4,3,2,1,0:T(8,128)S(1)}, f32[6,2,2,16,12...) custom-call(f32[17,2,40,128]{3,2,1,0:T(8,128)S(1)} %get-tuple-elemen, ...), custom_call_target="tpu_custom_call", output_to_operand_aliasing={{0}: (0, {}), {1}: (1, {}), {2}: (2, {}), {3}: (3, {}), {4}... | custom-call | tf_op jit(solution)/shard_map/pallas_call | solution.py:634
Async XLA Ops:
  0.0 5.7 %copy-start = (s32[32,64,256]{2,1,0:T(8,128)S(1)}, s32[32,64,256]{2,1,0:T(8,128)}, u32[]{:S(2)}) copy-start(s32[32,64,256]{2,1,0:T(8,128)} %c.3) | copy-start | bytes 6291460
  3.2 5.2 %collective-permute-start.1 = (f32[176,128]{1,0:T(8,128)S(1)}, f32[176,128]{1,0:T(8,128)S(1)}, u32[]{:S(2)}, u32[]{:S(2)}) collective-permute-start(f32[176,128]{1,0:T(8,128)S(1)} %get-tuple-element.54), channel_id=1, source_target_pairs={{0,1},{1,2},{2,3},{3,0},{4,5},{5,6},{6,7},{7,4},{8,9},{9,10},{10,1... | collective-permute-start | bytes 270344 | tf_op jit(solution)/shard_map/ppermute | solution.py:23
  3.7 4.7 %collective-permute-start = (f32[152,128]{1,0:T(8,128)S(1)}, f32[152,128]{1,0:T(8,128)S(1)}, u32[]{:S(2)}, u32[]{:S(2)}) collective-permute-start(f32[152,128]{1,0:T(8,128)S(1)} %get-tuple-element.53), channel_id=1, source_target_pairs={{0,3},{1,0},{2,1},{3,2},{4,7},{5,4},{6,5},{7,6},{8,11},{9,8},{10,9... | collective-permute-start | bytes 233480 | tf_op jit(solution)/shard_map/ppermute | solution.py:23
  8.6 10.9 %collective-permute-start.3 = (f32[272,128]{1,0:T(8,128)S(1)}, f32[272,128]{1,0:T(8,128)S(1)}, u32[]{:S(2)}, u32[]{:S(2)}) collective-permute-start(f32[272,128]{1,0:T(8,128)S(1)} %get-tuple-element.64), channel_id=1, source_target_pairs={{0,4},{4,8},{8,12},{12,0},{1,5},{5,9},{9,13},{13,1},{2,6},{6,10},{... | collective-permute-start | bytes 417800 | tf_op jit(solution)/shard_map/ppermute | solution.py:23
  10.4 9.1 %collective-permute-start.2 = (f32[240,128]{1,0:T(8,128)S(1)}, f32[240,128]{1,0:T(8,128)S(1)}, u32[]{:S(2)}, u32[]{:S(2)}) collective-permute-start(f32[240,128]{1,0:T(8,128)S(1)} %get-tuple-element.63), channel_id=1, source_target_pairs={{0,12},{4,0},{8,4},{12,8},{1,13},{5,1},{9,5},{13,9},{2,14},{6,2},{... | collective-permute-start | bytes 368648 | tf_op jit(solution)/shard_map/ppermute | solution.py:23
  22.4 4.0 %collective-permute-start.5 = (f32[176,128]{1,0:T(8,128)S(1)}, f32[176,128]{1,0:T(8,128)S(1)}, u32[]{:S(2)}, u32[]{:S(2)}) collective-permute-start(f32[176,128]{1,0:T(8,128)S(1)} %get-tuple-element.76), channel_id=1, source_target_pairs={{0,1},{1,2},{2,3},{3,0},{4,5},{5,6},{6,7},{7,4},{8,9},{9,10},{10,1... | collective-permute-start | bytes 270344 | tf_op jit(solution)/shard_map/ppermute | solution.py:23
  22.5 3.7 %collective-permute-start.4 = (f32[152,128]{1,0:T(8,128)S(1)}, f32[152,128]{1,0:T(8,128)S(1)}, u32[]{:S(2)}, u32[]{:S(2)}) collective-permute-start(f32[152,128]{1,0:T(8,128)S(1)} %get-tuple-element.75), channel_id=1, source_target_pairs={{0,3},{1,0},{2,1},{3,2},{4,7},{5,4},{6,5},{7,6},{8,11},{9,8},{10,9... | collective-permute-start | bytes 233480 | tf_op jit(solution)/shard_map/ppermute | solution.py:23
  26.5 9.6 %collective-permute-start.7 = (f32[272,128]{1,0:T(8,128)S(1)}, f32[272,128]{1,0:T(8,128)S(1)}, u32[]{:S(2)}, u32[]{:S(2)}) collective-permute-start(f32[272,128]{1,0:T(8,128)S(1)} %get-tuple-element.87), channel_id=1, source_target_pairs={{0,4},{4,8},{8,12},{12,0},{1,5},{5,9},{9,13},{13,1},{2,6},{6,10},{... | collective-permute-start | bytes 417800 | tf_op jit(solution)/shard_map/ppermute | solution.py:23
  27.3 8.9 %collective-permute-start.6 = (f32[240,128]{1,0:T(8,128)S(1)}, f32[240,128]{1,0:T(8,128)S(1)}, u32[]{:S(2)}, u32[]{:S(2)}) collective-permute-start(f32[240,128]{1,0:T(8,128)S(1)} %get-tuple-element.86), channel_id=1, source_target_pairs={{0,12},{4,0},{8,4},{12,8},{1,13},{5,1},{9,5},{13,9},{2,14},{6,2},{... | collective-permute-start | bytes 368648 | tf_op jit(solution)/shard_map/ppermute | solution.py:23
